TPU v7x, 32 devices: a whole 2x2x4 slice. The times are simulated.
32 devices in a mesh: groups: 2 (over x), horiz: 4 (over y, core), level: 4 (over z).
Axes of the slice: x: 2, y: 2, z: 4, core: 2. Of those that a mesh axis runs over, the one named last changes fastest.
Arguments:
- fields: bfloat16 [8, 80, 32768], P(None, 'level', ('groups', 'horiz')), parts along dimension 2, may hold values from -6 to 6
- enc_in: bfloat16 [1024, 640], replicated, may hold values from -0.25 to 0.25
- enc_out: bfloat16 [1024, 64], replicated, may hold values from -0.1875 to 0.1875
- dec_in: bfloat16 [64, 1024], replicated, may hold values from -0.75 to 0.75
- dec_out: bfloat16 [1024, 640], replicated, may hold values from -0.1875 to 0.1875
- hyper_weight: bfloat16 [64, 128], replicated, may hold values from -1.5 to 1.5
- neighbours: int32 [6, 16384], P(None, ('horiz', 'level')), may hold values from 0 to 4352, as said below
- edge_rows: int32 [4, 2, 128], P('horiz'), may hold values from 0 to 4095, as said below
Outputs:
- grad_enc_in: float32 [2048, 640], P(('groups', 'horiz', 'level')), parts along dimension 0
- grad_enc_out: float32 [2048, 64], P('groups'), parts along dimension 0
- grad_dec_in: float32 [128, 1024], P('groups'), parts along dimension 0
- grad_dec_out: float32 [2048, 640], P(('groups', 'horiz', 'level')), parts along dimension 0
- grad_hyper: float32 [128, 128], P('groups'), parts along dimension 0
- cell_rate: float32 [32768], P(('groups', 'horiz', 'level')), parts along dimension 0
- loss: float32 [2], P('groups'), parts along dimension 0
There are 2 independent parts, one for each index of `groups`. A program takes and returns all parts, laid end to end along the dimension named above; an argument that names none is the same for every part. Nothing has to cross between parts.
Inputs may be any that keep to these rules, and one draw needn't show every extreme that they name: `neighbours`: entries of cell c of partition p: below 4096 a position in partition p; 4096 + e reads slot e of the list edge_rows[p - 1, 1] of the previous partition; 4224 + e slot e of edge_rows[p + 1, 0] of the next partition (modulo 4); 4352 marks no neighbour. Every cell has 5 or 6 valid entries. The slots read of one list are its first ones, their number differs between lists, and some list is read in all 128 slots. `edge_rows`: positions within the partition; the entries of one partition's two lists are all distinct.
All inputs are finite; a program needn't handle non-finite values.
Results may differ from a plain program's by a relative error of at most 0.0038.
Values may be sent and summed in bfloat16 or wider, within the bound.
No kernel may reach another device: no remote copies, remote signals or barrier semaphores. Data moves between devices by JAX's collectives and lax.ppermute only.
A program may use at most 128 MiB of HBM per device.

v0:
```python
import math

import jax
import jax.numpy as jnp
from jax import lax
from jax.sharding import PartitionSpec as P

LATENT = 64
EDGE = 128

BF = jnp.bfloat16
F32 = jnp.float32
scale_offset = 0.1


def mm(left, right):
    return jnp.dot(left, right, preferred_element_type=F32)


def mm_rows(left, right):
    return lax.dot_general(left, right, (((0,), (0,)), ((), ())), preferred_element_type=F32)


def mm_cells(left, right):
    return lax.dot_general(left, right, (((1,), (1,)), ((), ())), preferred_element_type=F32)


def silu_slope(preact):
    squash = jax.nn.sigmoid(preact)
    return squash * (1.0 + preact * (1.0 - squash))


def shift(block, axis, step):
    count = lax.axis_size(axis)
    return lax.ppermute(block, axis, [(i, (i + step) % count) for i in range(count)])


def swap(block, axis, bit):
    count = lax.axis_size(axis)
    return lax.ppermute(block, axis, [(i, i ^ bit) for i in range(count)])


def pick(block, index, dim):
    return lax.dynamic_index_in_dim(block, index, dim, keepdims=False)


def after(value, *others):
    return lax.optimization_barrier((value, *others))[0]


def swap_halves(block, dim):
    core = lax.axis_index("horiz") % 2
    other = swap(pick(block, 1 - core, dim).astype(BF), "horiz", 1)
    return pick(block, core, dim).astype(F32) + other.astype(F32)


def to_rows_y(far):
    return [shift(piece.astype(BF), "horiz", 2 * (d + 1)) for d, piece in enumerate(far)]


def to_level(block):
    n_l, me_l = lax.axis_size("level"), lax.axis_index("level")
    return [shift(pick(block, (me_l + d) % n_l, 0).astype(BF), "level", d) for d in range(1, n_l)]


def own_level(block, got):
    block = pick(block, lax.axis_index("level"), 0)
    for piece in got:
        block = block + piece.astype(F32)
    return block


def core_half(rows, product):
    half = rows.shape[0] // 2
    core = lax.axis_index("horiz") % 2
    mine = lax.dynamic_slice_in_dim(rows, core * half, half, 0)
    theirs = lax.dynamic_slice_in_dim(rows, (1 - core) * half, half, 0)
    return product(mine) + swap(product(theirs), "horiz", 1)


def both_halves(part):
    first = lax.axis_index("horiz") % 2 == 0
    other = swap(part, "horiz", 1)
    return jnp.concatenate([jnp.where(first, part, other), jnp.where(first, other, part)], axis=1)


def sum_pairs(part, axis, first, last, kind=F32):
    bit = first
    while bit < last:
        part = part.astype(kind)
        part = part.astype(F32) + swap(part, axis, bit).astype(F32)
        bit *= 2
    return part


def sum_pairs_split(part, axis, first, last):
    bit = first
    while bit < last:
        high = part.astype(BF)
        low = (part[:, -EDGE:] - high[:, -EDGE:].astype(F32)).astype(BF)
        mine = jnp.concatenate([high, low], axis=1)
        mine = mine.astype(F32) + swap(mine, axis, bit).astype(F32)
        part = mine[:, :-EDGE]
        part = jnp.concatenate([part[:, :-EDGE], part[:, -EDGE:] + mine[:, -EDGE:]], axis=1)
        bit *= 2
    return part


def local(fields, enc_in, enc_out, dec_in, dec_out, hyper_weight, neighbours, edge_rows):
    n_h, n_l = lax.axis_size("horiz"), lax.axis_size("level")
    n_y = n_h // 2
    me_l = lax.axis_index("level")
    me_y = lax.axis_index("horiz") // 2
    n_vars, n_lev, part = fields.shape
    cells = part // n_l
    slab = n_vars * n_lev
    feat = slab * n_l
    hidden = enc_in.shape[0]
    grad_scale = 1.0 / math.sqrt(part * n_h)

    stored = jnp.transpose(fields, (1, 0, 2)).reshape(slab, part)

    def slab_for(d):
        return lax.dynamic_slice(stored, (0, ((me_l + d) % n_l) * cells), (slab, cells))

    raw = jnp.concatenate(
        [slab_for(0)] + [shift(slab_for(d), "level", d) for d in range(1, n_l)], axis=0
    )
    place = jnp.arange(feat, dtype=jnp.int32)
    source = (me_l - place // slab) % n_l
    target = (place % n_vars) * (n_lev * n_l) + source * n_lev + (place % slab) // n_vars
    order = (place[:, None] == target[None, :]).astype(BF)

    def relative(position):
        return ((me_l - position // cells) % n_l) * cells + position % cells

    moved = jnp.where(neighbours < part, relative(neighbours), neighbours)
    limit = part + 2 * EDGE
    entry = lax.broadcasted_iota(jnp.int32, (limit, 1), 0)
    counts = jnp.zeros((limit, cells), F32)
    for k in range(6):
        counts = counts + (moved[k][None, :] == entry).astype(F32)
    counts = counts.astype(BF)
    valid = jnp.sum((neighbours < limit).astype(F32), axis=0)
    listed = (relative(edge_rows[0].reshape(1, 2 * EDGE)) == entry[:part]).astype(BF)
    placed = mm(enc_in, order).astype(BF)
    raw, counts, valid, listed, placed, order = lax.optimization_barrier(
        (raw, counts, valid, listed, placed, order)
    )

    pre_enc = mm(placed, raw)
    hidden_enc = jax.nn.silu(pre_enc).astype(BF)
    latent = mm_rows(enc_out, hidden_enc).astype(BF)

    table = jnp.concatenate(
        [latent] + [shift(latent, "level", d) for d in range(1, n_l)], axis=1
    )

    columns = mm(order, raw).astype(BF)
    pre_dec = mm_rows(dec_in, latent)
    hidden_dec = jax.nn.silu(pre_dec).astype(BF)
    residual = mm_rows(dec_out, hidden_dec) - columns.astype(F32)
    distortion = jnp.sum(residual * residual, axis=0)
    d_recon = (2.0 * grad_scale * residual).astype(BF)
    term = mm_cells(hidden_dec, d_recon).reshape(n_y, 2, n_l, hidden // (n_h * n_l), feat)
    term = swap_halves(term, 1)
    d_pre_dec = (mm(dec_out, d_recon) * silu_slope(pre_dec)).astype(BF)
    d_latent = mm(dec_in, d_pre_dec)
    table, d_latent, d_pre_dec, term = lax.optimization_barrier((table, d_latent, d_pre_dec, term))

    sent = mm(table, listed).astype(BF)
    halo = jnp.concatenate(
        [shift(sent[:, EDGE:], "horiz", 1), shift(sent[:, :EDGE], "horiz", -1)], axis=1
    )
    total = mm(table, counts[:part])
    halo, total = lax.optimization_barrier((halo, total))
    total = total + mm(halo, counts[part:])
    context_b = (total / valid).astype(BF)
    params = mm_rows(hyper_weight, context_b)
    centre, spread = params[:LATENT], params[LATENT:]
    sigma = scale_offset + jax.nn.softplus(spread)
    scaled = (latent.astype(F32) - centre) / sigma
    rate = jnp.sum(0.5 * scaled * scaled + jnp.log(sigma), axis=0)
    direct = grad_scale * scaled / sigma
    d_spread = grad_scale * (1.0 - scaled * scaled) / sigma * jax.nn.sigmoid(spread)
    d_params = jnp.concatenate([-direct, d_spread], axis=0).astype(BF)
    share = mm(hyper_weight, d_params) / valid
    high = share.astype(BF)
    low = (share - high.astype(F32)).astype(BF)
    share = jnp.concatenate([high, low], axis=0)

    both = mm_cells(share, counts[part:])
    back = (both[:LATENT] + both[LATENT:]).astype(BF)
    to_next, to_prev = back[:, EDGE:], back[:, :EDGE]
    back = jnp.concatenate([shift(to_next, "horiz", 1), shift(to_prev, "horiz", -1)], axis=1)
    both = mm_cells(after(share, to_next, to_prev), counts[:part])
    back, both = lax.optimization_barrier((back, both))
    own = both[:LATENT] + both[LATENT:] + mm_cells(back, listed)
    got = [
        shift(own[:, d * cells : (d + 1) * cells].astype(BF), "level", -d) for d in range(1, n_l)
    ]
    d_neighbour = own[:, :cells]
    for piece in got:
        d_neighbour = d_neighbour + piece.astype(F32)

    context_b, cell_loss, d_pre_dec, term = lax.optimization_barrier(
        (context_b, distortion / feat + rate / LATENT, d_pre_dec, term, got[0])
    )[:4]
    half_dec = core_half(d_pre_dec, lambda rows: mm_cells(latent, rows))
    small = jnp.concatenate(
        [
            mm_cells(context_b, d_params),
            jnp.pad(cell_loss.reshape(-1, EDGE), ((0, LATENT - cells // EDGE), (0, 0))),
        ],
        axis=1,
    )
    small = small + swap(small, "horiz", 1)
    near_dec = pick(term, me_y, 0)
    far_dec = to_rows_y([pick(term, (me_y + d) % n_y, 0) for d in range(1, n_y)])
    half_dec = sum_pairs(half_dec, "horiz", 2, n_h)
    dec_other = swap(half_dec, "level", 1)
    d_total = (d_latent + direct + d_neighbour).astype(BF)

    core = lax.axis_index("horiz") % 2
    rows = hidden // n_h

    def enc_rows(step, side):
        start = (((me_y + step) % n_y) * 2 + side) * rows
        weight = lax.dynamic_slice(enc_out, (start, 0), (rows, LATENT))
        preact = lax.dynamic_slice(pre_enc, (start, 0), (rows, cells))
        d_pre = lax.optimization_barrier((mm(weight, d_total) * silu_slope(preact)).astype(BF))
        return mm_cells(d_pre, columns)

    def enc_block(step):
        other = enc_rows(step, 1 - core).astype(BF)
        other = swap(other, "horiz", 1)
        kept = enc_rows(step, core)
        return (kept + other.astype(F32)).reshape(n_l, rows // n_l, feat)

    half_enc = core_half(hidden_enc, lambda rows: mm_cells(d_total, rows))
    small = jnp.concatenate([half_enc, small], axis=1)
    small = sum_pairs_split(small, "level", 1, 2)
    sent = [enc_block(d) for d in range(1, n_y)]
    sent, small = lax.optimization_barrier((sent, small))
    arrived = to_rows_y(sent)
    near_dec, half_dec, dec_other = lax.optimization_barrier(
        (near_dec, half_dec, dec_other, *sent)
    )[:3]
    for piece in far_dec:
        near_dec = near_dec + piece.astype(F32)
    got_dec = to_level(near_dec)
    small = sum_pairs_split(small, "level", 2, n_l)
    half_dec = sum_pairs(half_dec + dec_other, "level", 2, n_l, BF)
    near = enc_block(0)
    for piece in arrived:
        near = near + piece.astype(F32)
    near, small, half_dec, near_dec, *got_dec = lax.optimization_barrier(
        (near, small, half_dec, near_dec, *got_dec)
    )
    got_enc = to_level(near)
    small = sum_pairs(small, "horiz", 2, n_h)
    grad_dec_in = both_halves(half_dec)
    width = hidden // 2
    grad_hyper = small[:, width : width + 2 * LATENT]
    loss = (jnp.sum(small[:, width + 2 * LATENT :]) / (part * n_h)).reshape(1)
    grad_dec_out = own_level(near_dec, got_dec)
    grad_enc_out = both_halves(small[:, :width]).T
    grad_enc_in = own_level(near, got_enc)
    return (
        grad_enc_in,
        grad_enc_out,
        grad_dec_in,
        grad_dec_out,
        grad_hyper,
        rate / LATENT,
        loss,
    )


def solution(mesh):
    in_specs = (
        P(None, "level", ("groups", "horiz")),
        P(),
        P(),
        P(),
        P(),
        P(),
        P(None, ("horiz", "level")),
        P("horiz", None, None),
    )
    out_specs = (
        P(("groups", "horiz", "level"), None),
        P("groups", None),
        P("groups", None),
        P(("groups", "horiz", "level"), None),
        P("groups", None),
        P(("groups", "horiz", "level")),
        P("groups"),
    )
    return jax.shard_map(local, mesh=mesh, in_specs=in_specs, out_specs=out_specs, check_vma=False)
```

profile of v0, /device:TPU:1, one launch (start us, length us, event | category | flops | bytes accessed | tf_op | source)
XLA Modules:
  0.0 131.3 jit_solution(3388619652033057886)
XLA Ops:
  0.7 2.5 %constant_dynamic-slice_fusion.3 = (bf16[160,1024]{1,0:T(8,128)(2,1)}, bf16[160,1024]{1,0:T(8,128)(2,1)}, bf16[160,1024]{1,0:T(8,128)(2,1)}, bf16[160,1024]{1,0:T(8,128)(2,1)}) fusion(bf16[160,4096]{1,0:T(8,128)(2,1)} %bitcast.168, s32[]{:T(128)S(6)} %select_n.249, s32[]{:T(128)S(6)} %select_n.255, s32[]{:T(128)S(6)} %select_n.253, s32[]{:T(128)S(6)} %select_n.251), kind=kLoop, calls=%fused_computation.180 | loop fusion | bytes 2621456 | tf_op jit(solution)/shard_map/dynamic_slice | solution.py:124
  3.2 2.1 %collective-permute-start = (bf16[160,1024]{1,0:T(8,128)(2,1)}, bf16[160,1024]{1,0:T(8,128)(2,1)}, u32[]{:S(2)}, u32[]{:S(2)}) collective-permute-start(bf16[160,1024]{1,0:T(8,128)(2,1)} %get-tuple-element.78), channel_id=1, source_target_pairs={{0,1},{1,2},{2,3},{3,0},{4,5},{5,6},{6,7},{7,4},{8,9},{9,10},{10,1... | collective-permute-start | bytes 983048 | tf_op jit(solution)/shard_map/ppermute | solution.py:35
  5.3 2.3 %collective-permute-start.1 = (bf16[160,1024]{1,0:T(8,128)(2,1)}, bf16[160,1024]{1,0:T(8,128)(2,1)}, u32[]{:S(2)}, u32[]{:S(2)}) collective-permute-start(bf16[160,1024]{1,0:T(8,128)(2,1)} %get-tuple-element.77), channel_id=1, source_target_pairs={{0,2},{1,3},{2,0},{3,1},{4,6},{5,7},{6,4},{7,5},{8,10},{9,11},{10,... | collective-permute-start | bytes 983048 | tf_op jit(solution)/shard_map/ppermute | solution.py:35
  10.0 1.9 %compare_convert_fusion = bf16[4096,256]{1,0:T(8,128)(2,1)S(1)} fusion(s32[256]{0:T(256)S(1)} %fusion.94, s32[4096]{0:T(1024)S(1)} %bitcast.170), kind=kLoop, calls=%fused_computation.24 | loop fusion | flops 2097152 | bytes 2114560 | tf_op jit(solution)/shard_map/convert_element_type | solution.py:145
  11.9 15.1 %add_convert_fusion = bf16[4352,1024]{1,0:T(8,128)(2,1)} fusion(s32[1024]{0:T(1024)S(1)} %bitcast.174, s32[1024]{0:T(1024)S(1)} %bitcast.175, s32[1024]{0:T(1024)S(1)} %bitcast.176, s32[1024]{0:T(1024)S(1)} %bitcast.177, s32[1024]{0:T(1024)S(1)} %bitcast.178, s32[1024]{0:T(1024)S(1)} %bitcast.173), kind=kLoop, calls=%fused_computation | loop fusion | flops 80216064 | bytes 8937472 | tf_op jit(solution)/shard_map/convert_element_type | solution.py:143
  27.2 2.6 %fusion.12 = bf16[1024,640]{0,1:T(8,128)(2,1)S(1)} fusion(bf16[1024,640]{1,0:T(8,128)(2,1)} %param.9, s32[640]{0:T(1024)S(1)} %fusion.81), kind=kOutput, calls=%fused_computation.32 | convolution fusion | flops 840335360 | bytes 2624000 | tf_op jit(solution)/shard_map/dot_general | solution.py:17
  31.2 4.5 %multiply_convert_fusion = (bf16[1024,1024]{1,0:T(8,128)(2,1)S(1)}, f32[1024,1024]{1,0:T(8,128)}) fusion(bf16[1024,640]{0,1:T(8,128)(2,1)S(1)} %fusion.12, bf16[640,1024]{1,0:T(8,128)(2,1)S(1)} %pad_maximum_fusion), kind=kOutput, calls=%fused_computation.23 | convolution fusion | flops 1347420160 | bytes 8912896 | tf_op jit(solution)/shard_map/dot_general | solution.py:17
  36.2 7.4 %collective-permute-start.3 = (bf16[64,1024]{1,0:T(8,128)(2,1)S(1)}, bf16[64,1024]{1,0:T(8,128)(2,1)S(1)}, u32[]{:S(2)}, u32[]{:S(2)}) collective-permute-start(bf16[64,1024]{1,0:T(8,128)(2,1)S(1)} %bitcast.161), channel_id=1, source_target_pairs={{0,1},{1,2},{2,3},{3,0},{4,5},{5,6},{6,7},{7,4},{8,9},{9,10},{10,1... | collective-permute-start | bytes 393224 | tf_op jit(solution)/shard_map/ppermute | solution.py:35
  43.8 1.9 %collective-permute-start.5 = (bf16[64,1024]{1,0:T(8,128)(2,1)S(1)}, bf16[64,1024]{1,0:T(8,128)(2,1)S(1)}, u32[]{:S(2)}, u32[]{:S(2)}) collective-permute-start(bf16[64,1024]{1,0:T(8,128)(2,1)S(1)} %bitcast.163), channel_id=1, source_target_pairs={{0,3},{1,0},{2,1},{3,2},{4,7},{5,4},{6,5},{7,6},{8,11},{9,8},{10,9... | collective-permute-start | bytes 393224 | tf_op jit(solution)/shard_map/ppermute | solution.py:35
  47.1 1.6 %fusion.108 = f32[1024,640]{0,1:T(8,128)S(1)} fusion(bf16[1024,1024]{1,0:T(8,128)(2,1)S(1)} %get-tuple-element.108, bf16[1024,640]{1,0:T(8,128)(2,1)S(1)} %copy-done), kind=kOutput, calls=%fused_computation.233 | convolution fusion | flops 1342177280 | bytes 6029312 | tf_op jit(solution)/shard_map/dot_general | solution.py:21
  49.9 1.9 %fusion.99 = f32[1024,640]{1,0:T(8,128)S(1)} fusion(bf16[1024,1024]{1,0:T(8,128)(2,1)S(1)} %get-tuple-element.108, bf16[640,1024]{1,0:T(8,128)(2,1)S(1)} %get-tuple-element.115, f32[1024,640]{0,1:T(8,128)S(1)} %fusion.108), kind=kOutput, calls=%fused_computation.226 | convolution fusion | flops 1344798720 | bytes 8650752 | tf_op jit(solution)/shard_map/dot_general | solution.py:25
  53.0 2.6 %fusion.4 = bf16[1024,1024]{1,0:T(8,128)(2,1)S(1)} fusion(f32[1024,1024]{0,1:T(8,128)S(1)} %get-tuple-element.109, bf16[1024,640]{1,0:T(8,128)(2,1)S(1)} %copy-done, bf16[640,1024]{1,0:T(8,128)(2,1)S(1)} %get-tuple-element.115, f32[1024,640]{0,1:T(8,128)S(1)} %fusion.108), kind=kOutput, calls=%fused_computation.13 | convolution fusion | flops 1354235904 | bytes 11534336 | tf_op jit(solution)/shard_map/dot_general | solution.py:17
  58.1 1.6 %fusion.2 = f32[64,1024]{1,0:T(8,128)S(1)} fusion(bf16[64,4096]{1,0:T(8,128)(2,1)S(1)} %pad_maximum_fusion.1, bf16[4352,1024]{1,0:T(8,128)(2,1)S(1)} %bitcast.160), kind=kOutput, calls=%fused_computation.9 | convolution fusion | flops 536870912 | bytes 9175040 | tf_op jit(solution)/shard_map/dot_general | solution.py:17
  63.0 1.7 %collective-permute-start.9 = (bf16[64,128]{1,0:T(8,128)(2,1)S(1)}, bf16[64,128]{1,0:T(8,128)(2,1)S(1)}, u32[]{:S(2)}, u32[]{:S(2)}) collective-permute-start(bf16[64,128]{1,0:T(8,128)(2,1)S(1)} %get-tuple-element.96), channel_id=1, source_target_pairs={{0,4},{4,8},{8,12},{12,0},{1,5},{5,9},{9,13},{13,1},{2,6},{6,10},{... | collective-permute-start | bytes 49160 | tf_op jit(solution)/shard_map/ppermute | solution.py:35
  64.7 2.9 %fusion = f32[128,4096]{1,0:T(8,128)S(1)} fusion(bf16[128,1024]{1,0:T(8,128)(2,1)S(1)} %pad_maximum_fusion.3, bf16[4352,1024]{1,0:T(8,128)(2,1)S(1)} %bitcast.160), kind=kOutput, calls=%fused_computation.7 | convolution fusion | flops 1073741824 | bytes 10747904 | tf_op jit(solution)/shard_map/dot_general | solution.py:25
  68.5 2.3 %collective-permute-start.11 = (bf16[64,1024]{1,0:T(8,128)(2,1)S(1)}, bf16[64,1024]{1,0:T(8,128)(2,1)S(1)}, u32[]{:S(2)}, u32[]{:S(2)}) collective-permute-start(bf16[64,1024]{1,0:T(8,128)(2,1)S(1)} %get-tuple-element.87), channel_id=1, source_target_pairs={{0,3},{1,0},{2,1},{3,2},{4,7},{5,4},{6,5},{7,6},{8,11},{9,8},{10,9... | collective-permute-start | bytes 393224 | tf_op jit(solution)/shard_map/ppermute | solution.py:35
  71.7 2.5 %collective-permute-done.11 = bf16[64,1024]{1,0:T(8,128)(2,1)S(1)} collective-permute-done((bf16[64,1024]{1,0:T(8,128)(2,1)S(1)}, bf16[64,1024]{1,0:T(8,128)(2,1)S(1)}, u32[]{:S(2)}, u32[]{:S(2)}) %collective-permute-start.11) | collective-permute-done | bytes 131104 | tf_op jit(solution)/shard_map/ppermute | solution.py:35
  76.2 6.5 %collective-permute-done.12 = bf16[64,1024]{1,0:T(8,128)(2,1)S(1)} collective-permute-done((bf16[64,1024]{1,0:T(8,128)(2,1)S(1)}, bf16[64,1024]{1,0:T(8,128)(2,1)S(1)}, u32[]{:S(2)}, u32[]{:S(2)}) %collective-permute-start.12) | collective-permute-done | bytes 131104 | tf_op jit(solution)/shard_map/ppermute | solution.py:35
  90.4 2.9 %collective-permute-done.18 = bf16[64,896]{1,0:T(8,128)(2,1)S(1)} collective-permute-done((bf16[64,896]{1,0:T(8,128)(2,1)S(1)}, bf16[64,896]{1,0:T(8,128)(2,1)S(1)}, u32[]{:S(2)}, u32[]{:S(2)}) %collective-permute-start.18) | collective-permute-done | bytes 114720 | tf_op jit(solution)/shard_map/ppermute | solution.py:40
  96.0 2.2 %collective-permute-start.20 = (bf16[64,896]{1,0:T(8,128)(2,1)S(1)}, bf16[64,896]{1,0:T(8,128)(2,1)S(1)}, u32[]{:S(2)}, u32[]{:S(2)}) collective-permute-start(bf16[64,896]{1,0:T(8,128)(2,1)S(1)} %pad_maximum_fusion.10), channel_id=1, source_target_pairs={{0,2},{1,3},{2,0},{3,1},{4,6},{5,7},{6,4},{7,5},{8,10},{9,11},{10,... | collective-permute-start | bytes 344072 | tf_op jit(solution)/shard_map/ppermute | solution.py:40
  104.5 9.0 %collective-permute-done.24 = bf16[64,512]{1,0:T(8,128)(2,1)S(1)} collective-permute-done((bf16[64,512]{1,0:T(8,128)(2,1)S(1)}, bf16[64,512]{1,0:T(8,128)(2,1)S(1)}, u32[]{:S(2)}, u32[]{:S(2)}) %collective-permute-start.24) | collective-permute-done | bytes 65568 | tf_op jit(solution)/shard_map/ppermute | solution.py:40
  115.7 2.7 %collective-permute-start.30 = (bf16[64,640]{1,0:T(8,128)(2,1)S(1)}, bf16[64,640]{1,0:T(8,128)(2,1)S(1)}, u32[]{:S(2)}, u32[]{:S(2)}) collective-permute-start(bf16[64,640]{1,0:T(8,128)(2,1)S(1)} %get-tuple-element.83), channel_id=1, source_target_pairs={{0,2},{1,3},{2,0},{3,1},{4,6},{5,7},{6,4},{7,5},{8,10},{9,11},{10,... | collective-permute-start | bytes 245768 | tf_op jit(solution)/shard_map/ppermute | solution.py:35
  121.2 2.8 %collective-permute-done.30 = bf16[64,640]{1,0:T(8,128)(2,1)S(1)} collective-permute-done((bf16[64,640]{1,0:T(8,128)(2,1)S(1)}, bf16[64,640]{1,0:T(8,128)(2,1)S(1)}, u32[]{:S(2)}, u32[]{:S(2)}) %collective-permute-start.30) | collective-permute-done | bytes 81952 | tf_op jit(solution)/shard_map/ppermute | solution.py:35
  125.5 2.0 %collective-permute-start.33 = (f32[64,512]{1,0:T(8,128)S(1)}, f32[64,512]{1,0:T(8,128)S(1)}, u32[]{:S(2)}, u32[]{:S(2)}) collective-permute-start(f32[64,512]{1,0:T(8,128)S(1)} %slice.183), channel_id=1, source_target_pairs={{0,4},{4,0},{8,12},{12,8},{1,5},{5,1},{9,13},{13,9},{2,6},{6,2},{1... | collective-permute-start | bytes 393224 | tf_op jit(solution)/shard_map/ppermute | solution.py:40
  (163 shorter events, 42.5 us)
Async XLA Ops:
  3.2 26.6 %collective-permute-start = (bf16[160,1024]{1,0:T(8,128)(2,1)}, bf16[160,1024]{1,0:T(8,128)(2,1)}, u32[]{:S(2)}, u32[]{:S(2)}) collective-permute-start(bf16[160,1024]{1,0:T(8,128)(2,1)} %get-tuple-element.78), channel_id=1, source_target_pairs={{0,1},{1,2},{2,3},{3,0},{4,5},{5,6},{6,7},{7,4},{8,9},{9,10},{10,1... | collective-permute-start | bytes 983048 | tf_op jit(solution)/shard_map/ppermute | solution.py:35
  5.3 24.6 %collective-permute-start.1 = (bf16[160,1024]{1,0:T(8,128)(2,1)}, bf16[160,1024]{1,0:T(8,128)(2,1)}, u32[]{:S(2)}, u32[]{:S(2)}) collective-permute-start(bf16[160,1024]{1,0:T(8,128)(2,1)} %get-tuple-element.77), channel_id=1, source_target_pairs={{0,2},{1,3},{2,0},{3,1},{4,6},{5,7},{6,4},{7,5},{8,10},{9,11},{10,... | collective-permute-start | bytes 983048 | tf_op jit(solution)/shard_map/ppermute | solution.py:35
  7.6 22.3 %collective-permute-start.2 = (bf16[160,1024]{1,0:T(8,128)(2,1)}, bf16[160,1024]{1,0:T(8,128)(2,1)}, u32[]{:S(2)}, u32[]{:S(2)}) collective-permute-start(bf16[160,1024]{1,0:T(8,128)(2,1)} %get-tuple-element.76), channel_id=1, source_target_pairs={{0,3},{1,0},{2,1},{3,2},{4,7},{5,4},{6,5},{7,6},{8,11},{9,8},{10,9... | collective-permute-start | bytes 983048 | tf_op jit(solution)/shard_map/ppermute | solution.py:35
  36.2 20.0 %collective-permute-start.3 = (bf16[64,1024]{1,0:T(8,128)(2,1)S(1)}, bf16[64,1024]{1,0:T(8,128)(2,1)S(1)}, u32[]{:S(2)}, u32[]{:S(2)}) collective-permute-start(bf16[64,1024]{1,0:T(8,128)(2,1)S(1)} %bitcast.161), channel_id=1, source_target_pairs={{0,1},{1,2},{2,3},{3,0},{4,5},{5,6},{6,7},{7,4},{8,9},{9,10},{10,1... | collective-permute-start | bytes 393224 | tf_op jit(solution)/shard_map/ppermute | solution.py:35
  43.5 12.6 %collective-permute-start.4 = (bf16[64,1024]{1,0:T(8,128)(2,1)S(1)}, bf16[64,1024]{1,0:T(8,128)(2,1)S(1)}, u32[]{:S(2)}, u32[]{:S(2)}) collective-permute-start(bf16[64,1024]{1,0:T(8,128)(2,1)S(1)} %bitcast.162), channel_id=1, source_target_pairs={{0,2},{1,3},{2,0},{3,1},{4,6},{5,7},{6,4},{7,5},{8,10},{9,11},{10,... | collective-permute-start | bytes 393224 | tf_op jit(solution)/shard_map/ppermute | solution.py:35
  43.8 12.4 %collective-permute-start.5 = (bf16[64,1024]{1,0:T(8,128)(2,1)S(1)}, bf16[64,1024]{1,0:T(8,128)(2,1)S(1)}, u32[]{:S(2)}, u32[]{:S(2)}) collective-permute-start(bf16[64,1024]{1,0:T(8,128)(2,1)S(1)} %bitcast.163), channel_id=1, source_target_pairs={{0,3},{1,0},{2,1},{3,2},{4,7},{5,4},{6,5},{7,6},{8,11},{9,8},{10,9... | collective-permute-start | bytes 393224 | tf_op jit(solution)/shard_map/ppermute | solution.py:35
  68.5 5.7 %collective-permute-start.11 = (bf16[64,1024]{1,0:T(8,128)(2,1)S(1)}, bf16[64,1024]{1,0:T(8,128)(2,1)S(1)}, u32[]{:S(2)}, u32[]{:S(2)}) collective-permute-start(bf16[64,1024]{1,0:T(8,128)(2,1)S(1)} %get-tuple-element.87), channel_id=1, source_target_pairs={{0,3},{1,0},{2,1},{3,2},{4,7},{5,4},{6,5},{7,6},{8,11},{9,8},{10,9... | collective-permute-start | bytes 393224 | tf_op jit(solution)/shard_map/ppermute | solution.py:35
  71.4 11.3 %collective-permute-start.12 = (bf16[64,1024]{1,0:T(8,128)(2,1)S(1)}, bf16[64,1024]{1,0:T(8,128)(2,1)S(1)}, u32[]{:S(2)}, u32[]{:S(2)}) collective-permute-start(bf16[64,1024]{1,0:T(8,128)(2,1)S(1)} %get-tuple-element.89), channel_id=1, source_target_pairs={{0,2},{1,3},{2,0},{3,1},{4,6},{5,7},{6,4},{7,5},{8,10},{9,11},{10,... | collective-permute-start | bytes 393224 | tf_op jit(solution)/shard_map/ppermute | solution.py:35
  71.4 11.3 %collective-permute-start.13 = (bf16[64,1024]{1,0:T(8,128)(2,1)S(1)}, bf16[64,1024]{1,0:T(8,128)(2,1)S(1)}, u32[]{:S(2)}, u32[]{:S(2)}) collective-permute-start(bf16[64,1024]{1,0:T(8,128)(2,1)S(1)} %get-tuple-element.88), channel_id=1, source_target_pairs={{0,1},{1,2},{2,3},{3,0},{4,5},{5,6},{6,7},{7,4},{8,9},{9,10},{10,1... | collective-permute-start | bytes 393224 | tf_op jit(solution)/shard_map/ppermute | solution.py:35
  74.2 25.2 %collective-permute-start.25 = (bf16[4,64,640]{2,1,0:T(8,128)(2,1)S(1)}, bf16[4,64,640]{2,1,0:T(8,128)(2,1)S(1)}, u32[]{:S(2)}, u32[]{:S(2)}) collective-permute-start(bf16[4,64,640]{2,1,0:T(8,128)(2,1)S(1)} %fusion.29), channel_id=1, source_target_pairs={{0,8},{4,12},{8,0},{12,4},{1,9},{5,13},{9,1},{13,5},{2,10},{6,14},... | collective-permute-start | bytes 983048 | tf_op jit(solution)/shard_map/ppermute | solution.py:35
  74.7 14.6 %collective-permute-start.21 = (f32[64,512]{1,0:T(8,128)S(1)}, f32[64,512]{1,0:T(8,128)S(1)}, u32[]{:S(2)}, u32[]{:S(2)}) collective-permute-start(f32[64,512]{1,0:T(8,128)S(1)} %fusion.18), channel_id=1, source_target_pairs={{0,4},{4,0},{8,12},{12,8},{1,5},{5,1},{9,13},{13,9},{2,6},{6,2},{1... | collective-permute-start | bytes 393224 | tf_op jit(solution)/shard_map/ppermute | solution.py:40
  86.0 9.4 %collective-permute-start.15 = (bf16[256,640]{1,0:T(8,128)(2,1)S(1)}, bf16[256,640]{1,0:T(8,128)(2,1)S(1)}, u32[]{:S(2)}, u32[]{:S(2)}) collective-permute-start(bf16[256,640]{1,0:T(8,128)(2,1)S(1)} %convolution_convert_fusion.2), channel_id=1, source_target_pairs={{0,4},{4,0},{8,12},{12,8},{1,5},{5,1},{9,13},{13,9},{2,6},{6,2},{1... | collective-permute-start | bytes 983048 | tf_op jit(solution)/shard_map/ppermute | solution.py:40
  88.2 10.6 %collective-permute-start.14 = (bf16[256,640]{1,0:T(8,128)(2,1)S(1)}, bf16[256,640]{1,0:T(8,128)(2,1)S(1)}, u32[]{:S(2)}, u32[]{:S(2)}) collective-permute-start(bf16[256,640]{1,0:T(8,128)(2,1)S(1)} %convolution_convert_fusion.3), channel_id=1, source_target_pairs={{0,4},{4,0},{8,12},{12,8},{1,5},{5,1},{9,13},{13,9},{2,6},{6,2},{1... | collective-permute-start | bytes 983048 | tf_op jit(solution)/shard_map/ppermute | solution.py:40
  96.0 6.9 %collective-permute-start.20 = (bf16[64,896]{1,0:T(8,128)(2,1)S(1)}, bf16[64,896]{1,0:T(8,128)(2,1)S(1)}, u32[]{:S(2)}, u32[]{:S(2)}) collective-permute-start(bf16[64,896]{1,0:T(8,128)(2,1)S(1)} %pad_maximum_fusion.10), channel_id=1, source_target_pairs={{0,2},{1,3},{2,0},{3,1},{4,6},{5,7},{6,4},{7,5},{8,10},{9,11},{10,... | collective-permute-start | bytes 344072 | tf_op jit(solution)/shard_map/ppermute | solution.py:40
  98.2 15.3 %collective-permute-start.19 = (bf16[4,64,640]{2,1,0:T(8,128)(2,1)S(1)}, bf16[4,64,640]{2,1,0:T(8,128)(2,1)S(1)}, u32[]{:S(2)}, u32[]{:S(2)}) collective-permute-start(bf16[4,64,640]{2,1,0:T(8,128)(2,1)S(1)} %bitcast.169), channel_id=1, source_target_pairs={{0,8},{4,12},{8,0},{12,4},{1,9},{5,13},{9,1},{13,5},{2,10},{6,14},... | collective-permute-start | bytes 983048 | tf_op jit(solution)/shard_map/ppermute | solution.py:35
  99.6 14.1 %collective-permute-start.26 = (bf16[64,640]{1,0:T(8,128)(2,1)S(1)}, bf16[64,640]{1,0:T(8,128)(2,1)S(1)}, u32[]{:S(2)}, u32[]{:S(2)}) collective-permute-start(bf16[64,640]{1,0:T(8,128)(2,1)S(1)} %get-tuple-element.86), channel_id=1, source_target_pairs={{0,1},{1,2},{2,3},{3,0},{4,5},{5,6},{6,7},{7,4},{8,9},{9,10},{10,1... | collective-permute-start | bytes 245768 | tf_op jit(solution)/shard_map/ppermute | solution.py:35
  100.0 13.7 %collective-permute-start.27 = (bf16[64,640]{1,0:T(8,128)(2,1)S(1)}, bf16[64,640]{1,0:T(8,128)(2,1)S(1)}, u32[]{:S(2)}, u32[]{:S(2)}) collective-permute-start(bf16[64,640]{1,0:T(8,128)(2,1)S(1)} %get-tuple-element.85), channel_id=1, source_target_pairs={{0,2},{1,3},{2,0},{3,1},{4,6},{5,7},{6,4},{7,5},{8,10},{9,11},{10,... | collective-permute-start | bytes 245768 | tf_op jit(solution)/shard_map/ppermute | solution.py:35
  101.4 12.2 %collective-permute-start.28 = (bf16[64,640]{1,0:T(8,128)(2,1)S(1)}, bf16[64,640]{1,0:T(8,128)(2,1)S(1)}, u32[]{:S(2)}, u32[]{:S(2)}) collective-permute-start(bf16[64,640]{1,0:T(8,128)(2,1)S(1)} %get-tuple-element.84), channel_id=1, source_target_pairs={{0,3},{1,0},{2,1},{3,2},{4,7},{5,4},{6,5},{7,6},{8,11},{9,8},{10,9... | collective-permute-start | bytes 245768 | tf_op jit(solution)/shard_map/ppermute | solution.py:35
  102.9 10.6 %collective-permute-start.24 = (bf16[64,512]{1,0:T(8,128)(2,1)S(1)}, bf16[64,512]{1,0:T(8,128)(2,1)S(1)}, u32[]{:S(2)}, u32[]{:S(2)}) collective-permute-start(bf16[64,512]{1,0:T(8,128)(2,1)S(1)} %add_convert_fusion.1), channel_id=1, source_target_pairs={{0,2},{1,3},{2,0},{3,1},{4,6},{5,7},{6,4},{7,5},{8,10},{9,11},{10,... | collective-permute-start | bytes 196616 | tf_op jit(solution)/shard_map/ppermute | solution.py:40
  113.7 11.1 %collective-permute-start.34 = (f32[64,512]{1,0:T(8,128)S(1)}, f32[64,512]{1,0:T(8,128)S(1)}, u32[]{:S(2)}, u32[]{:S(2)}) collective-permute-start(f32[64,512]{1,0:T(8,128)S(1)} %convert_add_fusion.6), channel_id=1, source_target_pairs={{0,4},{4,0},{8,12},{12,8},{1,5},{5,1},{9,13},{13,9},{2,6},{6,2},{1... | collective-permute-start | bytes 393224 | tf_op jit(solution)/shard_map/ppermute | solution.py:40
  115.2 10.2 %collective-permute-start.32 = (f32[64,768]{1,0:T(8,128)S(1)}, f32[64,768]{1,0:T(8,128)S(1)}, u32[]{:S(2)}, u32[]{:S(2)}) collective-permute-start(f32[64,768]{1,0:T(8,128)S(1)} %pad_maximum_fusion.6), channel_id=1, source_target_pairs={{0,8},{4,12},{8,0},{12,4},{1,9},{5,13},{9,1},{13,5},{2,10},{6,14},... | collective-permute-start | bytes 589832 | tf_op jit(solution)/shard_map/ppermute | solution.py:40
  115.7 5.6 %collective-permute-start.29 = (bf16[64,640]{1,0:T(8,128)(2,1)S(1)}, bf16[64,640]{1,0:T(8,128)(2,1)S(1)}, u32[]{:S(2)}, u32[]{:S(2)}) collective-permute-start(bf16[64,640]{1,0:T(8,128)(2,1)S(1)} %get-tuple-element.81), channel_id=1, source_target_pairs={{0,1},{1,2},{2,3},{3,0},{4,5},{5,6},{6,7},{7,4},{8,9},{9,10},{10,1... | collective-permute-start | bytes 245768 | tf_op jit(solution)/shard_map/ppermute | solution.py:35
  115.7 8.3 %collective-permute-start.30 = (bf16[64,640]{1,0:T(8,128)(2,1)S(1)}, bf16[64,640]{1,0:T(8,128)(2,1)S(1)}, u32[]{:S(2)}, u32[]{:S(2)}) collective-permute-start(bf16[64,640]{1,0:T(8,128)(2,1)S(1)} %get-tuple-element.83), channel_id=1, source_target_pairs={{0,2},{1,3},{2,0},{3,1},{4,6},{5,7},{6,4},{7,5},{8,10},{9,11},{10,... | collective-permute-start | bytes 245768 | tf_op jit(solution)/shard_map/ppermute | solution.py:35
  118.4 5.6 %collective-permute-start.31 = (bf16[64,640]{1,0:T(8,128)(2,1)S(1)}, bf16[64,640]{1,0:T(8,128)(2,1)S(1)}, u32[]{:S(2)}, u32[]{:S(2)}) collective-permute-start(bf16[64,640]{1,0:T(8,128)(2,1)S(1)} %get-tuple-element.82), channel_id=1, source_target_pairs={{0,3},{1,0},{2,1},{3,2},{4,7},{5,4},{6,5},{7,6},{8,11},{9,8},{10,9... | collective-permute-start | bytes 245768 | tf_op jit(solution)/shard_map/ppermute | solution.py:35
  (24 other events, 182.2 us)
where the time goes:
time: 132 us; the launch traced here: 131 us
  starting transfers between devices  41.3 us (31%)
  matrix products  29.9 us (23%)
  waiting for transfers between devices  28.2 us (21%)
  other arithmetic  25.7 us (19%)
  between operations  3.4 us (3%)
  local copies, waits for them, and re-layouts  2.86 us (2%)
    ppermute x21, starting transfers between devices, shift(): lax.ppermute(block, axis, [(i, (i + step) % count) for i in range(count)])  27.9 us
    dot_general x13, matrix products, mm(): return jnp.dot(left, right, preferred_element_type=F32)  15.9 us
    convert_element_type x1, other arithmetic, local(): counts = counts.astype(BF)  15.1 us
    ppermute x21, waiting for transfers between devices, shift(): lax.ppermute(block, axis, [(i, (i + step) % count) for i in range(count)])  15 us
    ppermute x14, starting transfers between devices, swap(): return lax.ppermute(block, axis, [(i, i ^ bit) for i in range(count)])  13.3 us
    ppermute x14, waiting for transfers between devices, swap(): return lax.ppermute(block, axis, [(i, i ^ bit) for i in range(count)])  13.1 us
    dot_general x13, matrix products, mm_cells(): lax.dot_general(left, right, (((1,), (1,)), ((), ())), preferred_element_...  10.3 us
    dot_general x4, matrix products, mm_rows(): lax.dot_general(left, right, (((0,), (0,)), ((), ())), preferred_element_...  3.67 us
  transfers between devices with their start and end apart: 35, of which 9 were waited for; matrix products, arithmetic and copies ran while one was open for 35% of the time, Pallas kernels for 0%

commit v1 on v0

--- a/solution.py
+++ b/solution.py
@@ -56,6 +56,16 @@
 
 def to_rows_y(far):
     return [shift(piece.astype(BF), "horiz", 2 * (d + 1)) for d, piece in enumerate(far)]
+
+
+def sum_y(pieces):
+    count = len(pieces)
+    pieces = [piece.astype(F32) for piece in pieces]
+    if count > 2:
+        me_y = lax.axis_index("horiz") // 2
+        stacked = jnp.stack(pieces)
+        pieces = [pick(stacked, (me_y - y) % count, 0) for y in range(count)]
+    return sum(pieces)
 
 
 def to_level(block):
@@ -70,12 +80,12 @@
     return block
 
 
-def core_half(rows, product):
+def halves(rows, product):
     half = rows.shape[0] // 2
     core = lax.axis_index("horiz") % 2
     mine = lax.dynamic_slice_in_dim(rows, core * half, half, 0)
     theirs = lax.dynamic_slice_in_dim(rows, (1 - core) * half, half, 0)
-    return product(mine) + swap(product(theirs), "horiz", 1)
+    return product(mine), product(theirs)
 
 
 def both_halves(part):
@@ -84,26 +94,24 @@
     return jnp.concatenate([jnp.where(first, part, other), jnp.where(first, other, part)], axis=1)
 
 
-def sum_pairs(part, axis, first, last, kind=F32):
-    bit = first
-    while bit < last:
-        part = part.astype(kind)
-        part = part.astype(F32) + swap(part, axis, bit).astype(F32)
-        bit *= 2
-    return part
-
-
-def sum_pairs_split(part, axis, first, last):
-    bit = first
-    while bit < last:
-        high = part.astype(BF)
-        low = (part[:, -EDGE:] - high[:, -EDGE:].astype(F32)).astype(BF)
-        mine = jnp.concatenate([high, low], axis=1)
-        mine = mine.astype(F32) + swap(mine, axis, bit).astype(F32)
-        part = mine[:, :-EDGE]
-        part = jnp.concatenate([part[:, :-EDGE], part[:, -EDGE:] + mine[:, -EDGE:]], axis=1)
-        bit *= 2
-    return part
+def pack(block, extra):
+    high = extra.astype(BF)
+    low = (extra - high.astype(F32)).astype(BF)
+    both = jnp.concatenate([high, low], axis=0)
+    both = jnp.pad(both, ((0, 0), (0, block.shape[1] - both.shape[1])))
+    return jnp.concatenate([block.astype(BF), both], axis=0)
+
+
+def unpack(packed, rows, high):
+    packed = packed.astype(F32)
+    extra = packed[rows:, :EDGE]
+    return packed[:rows], extra[:high] + extra[high:]
+
+
+def tree(pieces):
+    while len(pieces) > 1:
+        pieces = [a + b for a, b in zip(pieces[::2], pieces[1::2])]
+    return pieces[0]
 
 
 def local(fields, enc_in, enc_out, dec_in, dec_out, hyper_weight, neighbours, edge_rows):
@@ -166,7 +174,8 @@
     term = swap_halves(term, 1)
     d_pre_dec = (mm(dec_out, d_recon) * silu_slope(pre_dec)).astype(BF)
     d_latent = mm(dec_in, d_pre_dec)
-    table, d_latent, d_pre_dec, term = lax.optimization_barrier((table, d_latent, d_pre_dec, term))
+    half_dec = halves(d_pre_dec, lambda rows: mm_cells(latent, rows))
+    table, d_latent, half_dec, term = lax.optimization_barrier((table, d_latent, half_dec, term))
 
     sent = mm(table, listed).astype(BF)
     halo = jnp.concatenate(
@@ -203,69 +212,85 @@
     for piece in got:
         d_neighbour = d_neighbour + piece.astype(F32)
 
-    context_b, cell_loss, d_pre_dec, term = lax.optimization_barrier(
-        (context_b, distortion / feat + rate / LATENT, d_pre_dec, term, got[0])
-    )[:4]
-    half_dec = core_half(d_pre_dec, lambda rows: mm_cells(latent, rows))
-    small = jnp.concatenate(
-        [
-            mm_cells(context_b, d_params),
-            jnp.pad(cell_loss.reshape(-1, EDGE), ((0, LATENT - cells // EDGE), (0, 0))),
-        ],
-        axis=1,
-    )
-    small = small + swap(small, "horiz", 1)
-    near_dec = pick(term, me_y, 0)
-    far_dec = to_rows_y([pick(term, (me_y + d) % n_y, 0) for d in range(1, n_y)])
-    half_dec = sum_pairs(half_dec, "horiz", 2, n_h)
-    dec_other = swap(half_dec, "level", 1)
-    d_total = (d_latent + direct + d_neighbour).astype(BF)
-
     core = lax.axis_index("horiz") % 2
     rows = hidden // n_h
-
-    def enc_rows(step, side):
-        start = (((me_y + step) % n_y) * 2 + side) * rows
-        weight = lax.dynamic_slice(enc_out, (start, 0), (rows, LATENT))
-        preact = lax.dynamic_slice(pre_enc, (start, 0), (rows, cells))
+    width = hidden // 2
+    term, half_dec = lax.optimization_barrier((term, half_dec, own))[:2]
+    half_dec = (half_dec[0] + swap(half_dec[1], "horiz", 1)).astype(BF)
+    rider = jnp.pad(half_dec, ((0, 0), (0, feat - width)))
+    near_dec = pick(term, me_y, 0)
+    far = [pick(term, (me_y + d) % n_y, 0).reshape(rows, feat) for d in range(1, n_y)]
+    far = to_rows_y([jnp.concatenate([piece.astype(BF), rider], axis=0) for piece in far])
+    context_b, cell_loss = lax.optimization_barrier(
+        (context_b, distortion / feat + rate / LATENT, got[0])
+    )[:2]
+    hyper = mm_cells(context_b, d_params)
+    hyper = hyper + swap(hyper, "horiz", 1)
+    cell_loss = cell_loss.reshape(-1, EDGE)
+    cell_loss = cell_loss + swap(cell_loss, "horiz", 1)
+    high = cell_loss.shape[0]
+    d_total = (d_latent + direct + d_neighbour).astype(BF)
+    d_total, hyper, cell_loss, *far = lax.optimization_barrier((d_total, hyper, cell_loss, *far))
+
+    half_enc = halves(hidden_enc, lambda block: mm_cells(d_total, block))
+    half_enc = half_enc[0] + swap(half_enc[1], "horiz", 1)
+
+    def enc_rows(side):
+        weight = pick(enc_out.reshape(n_y, 2, rows, LATENT), side, 1).reshape(n_y * rows, LATENT)
+        preact = pick(pre_enc.reshape(n_y, 2, rows, cells), side, 1).reshape(n_y * rows, cells)
         d_pre = lax.optimization_barrier((mm(weight, d_total) * silu_slope(preact)).astype(BF))
         return mm_cells(d_pre, columns)
 
-    def enc_block(step):
-        other = enc_rows(step, 1 - core).astype(BF)
-        other = swap(other, "horiz", 1)
-        kept = enc_rows(step, core)
-        return (kept + other.astype(F32)).reshape(n_l, rows // n_l, feat)
-
-    half_enc = core_half(hidden_enc, lambda rows: mm_cells(d_total, rows))
-    small = jnp.concatenate([half_enc, small], axis=1)
-    small = sum_pairs_split(small, "level", 1, 2)
-    sent = [enc_block(d) for d in range(1, n_y)]
-    sent, small = lax.optimization_barrier((sent, small))
+    other = swap(enc_rows(1 - core).astype(BF), "horiz", 1)
+    near = (enc_rows(core) + other.astype(F32)).reshape(n_y, rows, feat)
+    rider = pack(jnp.concatenate([half_enc, hyper], axis=1), cell_loss)
+    sent = [pick(near, (me_y + d) % n_y, 0).astype(BF) for d in range(1, n_y)]
+    sent = [jnp.concatenate([piece, rider], axis=0) for piece in sent]
+    for piece in far:
+        near_dec = near_dec + piece[:rows].reshape(near_dec.shape).astype(F32)
+    half_dec = sum_y([half_dec] + [piece[rows:, :width] for piece in far]).astype(BF)
+    near, near_dec, half_dec, sent = lax.optimization_barrier(
+        (pick(near, me_y, 0), near_dec, half_dec, sent)
+    )
+
     arrived = to_rows_y(sent)
-    near_dec, half_dec, dec_other = lax.optimization_barrier(
-        (near_dec, half_dec, dec_other, *sent)
-    )[:3]
-    for piece in far_dec:
-        near_dec = near_dec + piece.astype(F32)
-    got_dec = to_level(near_dec)
-    small = sum_pairs_split(small, "level", 2, n_l)
-    half_dec = sum_pairs(half_dec + dec_other, "level", 2, n_l, BF)
-    near = enc_block(0)
+    got_dec = [
+        swap(
+            jnp.concatenate(
+                [pick(near_dec, me_l ^ d, 0).astype(BF).reshape(LATENT, -1), half_dec], axis=1
+            ),
+            "level",
+            d,
+        )
+        for d in range(1, n_l)
+    ]
+    near, arrived, got_dec = lax.optimization_barrier((near, arrived, got_dec))
+
     for piece in arrived:
-        near = near + piece.astype(F32)
-    near, small, half_dec, near_dec, *got_dec = lax.optimization_barrier(
-        (near, small, half_dec, near_dec, *got_dec)
-    )
-    got_enc = to_level(near)
-    small = sum_pairs(small, "horiz", 2, n_h)
+        near = near + piece[:rows].astype(F32)
+    near = near.reshape(n_l, rows // n_l, feat)
+    riders = [rider] + [piece[rows:] for piece in arrived]
+    riders = [unpack(piece, LATENT, high) for piece in riders]
+    rider = pack(*(sum_y(list(pieces)) for pieces in zip(*riders)))
+    got_enc = [
+        swap(jnp.concatenate([pick(near, me_l ^ d, 0).astype(BF), rider], axis=0), "level", d)
+        for d in range(1, n_l)
+    ]
+    few = rows // n_l
+    riders = [unpack(piece, LATENT, high) for piece in [rider] + [p[few:] for p in got_enc]]
+    half_enc, cell_loss = (tree(list(pieces)) for pieces in zip(*riders))
+    grad_dec_out = pick(near_dec, me_l, 0)
+    for piece in got_dec:
+        piece = piece[:, :-width].reshape(grad_dec_out.shape)
+        grad_dec_out = grad_dec_out + piece.astype(F32)
+    half_dec = tree([half_dec.astype(F32)] + [piece[:, -width:].astype(F32) for piece in got_dec])
     grad_dec_in = both_halves(half_dec)
-    width = hidden // 2
-    grad_hyper = small[:, width : width + 2 * LATENT]
-    loss = (jnp.sum(small[:, width + 2 * LATENT :]) / (part * n_h)).reshape(1)
-    grad_dec_out = own_level(near_dec, got_dec)
-    grad_enc_out = both_halves(small[:, :width]).T
-    grad_enc_in = own_level(near, got_enc)
+    grad_hyper = half_enc[:, width:]
+    loss = (jnp.sum(cell_loss) / (part * n_h)).reshape(1)
+    grad_enc_out = both_halves(half_enc[:, :width]).T
+    grad_enc_in = pick(near, me_l, 0)
+    for piece in got_enc:
+        grad_enc_in = grad_enc_in + piece[:few].astype(F32)
     return (
         grad_enc_in,
         grad_enc_out,

time: 132 us -> 129 us (0.977)
  local copies, waits for them, and re-layouts: 2.86 us -> 5.99 us
  starting transfers between devices: 41.3 us -> 38.4 us
  matrix products: 29.9 us -> 27.3 us
    ppermute x21 -> x15, starting transfers between devices: 27.9 us -> 18.9 us  [shift(): lax.ppermute(block, axis, [(i, (i + step) % count) for i in range(count)])]
    ppermute x14, starting transfers between devices: 13.3 us -> 19.6 us  [swap(): return lax.ppermute(block, axis, [(i, i ^ bit) for i in range(count)])]
    ppermute x14, waiting for transfers between devices: 13.1 us -> 18.1 us  [swap(): return lax.ppermute(block, axis, [(i, i ^ bit) for i in range(count)])]
    ppermute x21 -> x15, waiting for transfers between devices: 15 us -> 10.6 us  [shift(): lax.ppermute(block, axis, [(i, (i + step) % count) for i in range(count)])]
    dot_general x13 -> x11, matrix products: 15.9 us -> 13.7 us  [mm(): return jnp.dot(left, right, preferred_element_type=F32)]
    dynamic_slice x0 -> x2, local copies, waits for them, and re-layouts: none -> 1.42 us  [pick(): return lax.dynamic_index_in_dim(block, index, dim, keepdims=False)]
    dot_general x13 -> x11, matrix products: 10.3 us -> 9.9 us  [mm_cells(): lax.dot_general(left, right, (((1,), (1,)), ((), ())), preferred_element_...]
  transfers between devices with their start and end apart: 35 -> 29, of which waited for: 9 -> 8; matrix products, arithmetic and copies ran while one was open for 35% -> 35% of each run, Pallas kernels for 0% -> 0%
where the time goes in v1:
time: 129 us
  starting transfers between devices  38.4 us (30%)
  waiting for transfers between devices  28.7 us (22%)
  matrix products  27.3 us (21%)
  other arithmetic  25.3 us (20%)
  local copies, waits for them, and re-layouts  5.99 us (5%)
  between operations  3.41 us (3%)
    ppermute x14, starting transfers between devices, swap(): return lax.ppermute(block, axis, [(i, i ^ bit) for i in range(count)])  19.6 us
    ppermute x15, starting transfers between devices, shift(): lax.ppermute(block, axis, [(i, (i + step) % count) for i in range(count)])  18.9 us
    ppermute x14, waiting for transfers between devices, swap(): return lax.ppermute(block, axis, [(i, i ^ bit) for i in range(count)])  18.1 us
    convert_element_type x1, other arithmetic, local(): counts = counts.astype(BF)  15.1 us
    dot_general x11, matrix products, mm(): return jnp.dot(left, right, preferred_element_type=F32)  13.7 us
    ppermute x15, waiting for transfers between devices, shift(): lax.ppermute(block, axis, [(i, (i + step) % count) for i in range(count)])  10.6 us
    dot_general x11, matrix products, mm_cells(): lax.dot_general(left, right, (((1,), (1,)), ((), ())), preferred_element_...  9.9 us
    dot_general x4, matrix products, mm_rows(): lax.dot_general(left, right, (((0,), (0,)), ((), ())), preferred_element_...  3.69 us
  transfers between devices with their start and end apart: 29, of which 8 were waited for; matrix products, arithmetic and copies ran while one was open for 35% of the time, Pallas kernels for 0%

profile of v1, /device:TPU:1, one launch (start us, length us, event | category | flops | bytes accessed | tf_op | source)
XLA Modules:
  0.0 129.1 jit_solution(18277374972030250771)
XLA Ops:
  0.7 2.4 %constant_dynamic-slice_fusion.5 = (bf16[160,1024]{1,0:T(8,128)(2,1)}, bf16[160,1024]{1,0:T(8,128)(2,1)}, bf16[160,1024]{1,0:T(8,128)(2,1)}, bf16[160,1024]{1,0:T(8,128)(2,1)}) fusion(bf16[160,4096]{1,0:T(8,128)(2,1)} %bitcast.222, s32[]{:T(128)S(6)} %select_n.220, s32[]{:T(128)S(6)} %select_n.226, s32[]{:T(128)S(6)} %select_n.224, s32[]{:T(128)S(6)} %select_n.222), kind=kLoop, calls=%fused_computation.203 | loop fusion | bytes 2621456 | tf_op jit(solution)/shard_map/dynamic_slice | solution.py:132
  3.2 2.1 %collective-permute-start = (bf16[160,1024]{1,0:T(8,128)(2,1)}, bf16[160,1024]{1,0:T(8,128)(2,1)}, u32[]{:S(2)}, u32[]{:S(2)}) collective-permute-start(bf16[160,1024]{1,0:T(8,128)(2,1)} %get-tuple-element.90), channel_id=1, source_target_pairs={{0,1},{1,2},{2,3},{3,0},{4,5},{5,6},{6,7},{7,4},{8,9},{9,10},{10,1... | collective-permute-start | bytes 983048 | tf_op jit(solution)/shard_map/ppermute | solution.py:35
  5.3 2.3 %collective-permute-start.1 = (bf16[160,1024]{1,0:T(8,128)(2,1)}, bf16[160,1024]{1,0:T(8,128)(2,1)}, u32[]{:S(2)}, u32[]{:S(2)}) collective-permute-start(bf16[160,1024]{1,0:T(8,128)(2,1)} %get-tuple-element.89), channel_id=1, source_target_pairs={{0,2},{1,3},{2,0},{3,1},{4,6},{5,7},{6,4},{7,5},{8,10},{9,11},{10,... | collective-permute-start | bytes 983048 | tf_op jit(solution)/shard_map/ppermute | solution.py:35
  10.0 1.9 %compare_convert_fusion = bf16[4096,256]{1,0:T(8,128)(2,1)S(1)} fusion(s32[256]{0:T(256)S(1)} %fusion.111, s32[4096]{0:T(1024)S(1)} %bitcast.228), kind=kLoop, calls=%fused_computation.24 | loop fusion | flops 2097152 | bytes 2114560 | tf_op jit(solution)/shard_map/convert_element_type | solution.py:153
  11.9 15.1 %add_convert_fusion = bf16[4352,1024]{1,0:T(8,128)(2,1)} fusion(s32[1024]{0:T(1024)S(1)} %bitcast.232, s32[1024]{0:T(1024)S(1)} %bitcast.233, s32[1024]{0:T(1024)S(1)} %bitcast.234, s32[1024]{0:T(1024)S(1)} %bitcast.235, s32[1024]{0:T(1024)S(1)} %bitcast.236, s32[1024]{0:T(1024)S(1)} %bitcast.231), kind=kLoop, calls=%fused_computation | loop fusion | flops 80216064 | bytes 8937472 | tf_op jit(solution)/shard_map/convert_element_type | solution.py:151
  29.1 2.6 %fusion.26 = bf16[1024,640]{0,1:T(8,128)(2,1)S(1)} fusion(bf16[1024,640]{1,0:T(8,128)(2,1)} %param.9, s32[640]{0:T(1024)S(1)} %fusion.93), kind=kOutput, calls=%fused_computation.50 | convolution fusion | flops 840335360 | bytes 2624000 | tf_op jit(solution)/shard_map/dot_general | solution.py:17
  33.0 2.4 %multiply_convert_fusion = (bf16[1024,1024]{1,0:T(8,128)(2,1)S(1)}, f32[1024,1024]{1,0:T(8,128)S(1)}) fusion(bf16[1024,640]{0,1:T(8,128)(2,1)S(1)} %fusion.26, bf16[640,1024]{1,0:T(8,128)(2,1)S(1)} %pad_maximum_fusion), kind=kOutput, calls=%fused_computation.23 | convolution fusion | flops 1347420160 | bytes 8912896 | tf_op jit(solution)/shard_map/dot_general | solution.py:17
  36.0 5.5 %collective-permute-start.3 = (bf16[64,1024]{1,0:T(8,128)(2,1)S(1)}, bf16[64,1024]{1,0:T(8,128)(2,1)S(1)}, u32[]{:S(2)}, u32[]{:S(2)}) collective-permute-start(bf16[64,1024]{1,0:T(8,128)(2,1)S(1)} %bitcast.213), channel_id=1, source_target_pairs={{0,1},{1,2},{2,3},{3,0},{4,5},{5,6},{6,7},{7,4},{8,9},{9,10},{10,1... | collective-permute-start | bytes 393224 | tf_op jit(solution)/shard_map/ppermute | solution.py:35
  41.8 1.9 %collective-permute-start.5 = (bf16[64,1024]{1,0:T(8,128)(2,1)S(1)}, bf16[64,1024]{1,0:T(8,128)(2,1)S(1)}, u32[]{:S(2)}, u32[]{:S(2)}) collective-permute-start(bf16[64,1024]{1,0:T(8,128)(2,1)S(1)} %bitcast.215), channel_id=1, source_target_pairs={{0,3},{1,0},{2,1},{3,2},{4,7},{5,4},{6,5},{7,6},{8,11},{9,8},{10,9... | collective-permute-start | bytes 393224 | tf_op jit(solution)/shard_map/ppermute | solution.py:35
  47.9 1.9 %fusion.115 = f32[1024,640]{1,0:T(8,128)S(1)} fusion(bf16[1024,1024]{1,0:T(8,128)(2,1)S(1)} %get-tuple-element.124, bf16[640,1024]{1,0:T(8,128)(2,1)S(1)} %get-tuple-element.131, f32[1024,640]{0,1:T(8,128)S(1)} %fusion.122), kind=kOutput, calls=%fused_computation.262 | convolution fusion | flops 1344798720 | bytes 8650752 | tf_op jit(solution)/shard_map/dot_general | solution.py:25
  51.0 2.7 %fusion.4 = bf16[1024,1024]{1,0:T(8,128)(2,1)S(1)} fusion(f32[1024,1024]{0,1:T(8,128)S(1)} %get-tuple-element.125, bf16[1024,640]{1,0:T(8,128)(2,1)S(1)} %copy-done, bf16[640,1024]{1,0:T(8,128)(2,1)S(1)} %get-tuple-element.131, f32[1024,640]{0,1:T(8,128)S(1)} %fusion.122), kind=kOutput, calls=%fused_computation.13 | convolution fusion | flops 1354235904 | bytes 11534336 | tf_op jit(solution)/shard_map/dot_general | solution.py:17
  62.5 1.7 %collective-permute-start.9 = (bf16[64,128]{1,0:T(8,128)(2,1)S(1)}, bf16[64,128]{1,0:T(8,128)(2,1)S(1)}, u32[]{:S(2)}, u32[]{:S(2)}) collective-permute-start(bf16[64,128]{1,0:T(8,128)(2,1)S(1)} %get-tuple-element.112), channel_id=1, source_target_pairs={{0,4},{4,8},{8,12},{12,0},{1,5},{5,9},{9,13},{13,1},{2,6},{6,10},{... | collective-permute-start | bytes 49160 | tf_op jit(solution)/shard_map/ppermute | solution.py:35
  64.2 2.9 %fusion = f32[128,4096]{1,0:T(8,128)S(1)} fusion(bf16[128,1024]{1,0:T(8,128)(2,1)S(1)} %pad_maximum_fusion.7, bf16[4352,1024]{1,0:T(8,128)(2,1)S(1)} %bitcast.211), kind=kOutput, calls=%fused_computation.7 | convolution fusion | flops 1073741824 | bytes 10747904 | tf_op jit(solution)/shard_map/dot_general | solution.py:25
  68.6 1.7 %collective-permute-start.11 = (bf16[64,1024]{1,0:T(8,128)(2,1)S(1)}, bf16[64,1024]{1,0:T(8,128)(2,1)S(1)}, u32[]{:S(2)}, u32[]{:S(2)}) collective-permute-start(bf16[64,1024]{1,0:T(8,128)(2,1)S(1)} %get-tuple-element.99), channel_id=1, source_target_pairs={{0,3},{1,0},{2,1},{3,2},{4,7},{5,4},{6,5},{7,6},{8,11},{9,8},{10,9... | collective-permute-start | bytes 393224 | tf_op jit(solution)/shard_map/ppermute | solution.py:35
  71.1 2.1 %collective-permute-done.11 = bf16[64,1024]{1,0:T(8,128)(2,1)S(1)} collective-permute-done((bf16[64,1024]{1,0:T(8,128)(2,1)S(1)}, bf16[64,1024]{1,0:T(8,128)(2,1)S(1)}, u32[]{:S(2)}, u32[]{:S(2)}) %collective-permute-start.11) | collective-permute-done | bytes 131104 | tf_op jit(solution)/shard_map/ppermute | solution.py:35
  73.2 1.8 %collective-permute-start.15 = (f32[8,128]{1,0:T(8,128)S(1)}, f32[8,128]{1,0:T(8,128)S(1)}, u32[]{:S(2)}, u32[]{:S(2)}) collective-permute-start(f32[8,128]{1,0:T(8,128)S(1)} %bitcast.237), channel_id=1, source_target_pairs={{0,4},{4,0},{8,12},{12,8},{1,5},{5,1},{9,13},{13,9},{2,6},{6,2},{1... | collective-permute-start | bytes 12296 | tf_op jit(solution)/shard_map/ppermute | solution.py:40
  75.3 6.9 %collective-permute-done.12 = bf16[64,1024]{1,0:T(8,128)(2,1)S(1)} collective-permute-done((bf16[64,1024]{1,0:T(8,128)(2,1)S(1)}, bf16[64,1024]{1,0:T(8,128)(2,1)S(1)}, u32[]{:S(2)}, u32[]{:S(2)}) %collective-permute-start.12) | collective-permute-done | bytes 131104 | tf_op jit(solution)/shard_map/ppermute | solution.py:35
  93.8 2.8 %collective-permute-done.21 = bf16[64,1152]{1,0:T(8,128)(2,1)S(1)} collective-permute-done((bf16[64,1152]{1,0:T(8,128)(2,1)S(1)}, bf16[64,1152]{1,0:T(8,128)(2,1)S(1)}, u32[]{:S(2)}, u32[]{:S(2)}) %collective-permute-start.21) | collective-permute-done | bytes 147488 | tf_op jit(solution)/shard_map/ppermute | solution.py:40
  97.8 4.6 %collective-permute-done.23 = bf16[64,1152]{1,0:T(8,128)(2,1)S(1)} collective-permute-done((bf16[64,1152]{1,0:T(8,128)(2,1)S(1)}, bf16[64,1152]{1,0:T(8,128)(2,1)S(1)}, u32[]{:S(2)}, u32[]{:S(2)}) %collective-permute-start.23) | collective-permute-done | bytes 147488 | tf_op jit(solution)/shard_map/ppermute | solution.py:40
  102.7 2.1 %collective-permute-start.26 = (bf16[144,640]{1,0:T(8,128)(2,1)S(1)}, bf16[144,640]{1,0:T(8,128)(2,1)S(1)}, u32[]{:S(2)}, u32[]{:S(2)}) collective-permute-start(bf16[144,640]{1,0:T(8,128)(2,1)S(1)} %get-tuple-element.107), channel_id=1, source_target_pairs={{0,3},{1,2},{2,1},{3,0},{4,7},{5,6},{6,5},{7,4},{8,11},{9,10},{10,... | collective-permute-start | bytes 552968 | tf_op jit(solution)/shard_map/ppermute | solution.py:40
  104.8 3.5 %collective-permute-start.25 = (bf16[144,640]{1,0:T(8,128)(2,1)S(1)}, bf16[144,640]{1,0:T(8,128)(2,1)S(1)}, u32[]{:S(2)}, u32[]{:S(2)}) collective-permute-start(bf16[144,640]{1,0:T(8,128)(2,1)S(1)} %get-tuple-element.108), channel_id=1, source_target_pairs={{0,2},{1,3},{2,0},{3,1},{4,6},{5,7},{6,4},{7,5},{8,10},{9,11},{10,... | collective-permute-start | bytes 552968 | tf_op jit(solution)/shard_map/ppermute | solution.py:40
  108.3 4.1 %collective-permute-start.28 = (f32[64,512]{1,0:T(8,128)S(1)}, f32[64,512]{1,0:T(8,128)S(1)}, u32[]{:S(2)}, u32[]{:S(2)}) collective-permute-start(f32[64,512]{1,0:T(8,128)S(1)} %add_add_fusion), channel_id=1, source_target_pairs={{0,4},{4,0},{8,12},{12,8},{1,5},{5,1},{9,13},{13,9},{2,6},{6,2},{1... | collective-permute-start | bytes 393224 | tf_op jit(solution)/shard_map/ppermute | solution.py:40
  113.2 8.9 %collective-permute-done.25 = bf16[144,640]{1,0:T(8,128)(2,1)S(1)} collective-permute-done((bf16[144,640]{1,0:T(8,128)(2,1)S(1)}, bf16[144,640]{1,0:T(8,128)(2,1)S(1)}, u32[]{:S(2)}, u32[]{:S(2)}) %collective-permute-start.25) | collective-permute-done | bytes 184352 | tf_op jit(solution)/shard_map/ppermute | solution.py:40
  123.4 1.7 %collective-permute-start.27 = (f32[64,512]{1,0:T(8,128)S(1)}, f32[64,512]{1,0:T(8,128)S(1)}, u32[]{:S(2)}, u32[]{:S(2)}) collective-permute-start(f32[64,512]{1,0:T(8,128)S(1)} %slice.291), channel_id=1, source_target_pairs={{0,4},{4,0},{8,12},{12,8},{1,5},{5,1},{9,13},{13,9},{2,6},{6,2},{1... | collective-permute-start | bytes 393224 | tf_op jit(solution)/shard_map/ppermute | solution.py:40
  (157 shorter events, 40.0 us)
Async XLA Ops:
  3.2 28.5 %collective-permute-start = (bf16[160,1024]{1,0:T(8,128)(2,1)}, bf16[160,1024]{1,0:T(8,128)(2,1)}, u32[]{:S(2)}, u32[]{:S(2)}) collective-permute-start(bf16[160,1024]{1,0:T(8,128)(2,1)} %get-tuple-element.90), channel_id=1, source_target_pairs={{0,1},{1,2},{2,3},{3,0},{4,5},{5,6},{6,7},{7,4},{8,9},{9,10},{10,1... | collective-permute-start | bytes 983048 | tf_op jit(solution)/shard_map/ppermute | solution.py:35
  5.3 26.4 %collective-permute-start.1 = (bf16[160,1024]{1,0:T(8,128)(2,1)}, bf16[160,1024]{1,0:T(8,128)(2,1)}, u32[]{:S(2)}, u32[]{:S(2)}) collective-permute-start(bf16[160,1024]{1,0:T(8,128)(2,1)} %get-tuple-element.89), channel_id=1, source_target_pairs={{0,2},{1,3},{2,0},{3,1},{4,6},{5,7},{6,4},{7,5},{8,10},{9,11},{10,... | collective-permute-start | bytes 983048 | tf_op jit(solution)/shard_map/ppermute | solution.py:35
  7.6 24.1 %collective-permute-start.2 = (bf16[160,1024]{1,0:T(8,128)(2,1)}, bf16[160,1024]{1,0:T(8,128)(2,1)}, u32[]{:S(2)}, u32[]{:S(2)}) collective-permute-start(bf16[160,1024]{1,0:T(8,128)(2,1)} %get-tuple-element.88), channel_id=1, source_target_pairs={{0,3},{1,0},{2,1},{3,2},{4,7},{5,4},{6,5},{7,6},{8,11},{9,8},{10,9... | collective-permute-start | bytes 983048 | tf_op jit(solution)/shard_map/ppermute | solution.py:35
  36.0 19.7 %collective-permute-start.3 = (bf16[64,1024]{1,0:T(8,128)(2,1)S(1)}, bf16[64,1024]{1,0:T(8,128)(2,1)S(1)}, u32[]{:S(2)}, u32[]{:S(2)}) collective-permute-start(bf16[64,1024]{1,0:T(8,128)(2,1)S(1)} %bitcast.213), channel_id=1, source_target_pairs={{0,1},{1,2},{2,3},{3,0},{4,5},{5,6},{6,7},{7,4},{8,9},{9,10},{10,1... | collective-permute-start | bytes 393224 | tf_op jit(solution)/shard_map/ppermute | solution.py:35
  41.5 14.2 %collective-permute-start.4 = (bf16[64,1024]{1,0:T(8,128)(2,1)S(1)}, bf16[64,1024]{1,0:T(8,128)(2,1)S(1)}, u32[]{:S(2)}, u32[]{:S(2)}) collective-permute-start(bf16[64,1024]{1,0:T(8,128)(2,1)S(1)} %bitcast.214), channel_id=1, source_target_pairs={{0,2},{1,3},{2,0},{3,1},{4,6},{5,7},{6,4},{7,5},{8,10},{9,11},{10,... | collective-permute-start | bytes 393224 | tf_op jit(solution)/shard_map/ppermute | solution.py:35
  41.8 13.9 %collective-permute-start.5 = (bf16[64,1024]{1,0:T(8,128)(2,1)S(1)}, bf16[64,1024]{1,0:T(8,128)(2,1)S(1)}, u32[]{:S(2)}, u32[]{:S(2)}) collective-permute-start(bf16[64,1024]{1,0:T(8,128)(2,1)S(1)} %bitcast.215), channel_id=1, source_target_pairs={{0,3},{1,0},{2,1},{3,2},{4,7},{5,4},{6,5},{7,6},{8,11},{9,8},{10,9... | collective-permute-start | bytes 393224 | tf_op jit(solution)/shard_map/ppermute | solution.py:35
  49.9 5.8 %collective-permute-start.6 = (bf16[2,4,64,640]{3,2,1,0:T(8,128)(2,1)S(1)}, bf16[2,4,64,640]{3,2,1,0:T(8,128)(2,1)S(1)}, u32[]{:S(2)}, u32[]{:S(2)}) collective-permute-start(bf16[2,4,64,640]{3,2,1,0:T(8,128)(2,1)S(1)} %fusion.36), channel_id=1, source_target_pairs={{0,4},{4,0},{8,12},{12,8},{1,5},{5,1},{9,13},{13,9},{2,6},{6,2},{1... | collective-permute-start | bytes 1966088 | tf_op jit(solution)/shard_map/ppermute | solution.py:40
  62.4 5.3 %collective-permute-start.10 = (bf16[64,128]{1,0:T(8,128)(2,1)S(1)}, bf16[64,128]{1,0:T(8,128)(2,1)S(1)}, u32[]{:S(2)}, u32[]{:S(2)}) collective-permute-start(bf16[64,128]{1,0:T(8,128)(2,1)S(1)} %get-tuple-element.113), channel_id=1, source_target_pairs={{0,12},{4,0},{8,4},{12,8},{1,13},{5,1},{9,5},{13,9},{2,14},{6,2},{... | collective-permute-start | bytes 49160 | tf_op jit(solution)/shard_map/ppermute | solution.py:35
  62.5 5.2 %collective-permute-start.9 = (bf16[64,128]{1,0:T(8,128)(2,1)S(1)}, bf16[64,128]{1,0:T(8,128)(2,1)S(1)}, u32[]{:S(2)}, u32[]{:S(2)}) collective-permute-start(bf16[64,128]{1,0:T(8,128)(2,1)S(1)} %get-tuple-element.112), channel_id=1, source_target_pairs={{0,4},{4,8},{8,12},{12,0},{1,5},{5,9},{9,13},{13,1},{2,6},{6,10},{... | collective-permute-start | bytes 49160 | tf_op jit(solution)/shard_map/ppermute | solution.py:35
  68.6 4.6 %collective-permute-start.11 = (bf16[64,1024]{1,0:T(8,128)(2,1)S(1)}, bf16[64,1024]{1,0:T(8,128)(2,1)S(1)}, u32[]{:S(2)}, u32[]{:S(2)}) collective-permute-start(bf16[64,1024]{1,0:T(8,128)(2,1)S(1)} %get-tuple-element.99), channel_id=1, source_target_pairs={{0,3},{1,0},{2,1},{3,2},{4,7},{5,4},{6,5},{7,6},{8,11},{9,8},{10,9... | collective-permute-start | bytes 393224 | tf_op jit(solution)/shard_map/ppermute | solution.py:35
  70.3 11.9 %collective-permute-start.12 = (bf16[64,1024]{1,0:T(8,128)(2,1)S(1)}, bf16[64,1024]{1,0:T(8,128)(2,1)S(1)}, u32[]{:S(2)}, u32[]{:S(2)}) collective-permute-start(bf16[64,1024]{1,0:T(8,128)(2,1)S(1)} %get-tuple-element.101), channel_id=1, source_target_pairs={{0,2},{1,3},{2,0},{3,1},{4,6},{5,7},{6,4},{7,5},{8,10},{9,11},{10,... | collective-permute-start | bytes 393224 | tf_op jit(solution)/shard_map/ppermute | solution.py:35
  70.7 11.5 %collective-permute-start.13 = (bf16[64,1024]{1,0:T(8,128)(2,1)S(1)}, bf16[64,1024]{1,0:T(8,128)(2,1)S(1)}, u32[]{:S(2)}, u32[]{:S(2)}) collective-permute-start(bf16[64,1024]{1,0:T(8,128)(2,1)S(1)} %get-tuple-element.100), channel_id=1, source_target_pairs={{0,1},{1,2},{2,3},{3,0},{4,5},{5,6},{6,7},{7,4},{8,9},{9,10},{10,1... | collective-permute-start | bytes 393224 | tf_op jit(solution)/shard_map/ppermute | solution.py:35
  70.9 11.7 %collective-permute-start.17 = (bf16[320,640]{1,0:T(8,128)(2,1)S(1)}, bf16[320,640]{1,0:T(8,128)(2,1)S(1)}, u32[]{:S(2)}, u32[]{:S(2)}) collective-permute-start(bf16[320,640]{1,0:T(8,128)(2,1)S(1)} %fusion.41), channel_id=1, source_target_pairs={{0,8},{4,12},{8,0},{12,4},{1,9},{5,13},{9,1},{13,5},{2,10},{6,14},... | collective-permute-start | bytes 1228808 | tf_op jit(solution)/shard_map/ppermute | solution.py:35
  73.2 9.3 %collective-permute-start.15 = (f32[8,128]{1,0:T(8,128)S(1)}, f32[8,128]{1,0:T(8,128)S(1)}, u32[]{:S(2)}, u32[]{:S(2)}) collective-permute-start(f32[8,128]{1,0:T(8,128)S(1)} %bitcast.237), channel_id=1, source_target_pairs={{0,4},{4,0},{8,12},{12,8},{1,5},{5,1},{9,13},{13,9},{2,6},{6,2},{1... | collective-permute-start | bytes 12296 | tf_op jit(solution)/shard_map/ppermute | solution.py:40
  75.3 7.3 %collective-permute-start.14 = (f32[64,128]{1,0:T(8,128)S(1)}, f32[64,128]{1,0:T(8,128)S(1)}, u32[]{:S(2)}, u32[]{:S(2)}) collective-permute-start(f32[64,128]{1,0:T(8,128)S(1)} %fusion.53), channel_id=1, source_target_pairs={{0,4},{4,0},{8,12},{12,8},{1,5},{5,1},{9,13},{13,9},{2,6},{6,2},{1... | collective-permute-start | bytes 98312 | tf_op jit(solution)/shard_map/ppermute | solution.py:40
  83.1 4.5 %collective-permute-start.19 = (f32[64,512]{1,0:T(8,128)S(1)}, f32[64,512]{1,0:T(8,128)S(1)}, u32[]{:S(2)}, u32[]{:S(2)}) collective-permute-start(f32[64,512]{1,0:T(8,128)S(1)} %fusion.28), channel_id=1, source_target_pairs={{0,4},{4,0},{8,12},{12,8},{1,5},{5,1},{9,13},{13,9},{2,6},{6,2},{1... | collective-permute-start | bytes 393224 | tf_op jit(solution)/shard_map/ppermute | solution.py:40
  89.8 12.6 %collective-permute-start.20 = (bf16[336,640]{1,0:T(8,128)(2,1)S(1)}, bf16[336,640]{1,0:T(8,128)(2,1)S(1)}, u32[]{:S(2)}, u32[]{:S(2)}) collective-permute-start(bf16[336,640]{1,0:T(8,128)(2,1)S(1)} %pad_maximum_fusion.2), channel_id=1, source_target_pairs={{0,8},{4,12},{8,0},{12,4},{1,9},{5,13},{9,1},{13,5},{2,10},{6,14},... | collective-permute-start | bytes 1290248 | tf_op jit(solution)/shard_map/ppermute | solution.py:35
  90.1 6.4 %collective-permute-start.21 = (bf16[64,1152]{1,0:T(8,128)(2,1)S(1)}, bf16[64,1152]{1,0:T(8,128)(2,1)S(1)}, u32[]{:S(2)}, u32[]{:S(2)}) collective-permute-start(bf16[64,1152]{1,0:T(8,128)(2,1)S(1)} %get-tuple-element.111), channel_id=1, source_target_pairs={{0,1},{1,0},{2,3},{3,2},{4,5},{5,4},{6,7},{7,6},{8,9},{9,8},{10,11... | collective-permute-start | bytes 442376 | tf_op jit(solution)/shard_map/ppermute | solution.py:40
  91.3 6.6 %collective-permute-start.22 = (bf16[64,1152]{1,0:T(8,128)(2,1)S(1)}, bf16[64,1152]{1,0:T(8,128)(2,1)S(1)}, u32[]{:S(2)}, u32[]{:S(2)}) collective-permute-start(bf16[64,1152]{1,0:T(8,128)(2,1)S(1)} %get-tuple-element.110), channel_id=1, source_target_pairs={{0,2},{1,3},{2,0},{3,1},{4,6},{5,7},{6,4},{7,5},{8,10},{9,11},{10,... | collective-permute-start | bytes 442376 | tf_op jit(solution)/shard_map/ppermute | solution.py:40
  92.6 9.8 %collective-permute-start.23 = (bf16[64,1152]{1,0:T(8,128)(2,1)S(1)}, bf16[64,1152]{1,0:T(8,128)(2,1)S(1)}, u32[]{:S(2)}, u32[]{:S(2)}) collective-permute-start(bf16[64,1152]{1,0:T(8,128)(2,1)S(1)} %get-tuple-element.109), channel_id=1, source_target_pairs={{0,3},{1,2},{2,1},{3,0},{4,7},{5,6},{6,5},{7,4},{8,11},{9,10},{10,... | collective-permute-start | bytes 442376 | tf_op jit(solution)/shard_map/ppermute | solution.py:40
  102.7 10.4 %collective-permute-start.26 = (bf16[144,640]{1,0:T(8,128)(2,1)S(1)}, bf16[144,640]{1,0:T(8,128)(2,1)S(1)}, u32[]{:S(2)}, u32[]{:S(2)}) collective-permute-start(bf16[144,640]{1,0:T(8,128)(2,1)S(1)} %get-tuple-element.107), channel_id=1, source_target_pairs={{0,3},{1,2},{2,1},{3,0},{4,7},{5,6},{6,5},{7,4},{8,11},{9,10},{10,... | collective-permute-start | bytes 552968 | tf_op jit(solution)/shard_map/ppermute | solution.py:40
  104.8 17.3 %collective-permute-start.25 = (bf16[144,640]{1,0:T(8,128)(2,1)S(1)}, bf16[144,640]{1,0:T(8,128)(2,1)S(1)}, u32[]{:S(2)}, u32[]{:S(2)}) collective-permute-start(bf16[144,640]{1,0:T(8,128)(2,1)S(1)} %get-tuple-element.108), channel_id=1, source_target_pairs={{0,2},{1,3},{2,0},{3,1},{4,6},{5,7},{6,4},{7,5},{8,10},{9,11},{10,... | collective-permute-start | bytes 552968 | tf_op jit(solution)/shard_map/ppermute | solution.py:40
  108.2 13.8 %collective-permute-start.24 = (bf16[144,640]{1,0:T(8,128)(2,1)S(1)}, bf16[144,640]{1,0:T(8,128)(2,1)S(1)}, u32[]{:S(2)}, u32[]{:S(2)}) collective-permute-start(bf16[144,640]{1,0:T(8,128)(2,1)S(1)} %get-tuple-element.106), channel_id=1, source_target_pairs={{0,1},{1,0},{2,3},{3,2},{4,5},{5,4},{6,7},{7,6},{8,9},{9,8},{10,11... | collective-permute-start | bytes 552968 | tf_op jit(solution)/shard_map/ppermute | solution.py:40
  108.3 18.2 %collective-permute-start.28 = (f32[64,512]{1,0:T(8,128)S(1)}, f32[64,512]{1,0:T(8,128)S(1)}, u32[]{:S(2)}, u32[]{:S(2)}) collective-permute-start(f32[64,512]{1,0:T(8,128)S(1)} %add_add_fusion), channel_id=1, source_target_pairs={{0,4},{4,0},{8,12},{12,8},{1,5},{5,1},{9,13},{13,9},{2,6},{6,2},{1... | collective-permute-start | bytes 393224 | tf_op jit(solution)/shard_map/ppermute | solution.py:40
  (19 other events, 126.2 us)

commit v2 on v1

--- a/solution.py
+++ b/solution.py
@@ -1,8 +1,11 @@
+import functools
 import math
 
 import jax
 import jax.numpy as jnp
 from jax import lax
+from jax.experimental import pallas as pl
+from jax.experimental.pallas import tpu as pltpu
 from jax.sharding import PartitionSpec as P
 
 LATENT = 64
@@ -95,23 +98,62 @@
 
 
 def pack(block, extra):
-    high = extra.astype(BF)
-    low = (extra - high.astype(F32)).astype(BF)
-    both = jnp.concatenate([high, low], axis=0)
+    high = lax.reduce_precision(extra, 8, 7)
+    both = jnp.concatenate([high, extra - high], axis=1).astype(BF)
     both = jnp.pad(both, ((0, 0), (0, block.shape[1] - both.shape[1])))
     return jnp.concatenate([block.astype(BF), both], axis=0)
 
 
-def unpack(packed, rows, high):
+def unpack(packed, rows):
     packed = packed.astype(F32)
-    extra = packed[rows:, :EDGE]
-    return packed[:rows], extra[:high] + extra[high:]
+    return packed[:rows], packed[rows:, :EDGE] + packed[rows:, EDGE : 2 * EDGE]
 
 
 def tree(pieces):
     while len(pieces) > 1:
         pieces = [a + b for a, b in zip(pieces[::2], pieces[1::2])]
     return pieces[0]
+
+
+def encode_kernel(step, *refs):
+    *slab_refs, placed_ref, out_t_ref, raw_ref, pre_ref, hidden_ref, latent_ref = refs
+    slab = slab_refs[0].shape[0]
+    hidden, cells = pre_ref.shape
+    for d, slab_ref in enumerate(slab_refs):
+        raw_ref[d * slab : (d + 1) * slab, :] = slab_ref[...]
+
+    latent = jnp.zeros(latent_ref.shape, F32)
+    for start in range(0, hidden, step):
+        rows = slice(start, start + step)
+        preact = jnp.dot(placed_ref[rows, :], raw_ref[...], preferred_element_type=F32)
+        pre_ref[rows, :] = preact
+        active = (preact * jax.nn.sigmoid(preact)).astype(BF)
+        hidden_ref[rows, :] = active
+        latent += jnp.dot(out_t_ref[:, rows], active, preferred_element_type=F32)
+    latent_ref[...] = latent.astype(BF)
+
+
+def encode(slabs, placed, out_t):
+    slab, cells = slabs[0].shape
+    hidden, feat = placed.shape
+    vmem = pl.BlockSpec(memory_space=pltpu.VMEM)
+    flops = 2 * hidden * cells * (feat + out_t.shape[0])
+    size = 4 * hidden * cells + 2 * (hidden * cells + 2 * feat * cells + hidden * feat)
+    return pl.pallas_call(
+        functools.partial(encode_kernel, hidden // 4),
+        out_shape=[
+            jax.ShapeDtypeStruct((feat, cells), BF),
+            jax.ShapeDtypeStruct((hidden, cells), F32),
+            jax.ShapeDtypeStruct((hidden, cells), BF),
+            jax.ShapeDtypeStruct((out_t.shape[0], cells), BF),
+        ],
+        in_specs=[vmem] * (len(slabs) + 2),
+        out_specs=[vmem] * 4,
+        compiler_params=pltpu.CompilerParams(vmem_limit_bytes=24 * 2**20),
+        cost_estimate=pl.CostEstimate(
+            flops=flops, bytes_accessed=size, transcendentals=hidden * cells
+        ),
+    )(*slabs, placed, out_t)
 
 
 def local(fields, enc_in, enc_out, dec_in, dec_out, hyper_weight, neighbours, edge_rows):
@@ -131,9 +173,7 @@
     def slab_for(d):
         return lax.dynamic_slice(stored, (0, ((me_l + d) % n_l) * cells), (slab, cells))
 
-    raw = jnp.concatenate(
-        [slab_for(0)] + [shift(slab_for(d), "level", d) for d in range(1, n_l)], axis=0
-    )
+    slabs = [slab_for(0)] + [shift(slab_for(d), "level", d) for d in range(1, n_l)]
     place = jnp.arange(feat, dtype=jnp.int32)
     source = (me_l - place // slab) % n_l
     target = (place % n_vars) * (n_lev * n_l) + source * n_lev + (place % slab) // n_vars
@@ -152,13 +192,11 @@
     valid = jnp.sum((neighbours < limit).astype(F32), axis=0)
     listed = (relative(edge_rows[0].reshape(1, 2 * EDGE)) == entry[:part]).astype(BF)
     placed = mm(enc_in, order).astype(BF)
-    raw, counts, valid, listed, placed, order = lax.optimization_barrier(
-        (raw, counts, valid, listed, placed, order)
-    )
-
-    pre_enc = mm(placed, raw)
-    hidden_enc = jax.nn.silu(pre_enc).astype(BF)
-    latent = mm_rows(enc_out, hidden_enc).astype(BF)
+    slabs, counts, valid, listed, placed, order = lax.optimization_barrier(
+        (slabs, counts, valid, listed, placed, order)
+    )
+
+    raw, pre_enc, hidden_enc, latent = encode(slabs, placed, enc_out.T)
 
     table = jnp.concatenate(
         [latent] + [shift(latent, "level", d) for d in range(1, n_l)], axis=1
@@ -194,17 +232,14 @@
     d_spread = grad_scale * (1.0 - scaled * scaled) / sigma * jax.nn.sigmoid(spread)
     d_params = jnp.concatenate([-direct, d_spread], axis=0).astype(BF)
     share = mm(hyper_weight, d_params) / valid
-    high = share.astype(BF)
-    low = (share - high.astype(F32)).astype(BF)
-    share = jnp.concatenate([high, low], axis=0)
-
-    both = mm_cells(share, counts[part:])
-    back = (both[:LATENT] + both[LATENT:]).astype(BF)
+    share = share.astype(BF)
+
+    back = mm_cells(share, counts[part:]).astype(BF)
     to_next, to_prev = back[:, EDGE:], back[:, :EDGE]
     back = jnp.concatenate([shift(to_next, "horiz", 1), shift(to_prev, "horiz", -1)], axis=1)
-    both = mm_cells(after(share, to_next, to_prev), counts[:part])
-    back, both = lax.optimization_barrier((back, both))
-    own = both[:LATENT] + both[LATENT:] + mm_cells(back, listed)
+    own = mm_cells(after(share, to_next, to_prev), counts[:part])
+    back, own = lax.optimization_barrier((back, own))
+    own = own + mm_cells(back, listed)
     got = [
         shift(own[:, d * cells : (d + 1) * cells].astype(BF), "level", -d) for d in range(1, n_l)
     ]
@@ -228,7 +263,6 @@
     hyper = hyper + swap(hyper, "horiz", 1)
     cell_loss = cell_loss.reshape(-1, EDGE)
     cell_loss = cell_loss + swap(cell_loss, "horiz", 1)
-    high = cell_loss.shape[0]
     d_total = (d_latent + direct + d_neighbour).astype(BF)
     d_total, hyper, cell_loss, *far = lax.optimization_barrier((d_total, hyper, cell_loss, *far))
 
@@ -254,37 +288,47 @@
     )
 
     arrived = to_rows_y(sent)
-    got_dec = [
+    got_dec = []
+    for d in range(1, n_l):
+        piece = pick(near_dec, me_l ^ d, 0).astype(BF).reshape(LATENT, -1)
+        got_dec.append(swap(jnp.concatenate([piece] + [half_dec] * (d == 1), axis=1), "level", d))
+    near, arrived, got_dec = lax.optimization_barrier((near, arrived, got_dec))
+
+    for piece in arrived:
+        near = near + piece[:rows].astype(F32)
+    near = near.reshape(n_l, rows // n_l, feat)
+    riders = [rider] + [piece[rows:] for piece in arrived]
+    riders = [unpack(piece, LATENT) for piece in riders]
+    rider = pack(*(sum_y(list(pieces)) for pieces in zip(*riders)))
+    span = got_dec[1].shape[1]
+    half_dec = (half_dec.astype(F32) + got_dec[0][:, span:].astype(F32)).astype(BF)
+    few = rows // n_l
+    wide = jnp.pad(half_dec, ((0, 0), (0, feat - width)))
+    got_enc = [
         swap(
             jnp.concatenate(
-                [pick(near_dec, me_l ^ d, 0).astype(BF).reshape(LATENT, -1), half_dec], axis=1
+                [pick(near, me_l ^ d, 0).astype(BF), rider] + [wide] * (d == 2), axis=0
             ),
             "level",
             d,
         )
         for d in range(1, n_l)
     ]
-    near, arrived, got_dec = lax.optimization_barrier((near, arrived, got_dec))
-
-    for piece in arrived:
-        near = near + piece[:rows].astype(F32)
-    near = near.reshape(n_l, rows // n_l, feat)
-    riders = [rider] + [piece[rows:] for piece in arrived]
-    riders = [unpack(piece, LATENT, high) for piece in riders]
-    rider = pack(*(sum_y(list(pieces)) for pieces in zip(*riders)))
-    got_enc = [
-        swap(jnp.concatenate([pick(near, me_l ^ d, 0).astype(BF), rider], axis=0), "level", d)
-        for d in range(1, n_l)
-    ]
-    few = rows // n_l
-    riders = [unpack(piece, LATENT, high) for piece in [rider] + [p[few:] for p in got_enc]]
+    size = few + rider.shape[0]
+    half_dec = half_dec.astype(F32) + got_enc[1][size:, :width].astype(F32)
+    got_enc = [piece[:size] for piece in got_enc]
+    riders = [unpack(piece, LATENT) for piece in [rider] + [p[few:] for p in got_enc]]
     half_enc, cell_loss = (tree(list(pieces)) for pieces in zip(*riders))
     grad_dec_out = pick(near_dec, me_l, 0)
     for piece in got_dec:
-        piece = piece[:, :-width].reshape(grad_dec_out.shape)
+        piece = piece[:, :span].reshape(grad_dec_out.shape)
         grad_dec_out = grad_dec_out + piece.astype(F32)
-    half_dec = tree([half_dec.astype(F32)] + [piece[:, -width:].astype(F32) for piece in got_dec])
-    grad_dec_in = both_halves(half_dec)
+    bit = 4
+    while bit < n_l:
+        half_dec = half_dec.astype(BF)
+        half_dec = half_dec.astype(F32) + swap(half_dec, "level", bit).astype(F32)
+        bit *= 2
+    grad_dec_in = both_halves(after(half_dec, *got_enc))
     grad_hyper = half_enc[:, width:]
     loss = (jnp.sum(cell_loss) / (part * n_h)).reshape(1)
     grad_enc_out = both_halves(half_enc[:, :width]).T

time: 129 us -> 126 us (0.977)
  starting transfers between devices: 38.4 us -> 34 us
  matrix products: 27.3 us -> 24.1 us
  Pallas kernels: 0 us -> 2.45 us
  waiting for transfers between devices: 28.7 us -> 31 us
  other arithmetic: 25.3 us -> 23.9 us
    ppermute x14, starting transfers between devices: 19.6 us -> 13.9 us  [swap(): return lax.ppermute(block, axis, [(i, i ^ bit) for i in range(count)])]
    pallas_call x0 -> x1, Pallas kernels: none -> 2.45 us  [encode(): pl.pallas_call(functools.partial(encode_kernel, hidden // 4), out_shape=[...]
    dot_general x11 -> x10, matrix products: 13.7 us -> 11.5 us  [mm(): return jnp.dot(left, right, preferred_element_type=F32)]
    unnamed x28, local copies, waits for them, and re-layouts: 0.09 us -> 1.42 us
    concatenate x6 -> x5, other arithmetic: 1.39 us -> 0.08 us  [the longest x2 0.05 us: local(): jnp.concatenate([pick(near, me_l ^ d, 0).astype(BF), rider] + [wide] * (d...]
    ppermute x15, starting transfers between devices: 18.9 us -> 20.2 us  [shift(): lax.ppermute(block, axis, [(i, (i + step) % count) for i in range(count)])]
    dot_general x4 -> x3, matrix products: 3.69 us -> 3.15 us  [mm_rows(): lax.dot_general(left, right, (((0,), (0,)), ((), ())), preferred_element_...]
  transfers between devices with their start and end apart: 29 -> 29, of which waited for: 8 -> 10; matrix products, arithmetic and copies ran while one was open for 35% -> 34% of each run, Pallas kernels for 0% -> 0%
where the time goes in v2:
time: 126 us; the launch traced here: 125 us
  starting transfers between devices  34 us (27%)
  waiting for transfers between devices  31 us (25%)
  matrix products  24.1 us (19%)
  other arithmetic  23.9 us (19%)
  local copies, waits for them, and re-layouts  6.29 us (5%)
  between operations  3.34 us (3%)
  Pallas kernels  2.45 us (2%)
    ppermute x15, starting transfers between devices, shift(): lax.ppermute(block, axis, [(i, (i + step) % count) for i in range(count)])  20.2 us
    ppermute x14, waiting for transfers between devices, swap(): return lax.ppermute(block, axis, [(i, i ^ bit) for i in range(count)])  19.1 us
    convert_element_type x1, other arithmetic, local(): counts = counts.astype(BF)  15.1 us
    ppermute x14, starting transfers between devices, swap(): return lax.ppermute(block, axis, [(i, i ^ bit) for i in range(count)])  13.9 us
    ppermute x15, waiting for transfers between devices, shift(): lax.ppermute(block, axis, [(i, (i + step) % count) for i in range(count)])  11.9 us
    dot_general x10, matrix products, mm(): return jnp.dot(left, right, preferred_element_type=F32)  11.5 us
    dot_general x11, matrix products, mm_cells(): lax.dot_general(left, right, (((1,), (1,)), ((), ())), preferred_element_...  9.36 us
    dot_general x3, matrix products, mm_rows(): lax.dot_general(left, right, (((0,), (0,)), ((), ())), preferred_element_...  3.15 us
  transfers between devices with their start and end apart: 29, of which 10 were waited for; matrix products, arithmetic and copies ran while one was open for 34% of the time, Pallas kernels for 0%

profile of v2, /device:TPU:1, one launch (start us, length us, event | category | flops | bytes accessed | tf_op | source)
XLA Modules:
  0.0 125.1 jit_solution(6399058634406650574)
XLA Ops:
  0.7 2.2 %constant_dynamic-slice_fusion.2 = (bf16[160,1024]{1,0:T(8,128)(2,1)S(1)}, bf16[160,1024]{1,0:T(8,128)(2,1)S(1)}, bf16[160,1024]{1,0:T(8,128)(2,1)}, bf16[160,1024]{1,0:T(8,128)(2,1)S(1)}) fusion(bf16[160,4096]{1,0:T(8,128)(2,1)} %bitcast.208, s32[]{:T(128)S(6)} %select_n.226, s32[]{:T(128)S(6)} %select_n.224, s32[]{:T(128)S(6)} %select_n.222, s32[]{:T(128)S(6)} %select_n.220), kind=kLoop, calls=%fused_computation.192 | loop fusion | bytes 2621456 | tf_op jit(solution)/shard_map/dynamic_slice | solution.py:174
  3.0 2.1 %collective-permute-start = (bf16[160,1024]{1,0:T(8,128)(2,1)}, bf16[160,1024]{1,0:T(8,128)(2,1)S(1)}, u32[]{:S(2)}, u32[]{:S(2)}) collective-permute-start(bf16[160,1024]{1,0:T(8,128)(2,1)} %get-tuple-element.105), channel_id=1, source_target_pairs={{0,1},{1,2},{2,3},{3,0},{4,5},{5,6},{6,7},{7,4},{8,9},{9,10},{10,1... | collective-permute-start | bytes 983048 | tf_op jit(solution)/shard_map/ppermute | solution.py:38
  5.1 2.3 %collective-permute-start.1 = (bf16[160,1024]{1,0:T(8,128)(2,1)S(1)}, bf16[160,1024]{1,0:T(8,128)(2,1)S(1)}, u32[]{:S(2)}, u32[]{:S(2)}) collective-permute-start(bf16[160,1024]{1,0:T(8,128)(2,1)S(1)} %get-tuple-element.104), channel_id=1, source_target_pairs={{0,2},{1,3},{2,0},{3,1},{4,6},{5,7},{6,4},{7,5},{8,10},{9,11},{10,... | collective-permute-start | bytes 983048 | tf_op jit(solution)/shard_map/ppermute | solution.py:38
  9.8 1.7 %compare_convert_fusion = bf16[4096,256]{1,0:T(8,128)(2,1)} fusion(s32[256]{0:T(256)S(1)} %fusion.114, s32[4096]{0:T(1024)S(1)} %bitcast.214), kind=kLoop, calls=%fused_computation.22 | loop fusion | flops 2097152 | bytes 2114560 | tf_op jit(solution)/shard_map/convert_element_type | solution.py:193
  11.5 15.1 %add_convert_fusion = bf16[4352,1024]{1,0:T(8,128)(2,1)} fusion(s32[1024]{0:T(1024)S(1)} %bitcast.218, s32[1024]{0:T(1024)S(1)} %bitcast.219, s32[1024]{0:T(1024)S(1)} %bitcast.220, s32[1024]{0:T(1024)S(1)} %bitcast.221, s32[1024]{0:T(1024)S(1)} %bitcast.222, s32[1024]{0:T(1024)S(1)} %bitcast.217), kind=kLoop, calls=%fused_computation | loop fusion | flops 80216064 | bytes 8937472 | tf_op jit(solution)/shard_map/convert_element_type | solution.py:191
  27.8 2.7 %fusion.28.refs_4_ = bf16[1024,640]{1,0:T(8,128)(2,1)S(1)} fusion(bf16[1024,640]{1,0:T(8,128)(2,1)} %param.9, s32[640]{0:T(1024)S(1)} %fusion.96), kind=kOutput, calls=%fused_computation.49 | convolution fusion | flops 839925760 | bytes 2624000 | tf_op jit(solution)/shard_map/dot_general | solution.py:20
  30.5 2.5 %shard_map.135 = (bf16[640,1024]{1,0:T(8,128)(2,1)S(1)}, f32[1024,1024]{1,0:T(8,128)S(1)}, bf16[1024,1024]{1,0:T(8,128)(2,1)S(1)}, bf16[64,1024]{1,0:T(8,128)(2,1)S(1)}) custom-call(bf16[160,1024]{1,0:T(8,128)(2,1)S(1)} %get-tuple-element.49.refs_0_, bf16[160,1024]{1,0:T(8,128)(2,1)S(1)} %collective-permute-done.refs_1_, ...), custom_call_target="tpu_custom_call" | custom-call | flops 1476395008 | bytes 10223616 | tf_op jit(solution)/shard_map/pallas_call | solution.py:142
  32.9 6.5 %collective-permute-start.3 = (bf16[64,1024]{1,0:T(8,128)(2,1)S(1)}, bf16[64,1024]{1,0:T(8,128)(2,1)S(1)}, u32[]{:S(2)}, u32[]{:S(2)}) collective-permute-start(bf16[64,1024]{1,0:T(8,128)(2,1)S(1)} %get-tuple-element.54), channel_id=1, source_target_pairs={{0,1},{1,2},{2,3},{3,0},{4,5},{5,6},{6,7},{7,4},{8,9},{9,10},{10,1... | collective-permute-start | bytes 393224 | tf_op jit(solution)/shard_map/ppermute | solution.py:38
  39.7 1.9 %collective-permute-start.5 = (bf16[64,1024]{1,0:T(8,128)(2,1)S(1)}, bf16[64,1024]{1,0:T(8,128)(2,1)S(1)}, u32[]{:S(2)}, u32[]{:S(2)}) collective-permute-start(bf16[64,1024]{1,0:T(8,128)(2,1)S(1)} %get-tuple-element.54), channel_id=1, source_target_pairs={{0,3},{1,0},{2,1},{3,2},{4,7},{5,4},{6,5},{7,6},{8,11},{9,8},{10,9... | collective-permute-start | bytes 393224 | tf_op jit(solution)/shard_map/ppermute | solution.py:38
  42.9 1.6 %fusion.126 = f32[1024,640]{0,1:T(8,128)S(1)} fusion(bf16[1024,1024]{0,1:T(8,128)(2,1)S(1)} %get-tuple-element.136, bf16[1024,640]{1,0:T(8,128)(2,1)S(1)} %copy-done), kind=kOutput, calls=%fused_computation.264 | convolution fusion | flops 1342177280 | bytes 6029312 | tf_op jit(solution)/shard_map/dot_general | solution.py:24
  45.8 1.9 %fusion.118 = f32[1024,640]{1,0:T(8,128)S(1)} fusion(bf16[1024,1024]{0,1:T(8,128)(2,1)S(1)} %get-tuple-element.136, bf16[640,1024]{1,0:T(8,128)(2,1)S(1)} %get-tuple-element.139, f32[1024,640]{0,1:T(8,128)S(1)} %fusion.126), kind=kOutput, calls=%fused_computation.258 | convolution fusion | flops 1344798720 | bytes 8650752 | tf_op jit(solution)/shard_map/dot_general | solution.py:28
  48.9 2.7 %fusion.4 = bf16[1024,1024]{0,1:T(8,128)(2,1)S(1)} fusion(f32[1024,1024]{1,0:T(8,128)S(1)} %get-tuple-element.137, bf16[1024,640]{1,0:T(8,128)(2,1)S(1)} %copy-done, bf16[640,1024]{1,0:T(8,128)(2,1)S(1)} %get-tuple-element.139, f32[1024,640]{0,1:T(8,128)S(1)} %fusion.126), kind=kOutput, calls=%fused_computation.12 | convolution fusion | flops 1354235904 | bytes 11534336 | tf_op jit(solution)/shard_map/dot_general | solution.py:20
  61.7 1.7 %collective-permute-start.9 = (bf16[64,128]{1,0:T(8,128)(2,1)S(1)}, bf16[64,128]{1,0:T(8,128)(2,1)S(1)}, u32[]{:S(2)}, u32[]{:S(2)}) collective-permute-start(bf16[64,128]{1,0:T(8,128)(2,1)S(1)} %get-tuple-element.124), channel_id=1, source_target_pairs={{0,4},{4,8},{8,12},{12,0},{1,5},{5,9},{9,13},{13,1},{2,6},{6,10},{... | collective-permute-start | bytes 49160 | tf_op jit(solution)/shard_map/ppermute | solution.py:38
  63.4 2.7 %fusion = f32[64,4096]{1,0:T(8,128)S(1)} fusion(bf16[64,1024]{1,0:T(8,128)(2,1)S(1)} %bitcast.224, bf16[4352,1024]{1,0:T(8,128)(2,1)S(1)} %bitcast.202), kind=kOutput, calls=%fused_computation.7 | convolution fusion | flops 536870912 | bytes 9568256 | tf_op jit(solution)/shard_map/dot_general | solution.py:28
  67.7 1.7 %collective-permute-start.11 = (bf16[64,1024]{1,0:T(8,128)(2,1)S(1)}, bf16[64,1024]{1,0:T(8,128)(2,1)S(1)}, u32[]{:S(2)}, u32[]{:S(2)}) collective-permute-start(bf16[64,1024]{1,0:T(8,128)(2,1)S(1)} %get-tuple-element.115), channel_id=1, source_target_pairs={{0,3},{1,0},{2,1},{3,2},{4,7},{5,4},{6,5},{7,6},{8,11},{9,8},{10,9... | collective-permute-start | bytes 393224 | tf_op jit(solution)/shard_map/ppermute | solution.py:38
  70.4 1.9 %collective-permute-done.11 = bf16[64,1024]{1,0:T(8,128)(2,1)S(1)} collective-permute-done((bf16[64,1024]{1,0:T(8,128)(2,1)S(1)}, bf16[64,1024]{1,0:T(8,128)(2,1)S(1)}, u32[]{:S(2)}, u32[]{:S(2)}) %collective-permute-start.11) | collective-permute-done | bytes 131104 | tf_op jit(solution)/shard_map/ppermute | solution.py:38
  72.3 1.8 %collective-permute-start.15 = (f32[8,128]{1,0:T(8,128)S(1)}, f32[8,128]{1,0:T(8,128)S(1)}, u32[]{:S(2)}, u32[]{:S(2)}) collective-permute-start(f32[8,128]{1,0:T(8,128)S(1)} %bitcast.223), channel_id=1, source_target_pairs={{0,4},{4,0},{8,12},{12,8},{1,5},{5,1},{9,13},{13,9},{2,6},{6,2},{1... | collective-permute-start | bytes 12296 | tf_op jit(solution)/shard_map/ppermute | solution.py:43
  74.4 6.9 %collective-permute-done.12 = bf16[64,1024]{1,0:T(8,128)(2,1)S(1)} collective-permute-done((bf16[64,1024]{1,0:T(8,128)(2,1)S(1)}, bf16[64,1024]{1,0:T(8,128)(2,1)S(1)}, u32[]{:S(2)}, u32[]{:S(2)}) %collective-permute-start.12) | collective-permute-done | bytes 131104 | tf_op jit(solution)/shard_map/ppermute | solution.py:38
  92.8 1.8 %collective-permute-done.22 = bf16[64,640]{1,0:T(8,128)(2,1)S(1)} collective-permute-done((bf16[64,640]{1,0:T(8,128)(2,1)S(1)}, bf16[64,640]{1,0:T(8,128)(2,1)S(1)}, u32[]{:S(2)}, u32[]{:S(2)}) %collective-permute-start.22) | collective-permute-done | bytes 81952 | tf_op jit(solution)/shard_map/ppermute | solution.py:43
  94.6 3.5 %collective-permute-done.23 = bf16[64,640]{1,0:T(8,128)(2,1)S(1)} collective-permute-done((bf16[64,640]{1,0:T(8,128)(2,1)S(1)}, bf16[64,640]{1,0:T(8,128)(2,1)S(1)}, u32[]{:S(2)}, u32[]{:S(2)}) %collective-permute-start.23) | collective-permute-done | bytes 81952 | tf_op jit(solution)/shard_map/ppermute | solution.py:43
  101.1 2.1 %collective-permute-start.26 = (bf16[136,640]{1,0:T(8,128)(2,1)S(1)}, bf16[136,640]{1,0:T(8,128)(2,1)S(1)}, u32[]{:S(2)}, u32[]{:S(2)}) collective-permute-start(bf16[136,640]{1,0:T(8,128)(2,1)S(1)} %get-tuple-element.123), channel_id=1, source_target_pairs={{0,3},{1,2},{2,1},{3,0},{4,7},{5,6},{6,5},{7,4},{8,11},{9,10},{10,... | collective-permute-start | bytes 522248 | tf_op jit(solution)/shard_map/ppermute | solution.py:43
  103.9 8.0 %collective-permute-done.26 = bf16[136,640]{1,0:T(8,128)(2,1)S(1)} collective-permute-done((bf16[136,640]{1,0:T(8,128)(2,1)S(1)}, bf16[136,640]{1,0:T(8,128)(2,1)S(1)}, u32[]{:S(2)}, u32[]{:S(2)}) %collective-permute-start.26) | collective-permute-done | bytes 174112 | tf_op jit(solution)/shard_map/ppermute | solution.py:43
  112.8 4.5 %collective-permute-done.25 = bf16[200,640]{1,0:T(8,128)(2,1)S(1)} collective-permute-done((bf16[200,640]{1,0:T(8,128)(2,1)S(1)}, bf16[200,640]{1,0:T(8,128)(2,1)S(1)}, u32[]{:S(2)}, u32[]{:S(2)}) %collective-permute-start.25) | collective-permute-done | bytes 256032 | tf_op jit(solution)/shard_map/ppermute | solution.py:43
  118.6 2.4 %collective-permute-start.28 = (f32[64,512]{1,0:T(8,128)S(1)}, f32[64,512]{1,0:T(8,128)S(1)}, u32[]{:S(2)}, u32[]{:S(2)}) collective-permute-start(f32[64,512]{1,0:T(8,128)S(1)} %convert_add_fusion.3), channel_id=1, source_target_pairs={{0,4},{4,0},{8,12},{12,8},{1,5},{5,1},{9,13},{13,9},{2,6},{6,2},{1... | collective-permute-start | bytes 393224 | tf_op jit(solution)/shard_map/ppermute | solution.py:43
  (156 shorter events, 39.5 us)
Async XLA Ops:
  3.0 27.5 %collective-permute-start = (bf16[160,1024]{1,0:T(8,128)(2,1)}, bf16[160,1024]{1,0:T(8,128)(2,1)S(1)}, u32[]{:S(2)}, u32[]{:S(2)}) collective-permute-start(bf16[160,1024]{1,0:T(8,128)(2,1)} %get-tuple-element.105), channel_id=1, source_target_pairs={{0,1},{1,2},{2,3},{3,0},{4,5},{5,6},{6,7},{7,4},{8,9},{9,10},{10,1... | collective-permute-start | bytes 983048 | tf_op jit(solution)/shard_map/ppermute | solution.py:38
  5.1 25.4 %collective-permute-start.1 = (bf16[160,1024]{1,0:T(8,128)(2,1)S(1)}, bf16[160,1024]{1,0:T(8,128)(2,1)S(1)}, u32[]{:S(2)}, u32[]{:S(2)}) collective-permute-start(bf16[160,1024]{1,0:T(8,128)(2,1)S(1)} %get-tuple-element.104), channel_id=1, source_target_pairs={{0,2},{1,3},{2,0},{3,1},{4,6},{5,7},{6,4},{7,5},{8,10},{9,11},{10,... | collective-permute-start | bytes 983048 | tf_op jit(solution)/shard_map/ppermute | solution.py:38
  7.4 23.1 %collective-permute-start.2 = (bf16[160,1024]{1,0:T(8,128)(2,1)S(1)}, bf16[160,1024]{1,0:T(8,128)(2,1)S(1)}, u32[]{:S(2)}, u32[]{:S(2)}) collective-permute-start(bf16[160,1024]{1,0:T(8,128)(2,1)S(1)} %get-tuple-element.103), channel_id=1, source_target_pairs={{0,3},{1,0},{2,1},{3,2},{4,7},{5,4},{6,5},{7,6},{8,11},{9,8},{10,9... | collective-permute-start | bytes 983048 | tf_op jit(solution)/shard_map/ppermute | solution.py:38
  32.9 20.7 %collective-permute-start.3 = (bf16[64,1024]{1,0:T(8,128)(2,1)S(1)}, bf16[64,1024]{1,0:T(8,128)(2,1)S(1)}, u32[]{:S(2)}, u32[]{:S(2)}) collective-permute-start(bf16[64,1024]{1,0:T(8,128)(2,1)S(1)} %get-tuple-element.54), channel_id=1, source_target_pairs={{0,1},{1,2},{2,3},{3,0},{4,5},{5,6},{6,7},{7,4},{8,9},{9,10},{10,1... | collective-permute-start | bytes 393224 | tf_op jit(solution)/shard_map/ppermute | solution.py:38
  39.4 14.2 %collective-permute-start.4 = (bf16[64,1024]{1,0:T(8,128)(2,1)S(1)}, bf16[64,1024]{1,0:T(8,128)(2,1)S(1)}, u32[]{:S(2)}, u32[]{:S(2)}) collective-permute-start(bf16[64,1024]{1,0:T(8,128)(2,1)S(1)} %get-tuple-element.54), channel_id=1, source_target_pairs={{0,2},{1,3},{2,0},{3,1},{4,6},{5,7},{6,4},{7,5},{8,10},{9,11},{10,... | collective-permute-start | bytes 393224 | tf_op jit(solution)/shard_map/ppermute | solution.py:38
  39.7 14.0 %collective-permute-start.5 = (bf16[64,1024]{1,0:T(8,128)(2,1)S(1)}, bf16[64,1024]{1,0:T(8,128)(2,1)S(1)}, u32[]{:S(2)}, u32[]{:S(2)}) collective-permute-start(bf16[64,1024]{1,0:T(8,128)(2,1)S(1)} %get-tuple-element.54), channel_id=1, source_target_pairs={{0,3},{1,0},{2,1},{3,2},{4,7},{5,4},{6,5},{7,6},{8,11},{9,8},{10,9... | collective-permute-start | bytes 393224 | tf_op jit(solution)/shard_map/ppermute | solution.py:38
  47.8 5.9 %collective-permute-start.6 = (bf16[2,4,64,640]{3,2,1,0:T(8,128)(2,1)S(1)}, bf16[2,4,64,640]{3,2,1,0:T(8,128)(2,1)S(1)}, u32[]{:S(2)}, u32[]{:S(2)}) collective-permute-start(bf16[2,4,64,640]{3,2,1,0:T(8,128)(2,1)S(1)} %fusion.39), channel_id=1, source_target_pairs={{0,4},{4,0},{8,12},{12,8},{1,5},{5,1},{9,13},{13,9},{2,6},{6,2},{1... | collective-permute-start | bytes 1966088 | tf_op jit(solution)/shard_map/ppermute | solution.py:43
  61.6 5.1 %collective-permute-start.10 = (bf16[64,128]{1,0:T(8,128)(2,1)S(1)}, bf16[64,128]{1,0:T(8,128)(2,1)S(1)}, u32[]{:S(2)}, u32[]{:S(2)}) collective-permute-start(bf16[64,128]{1,0:T(8,128)(2,1)S(1)} %get-tuple-element.125), channel_id=1, source_target_pairs={{0,12},{4,0},{8,4},{12,8},{1,13},{5,1},{9,5},{13,9},{2,14},{6,2},{... | collective-permute-start | bytes 49160 | tf_op jit(solution)/shard_map/ppermute | solution.py:38
  61.7 5.0 %collective-permute-start.9 = (bf16[64,128]{1,0:T(8,128)(2,1)S(1)}, bf16[64,128]{1,0:T(8,128)(2,1)S(1)}, u32[]{:S(2)}, u32[]{:S(2)}) collective-permute-start(bf16[64,128]{1,0:T(8,128)(2,1)S(1)} %get-tuple-element.124), channel_id=1, source_target_pairs={{0,4},{4,8},{8,12},{12,0},{1,5},{5,9},{9,13},{13,1},{2,6},{6,10},{... | collective-permute-start | bytes 49160 | tf_op jit(solution)/shard_map/ppermute | solution.py:38
  67.7 4.6 %collective-permute-start.11 = (bf16[64,1024]{1,0:T(8,128)(2,1)S(1)}, bf16[64,1024]{1,0:T(8,128)(2,1)S(1)}, u32[]{:S(2)}, u32[]{:S(2)}) collective-permute-start(bf16[64,1024]{1,0:T(8,128)(2,1)S(1)} %get-tuple-element.115), channel_id=1, source_target_pairs={{0,3},{1,0},{2,1},{3,2},{4,7},{5,4},{6,5},{7,6},{8,11},{9,8},{10,9... | collective-permute-start | bytes 393224 | tf_op jit(solution)/shard_map/ppermute | solution.py:38
  69.4 12.0 %collective-permute-start.12 = (bf16[64,1024]{1,0:T(8,128)(2,1)S(1)}, bf16[64,1024]{1,0:T(8,128)(2,1)S(1)}, u32[]{:S(2)}, u32[]{:S(2)}) collective-permute-start(bf16[64,1024]{1,0:T(8,128)(2,1)S(1)} %get-tuple-element.117), channel_id=1, source_target_pairs={{0,2},{1,3},{2,0},{3,1},{4,6},{5,7},{6,4},{7,5},{8,10},{9,11},{10,... | collective-permute-start | bytes 393224 | tf_op jit(solution)/shard_map/ppermute | solution.py:38
  69.8 11.5 %collective-permute-start.13 = (bf16[64,1024]{1,0:T(8,128)(2,1)S(1)}, bf16[64,1024]{1,0:T(8,128)(2,1)S(1)}, u32[]{:S(2)}, u32[]{:S(2)}) collective-permute-start(bf16[64,1024]{1,0:T(8,128)(2,1)S(1)} %get-tuple-element.116), channel_id=1, source_target_pairs={{0,1},{1,2},{2,3},{3,0},{4,5},{5,6},{6,7},{7,4},{8,9},{9,10},{10,1... | collective-permute-start | bytes 393224 | tf_op jit(solution)/shard_map/ppermute | solution.py:38
  70.0 11.7 %collective-permute-start.17 = (bf16[320,640]{1,0:T(8,128)(2,1)S(1)}, bf16[320,640]{1,0:T(8,128)(2,1)S(1)}, u32[]{:S(2)}, u32[]{:S(2)}) collective-permute-start(bf16[320,640]{1,0:T(8,128)(2,1)S(1)} %fusion.44), channel_id=1, source_target_pairs={{0,8},{4,12},{8,0},{12,4},{1,9},{5,13},{9,1},{13,5},{2,10},{6,14},... | collective-permute-start | bytes 1228808 | tf_op jit(solution)/shard_map/ppermute | solution.py:38
  72.3 9.3 %collective-permute-start.15 = (f32[8,128]{1,0:T(8,128)S(1)}, f32[8,128]{1,0:T(8,128)S(1)}, u32[]{:S(2)}, u32[]{:S(2)}) collective-permute-start(f32[8,128]{1,0:T(8,128)S(1)} %bitcast.223), channel_id=1, source_target_pairs={{0,4},{4,0},{8,12},{12,8},{1,5},{5,1},{9,13},{13,9},{2,6},{6,2},{1... | collective-permute-start | bytes 12296 | tf_op jit(solution)/shard_map/ppermute | solution.py:43
  74.4 7.3 %collective-permute-start.14 = (f32[64,128]{1,0:T(8,128)S(1)}, f32[64,128]{1,0:T(8,128)S(1)}, u32[]{:S(2)}, u32[]{:S(2)}) collective-permute-start(f32[64,128]{1,0:T(8,128)S(1)} %fusion.55), channel_id=1, source_target_pairs={{0,4},{4,0},{8,12},{12,8},{1,5},{5,1},{9,13},{13,9},{2,6},{6,2},{1... | collective-permute-start | bytes 98312 | tf_op jit(solution)/shard_map/ppermute | solution.py:43
  83.7 3.8 %collective-permute-start.18 = (bf16[512,640]{1,0:T(8,128)(2,1)S(1)}, bf16[512,640]{1,0:T(8,128)(2,1)S(1)}, u32[]{:S(2)}, u32[]{:S(2)}) collective-permute-start(bf16[512,640]{1,0:T(8,128)(2,1)S(1)} %convolution_convert_fusion.1), channel_id=1, source_target_pairs={{0,4},{4,0},{8,12},{12,8},{1,5},{5,1},{9,13},{13,9},{2,6},{6,2},{1... | collective-permute-start | bytes 1966088 | tf_op jit(solution)/shard_map/ppermute | solution.py:43
  88.6 11.0 %collective-permute-start.20 = (bf16[328,640]{1,0:T(8,128)(2,1)S(1)}, bf16[328,640]{1,0:T(8,128)(2,1)S(1)}, u32[]{:S(2)}, u32[]{:S(2)}) collective-permute-start(bf16[328,640]{1,0:T(8,128)(2,1)S(1)} %pad_maximum_fusion.1), channel_id=1, source_target_pairs={{0,8},{4,12},{8,0},{12,4},{1,9},{5,13},{9,1},{13,5},{2,10},{6,14},... | collective-permute-start | bytes 1259528 | tf_op jit(solution)/shard_map/ppermute | solution.py:38
  89.1 9.0 %collective-permute-start.21 = (bf16[64,1152]{1,0:T(8,128)(2,1)S(1)}, bf16[64,1152]{1,0:T(8,128)(2,1)S(1)}, u32[]{:S(2)}, u32[]{:S(2)}) collective-permute-start(bf16[64,1152]{1,0:T(8,128)(2,1)S(1)} %pad_maximum_fusion.10), channel_id=1, source_target_pairs={{0,1},{1,0},{2,3},{3,2},{4,5},{5,4},{6,7},{7,6},{8,9},{9,8},{10,11... | collective-permute-start | bytes 442376 | tf_op jit(solution)/shard_map/ppermute | solution.py:43
  90.3 4.3 %collective-permute-start.22 = (bf16[64,640]{1,0:T(8,128)(2,1)S(1)}, bf16[64,640]{1,0:T(8,128)(2,1)S(1)}, u32[]{:S(2)}, u32[]{:S(2)}) collective-permute-start(bf16[64,640]{1,0:T(8,128)(2,1)S(1)} %get-tuple-element.113), channel_id=1, source_target_pairs={{0,2},{1,3},{2,0},{3,1},{4,6},{5,7},{6,4},{7,5},{8,10},{9,11},{10,... | collective-permute-start | bytes 245768 | tf_op jit(solution)/shard_map/ppermute | solution.py:43
  91.6 6.5 %collective-permute-start.23 = (bf16[64,640]{1,0:T(8,128)(2,1)S(1)}, bf16[64,640]{1,0:T(8,128)(2,1)S(1)}, u32[]{:S(2)}, u32[]{:S(2)}) collective-permute-start(bf16[64,640]{1,0:T(8,128)(2,1)S(1)} %get-tuple-element.112), channel_id=1, source_target_pairs={{0,3},{1,2},{2,1},{3,0},{4,7},{5,6},{6,5},{7,4},{8,11},{9,10},{10,... | collective-permute-start | bytes 245768 | tf_op jit(solution)/shard_map/ppermute | solution.py:43
  99.9 17.4 %collective-permute-start.25 = (bf16[200,640]{1,0:T(8,128)(2,1)S(1)}, bf16[200,640]{1,0:T(8,128)(2,1)S(1)}, u32[]{:S(2)}, u32[]{:S(2)}) collective-permute-start(bf16[200,640]{1,0:T(8,128)(2,1)S(1)} %fusion.54), channel_id=1, source_target_pairs={{0,2},{1,3},{2,0},{3,1},{4,6},{5,7},{6,4},{7,5},{8,10},{9,11},{10,... | collective-permute-start | bytes 768008 | tf_op jit(solution)/shard_map/ppermute | solution.py:43
  101.1 10.8 %collective-permute-start.26 = (bf16[136,640]{1,0:T(8,128)(2,1)S(1)}, bf16[136,640]{1,0:T(8,128)(2,1)S(1)}, u32[]{:S(2)}, u32[]{:S(2)}) collective-permute-start(bf16[136,640]{1,0:T(8,128)(2,1)S(1)} %get-tuple-element.123), channel_id=1, source_target_pairs={{0,3},{1,2},{2,1},{3,0},{4,7},{5,6},{6,5},{7,4},{8,11},{9,10},{10,... | collective-permute-start | bytes 522248 | tf_op jit(solution)/shard_map/ppermute | solution.py:43
  103.2 9.7 %collective-permute-start.24 = (bf16[136,640]{1,0:T(8,128)(2,1)S(1)}, bf16[136,640]{1,0:T(8,128)(2,1)S(1)}, u32[]{:S(2)}, u32[]{:S(2)}) collective-permute-start(bf16[136,640]{1,0:T(8,128)(2,1)S(1)} %get-tuple-element.122), channel_id=1, source_target_pairs={{0,1},{1,0},{2,3},{3,2},{4,5},{5,4},{6,7},{7,6},{8,9},{9,8},{10,11... | collective-permute-start | bytes 522248 | tf_op jit(solution)/shard_map/ppermute | solution.py:43
  118.6 3.8 %collective-permute-start.28 = (f32[64,512]{1,0:T(8,128)S(1)}, f32[64,512]{1,0:T(8,128)S(1)}, u32[]{:S(2)}, u32[]{:S(2)}) collective-permute-start(f32[64,512]{1,0:T(8,128)S(1)} %convert_add_fusion.3), channel_id=1, source_target_pairs={{0,4},{4,0},{8,12},{12,8},{1,5},{5,1},{9,13},{13,9},{2,6},{6,2},{1... | collective-permute-start | bytes 393224 | tf_op jit(solution)/shard_map/ppermute | solution.py:43
  (19 other events, 132.9 us)

commit v3 on v2

--- a/solution.py
+++ b/solution.py
@@ -107,6 +107,15 @@
 def unpack(packed, rows):
     packed = packed.astype(F32)
     return packed[:rows], packed[rows:, :EDGE] + packed[rows:, EDGE : 2 * EDGE]
+
+
+def sum_pairs(part, axis, first, last, kind):
+    bit = first
+    while bit < last:
+        part = part.astype(kind)
+        part = part.astype(F32) + swap(part, axis, bit).astype(F32)
+        bit *= 2
+    return part
 
 
 def tree(pieces):
@@ -180,7 +189,7 @@
     order = (place[:, None] == target[None, :]).astype(BF)
 
     def relative(position):
-        return ((me_l - position // cells) % n_l) * cells + position % cells
+        return (me_l ^ (position // cells)) * cells + position % cells
 
     moved = jnp.where(neighbours < part, relative(neighbours), neighbours)
     limit = part + 2 * EDGE
@@ -199,7 +208,7 @@
     raw, pre_enc, hidden_enc, latent = encode(slabs, placed, enc_out.T)
 
     table = jnp.concatenate(
-        [latent] + [shift(latent, "level", d) for d in range(1, n_l)], axis=1
+        [latent] + [swap(latent, "level", d) for d in range(1, n_l)], axis=1
     )
 
     columns = mm(order, raw).astype(BF)
@@ -240,22 +249,24 @@
     own = mm_cells(after(share, to_next, to_prev), counts[:part])
     back, own = lax.optimization_barrier((back, own))
     own = own + mm_cells(back, listed)
-    got = [
-        shift(own[:, d * cells : (d + 1) * cells].astype(BF), "level", -d) for d in range(1, n_l)
-    ]
-    d_neighbour = own[:, :cells]
-    for piece in got:
-        d_neighbour = d_neighbour + piece.astype(F32)
-
     core = lax.axis_index("horiz") % 2
     rows = hidden // n_h
     width = hidden // 2
-    term, half_dec = lax.optimization_barrier((term, half_dec, own))[:2]
     half_dec = (half_dec[0] + swap(half_dec[1], "horiz", 1)).astype(BF)
-    rider = jnp.pad(half_dec, ((0, 0), (0, feat - width)))
+    own, half_dec = lax.optimization_barrier((own, half_dec))
+    got = []
+    for d in range(1, n_l):
+        piece = own[:, d * cells : (d + 1) * cells].astype(BF)
+        got.append(swap(jnp.concatenate([piece] + [half_dec] * (d == 1), axis=1), "level", d))
+    half_dec = half_dec.astype(F32) + got[0][:, cells:].astype(F32)
+    d_neighbour = own[:, :cells]
+    for piece in got:
+        d_neighbour = d_neighbour + piece[:, :cells].astype(F32)
+
+    term = after(term, own)
     near_dec = pick(term, me_y, 0)
     far = [pick(term, (me_y + d) % n_y, 0).reshape(rows, feat) for d in range(1, n_y)]
-    far = to_rows_y([jnp.concatenate([piece.astype(BF), rider], axis=0) for piece in far])
+    far = to_rows_y([piece.astype(BF) for piece in far])
     context_b, cell_loss = lax.optimization_barrier(
         (context_b, distortion / feat + rate / LATENT, got[0])
     )[:2]
@@ -281,8 +292,8 @@
     sent = [pick(near, (me_y + d) % n_y, 0).astype(BF) for d in range(1, n_y)]
     sent = [jnp.concatenate([piece, rider], axis=0) for piece in sent]
     for piece in far:
-        near_dec = near_dec + piece[:rows].reshape(near_dec.shape).astype(F32)
-    half_dec = sum_y([half_dec] + [piece[rows:, :width] for piece in far]).astype(BF)
+        near_dec = near_dec + piece.reshape(near_dec.shape).astype(F32)
+    half_dec = half_dec.astype(BF)
     near, near_dec, half_dec, sent = lax.optimization_barrier(
         (pick(near, me_y, 0), near_dec, half_dec, sent)
     )
@@ -291,7 +302,7 @@
     got_dec = []
     for d in range(1, n_l):
         piece = pick(near_dec, me_l ^ d, 0).astype(BF).reshape(LATENT, -1)
-        got_dec.append(swap(jnp.concatenate([piece] + [half_dec] * (d == 1), axis=1), "level", d))
+        got_dec.append(swap(jnp.concatenate([piece] + [half_dec] * (d == 2), axis=1), "level", d))
     near, arrived, got_dec = lax.optimization_barrier((near, arrived, got_dec))
 
     for piece in arrived:
@@ -300,25 +311,24 @@
     riders = [rider] + [piece[rows:] for piece in arrived]
     riders = [unpack(piece, LATENT) for piece in riders]
     rider = pack(*(sum_y(list(pieces)) for pieces in zip(*riders)))
-    span = got_dec[1].shape[1]
-    half_dec = (half_dec.astype(F32) + got_dec[0][:, span:].astype(F32)).astype(BF)
+    span = got_dec[0].shape[1]
+    half_dec = half_dec.astype(F32) + got_dec[1][:, span:].astype(F32)
     few = rows // n_l
-    wide = jnp.pad(half_dec, ((0, 0), (0, feat - width)))
-    got_enc = [
-        swap(
-            jnp.concatenate(
-                [pick(near, me_l ^ d, 0).astype(BF), rider] + [wide] * (d == 2), axis=0
-            ),
-            "level",
-            d,
-        )
-        for d in range(1, n_l)
-    ]
-    size = few + rider.shape[0]
-    half_dec = half_dec.astype(F32) + got_enc[1][size:, :width].astype(F32)
-    got_enc = [piece[:size] for piece in got_enc]
-    riders = [unpack(piece, LATENT) for piece in [rider] + [p[few:] for p in got_enc]]
-    half_enc, cell_loss = (tree(list(pieces)) for pieces in zip(*riders))
+    got_enc = []
+    for d in range(1, n_l):
+        piece = pick(near, me_l ^ d, 0).astype(BF)
+        got_enc.append(swap(jnp.concatenate([piece] + [rider] * (d == 1), axis=0), "level", d))
+    theirs = got_enc[0][few:]
+    bit = 2
+    while bit < n_l:
+        pieces = [unpack(piece, LATENT) for piece in (rider, theirs)]
+        rider = pack(*(tree(list(parts)) for parts in zip(*pieces)))
+        theirs = swap(rider, "level", bit)
+        bit *= 2
+    riders = [rider, theirs]
+    half_enc = tree([piece[:LATENT, :width].astype(F32) for piece in riders])
+    grad_hyper = tree([piece[:LATENT, width:].astype(F32) for piece in riders])
+    cell_loss = tree([piece[LATENT:, : 2 * EDGE].astype(F32) for piece in riders])
     grad_dec_out = pick(near_dec, me_l, 0)
     for piece in got_dec:
         piece = piece[:, :span].reshape(grad_dec_out.shape)
@@ -328,10 +338,10 @@
         half_dec = half_dec.astype(BF)
         half_dec = half_dec.astype(F32) + swap(half_dec, "level", bit).astype(F32)
         bit *= 2
+    half_dec = sum_pairs(half_dec, "horiz", 2, n_h, BF)
     grad_dec_in = both_halves(after(half_dec, *got_enc))
-    grad_hyper = half_enc[:, width:]
     loss = (jnp.sum(cell_loss) / (part * n_h)).reshape(1)
-    grad_enc_out = both_halves(half_enc[:, :width]).T
+    grad_enc_out = both_halves(half_enc).T
     grad_enc_in = pick(near, me_l, 0)
     for piece in got_enc:
         grad_enc_in = grad_enc_in + piece[:few].astype(F32)

time: 126 us -> 124 us (0.984)
  waiting for transfers between devices: 31 us -> 21.3 us
  starting transfers between devices: 34 us -> 42.4 us
    ppermute x14 -> x22, starting transfers between devices: 13.9 us -> 33.3 us  [swap(): return lax.ppermute(block, axis, [(i, i ^ bit) for i in range(count)])]
    ppermute x15 -> x9, starting transfers between devices: 20.2 us -> 9.11 us  [shift(): lax.ppermute(block, axis, [(i, (i + step) % count) for i in range(count)])]
    ppermute x15 -> x9, waiting for transfers between devices: 11.9 us -> 1.53 us  [shift(): lax.ppermute(block, axis, [(i, (i + step) % count) for i in range(count)])]
    ppermute x14 -> x22, waiting for transfers between devices: 19.1 us -> 19.8 us  [swap(): return lax.ppermute(block, axis, [(i, i ^ bit) for i in range(count)])]
  transfers between devices with their start and end apart: 29 -> 31, of which waited for: 10 -> 9; matrix products, arithmetic and copies ran while one was open for 34% -> 38% of each run, Pallas kernels for 0% -> 0%
where the time goes in v3:
time: 124 us
  starting transfers between devices  42.4 us (34%)
  other arithmetic  24.5 us (20%)
  matrix products  24.5 us (20%)
  waiting for transfers between devices  21.3 us (17%)
  local copies, waits for them, and re-layouts  5.2 us (4%)
  between operations  3.36 us (3%)
  Pallas kernels  2.5 us (2%)
    ppermute x22, starting transfers between devices, swap(): return lax.ppermute(block, axis, [(i, i ^ bit) for i in range(count)])  33.3 us
    ppermute x22, waiting for transfers between devices, swap(): return lax.ppermute(block, axis, [(i, i ^ bit) for i in range(count)])  19.8 us
    convert_element_type x1, other arithmetic, local(): counts = counts.astype(BF)  15.1 us
    dot_general x10, matrix products, mm(): return jnp.dot(left, right, preferred_element_type=F32)  11.9 us
    dot_general x11, matrix products, mm_cells(): lax.dot_general(left, right, (((1,), (1,)), ((), ())), preferred_element_...  9.39 us
    ppermute x9, starting transfers between devices, shift(): lax.ppermute(block, axis, [(i, (i + step) % count) for i in range(count)])  9.11 us
    dot_general x3, matrix products, mm_rows(): lax.dot_general(left, right, (((0,), (0,)), ((), ())), preferred_element_...  3.17 us
    pallas_call x1, Pallas kernels, encode(): pl.pallas_call(functools.partial(encode_kernel, hidden // 4), out_shape=[...  2.5 us
  transfers between devices with their start and end apart: 31, of which 9 were waited for; matrix products, arithmetic and copies ran while one was open for 38% of the time, Pallas kernels for 0%

profile of v3, /device:TPU:1, one launch (start us, length us, event | category | flops | bytes accessed | tf_op | source)
XLA Modules:
  0.0 123.8 jit_solution(15466757967788485739)
XLA Ops:
  0.7 2.2 %constant_dynamic-slice_fusion.2 = (bf16[160,1024]{1,0:T(8,128)(2,1)S(1)}, bf16[160,1024]{1,0:T(8,128)(2,1)S(1)}, bf16[160,1024]{1,0:T(8,128)(2,1)}, bf16[160,1024]{1,0:T(8,128)(2,1)S(1)}) fusion(bf16[160,4096]{1,0:T(8,128)(2,1)} %bitcast.207, s32[]{:T(128)S(6)} %select_n.213, s32[]{:T(128)S(6)} %select_n.211, s32[]{:T(128)S(6)} %select_n.209, s32[]{:T(128)S(6)} %select_n.207), kind=kLoop, calls=%fused_computation.180 | loop fusion | bytes 2621456 | tf_op jit(solution)/shard_map/dynamic_slice | solution.py:183
  3.0 2.1 %collective-permute-start = (bf16[160,1024]{1,0:T(8,128)(2,1)}, bf16[160,1024]{1,0:T(8,128)(2,1)S(1)}, u32[]{:S(2)}, u32[]{:S(2)}) collective-permute-start(bf16[160,1024]{1,0:T(8,128)(2,1)} %get-tuple-element.105), channel_id=1, source_target_pairs={{0,1},{1,2},{2,3},{3,0},{4,5},{5,6},{6,7},{7,4},{8,9},{9,10},{10,1... | collective-permute-start | bytes 983048 | tf_op jit(solution)/shard_map/ppermute | solution.py:38
  5.1 2.3 %collective-permute-start.1 = (bf16[160,1024]{1,0:T(8,128)(2,1)S(1)}, bf16[160,1024]{1,0:T(8,128)(2,1)S(1)}, u32[]{:S(2)}, u32[]{:S(2)}) collective-permute-start(bf16[160,1024]{1,0:T(8,128)(2,1)S(1)} %get-tuple-element.104), channel_id=1, source_target_pairs={{0,2},{1,3},{2,0},{3,1},{4,6},{5,7},{6,4},{7,5},{8,10},{9,11},{10,... | collective-permute-start | bytes 983048 | tf_op jit(solution)/shard_map/ppermute | solution.py:38
  11.4 15.1 %add_convert_fusion = bf16[4352,1024]{1,0:T(8,128)(2,1)} fusion(s32[1024]{0:T(1024)S(1)} %bitcast.218, s32[1024]{0:T(1024)S(1)} %bitcast.219, s32[1024]{0:T(1024)S(1)} %bitcast.220, s32[1024]{0:T(1024)S(1)} %bitcast.221, s32[1024]{0:T(1024)S(1)} %bitcast.222, s32[1024]{0:T(1024)S(1)} %bitcast.217), kind=kLoop, calls=%fused_computation | loop fusion | flops 80216064 | bytes 8937472 | tf_op jit(solution)/shard_map/convert_element_type | solution.py:200
  27.8 2.7 %fusion.28.refs_4_ = bf16[1024,640]{1,0:T(8,128)(2,1)S(1)} fusion(bf16[1024,640]{1,0:T(8,128)(2,1)} %param.9, s32[640]{0:T(1024)S(1)} %fusion.91), kind=kOutput, calls=%fused_computation.49 | convolution fusion | flops 839925760 | bytes 2624000 | tf_op jit(solution)/shard_map/dot_general | solution.py:20
  30.5 2.5 %shard_map.135 = (bf16[640,1024]{1,0:T(8,128)(2,1)S(1)}, f32[1024,1024]{1,0:T(8,128)S(1)}, bf16[1024,1024]{1,0:T(8,128)(2,1)S(1)}, bf16[64,1024]{1,0:T(8,128)(2,1)S(1)}) custom-call(bf16[160,1024]{1,0:T(8,128)(2,1)S(1)} %get-tuple-element.49.refs_0_, bf16[160,1024]{1,0:T(8,128)(2,1)S(1)} %collective-permute-done.refs_1_, ...), custom_call_target="tpu_custom_call" | custom-call | flops 1476395008 | bytes 10223616 | tf_op jit(solution)/shard_map/pallas_call | solution.py:151
  33.0 6.5 %collective-permute-start.3 = (bf16[64,1024]{1,0:T(8,128)(2,1)S(1)}, bf16[64,1024]{1,0:T(8,128)(2,1)S(1)}, u32[]{:S(2)}, u32[]{:S(2)}) collective-permute-start(bf16[64,1024]{1,0:T(8,128)(2,1)S(1)} %get-tuple-element.54), channel_id=1, source_target_pairs={{0,1},{1,0},{2,3},{3,2},{4,5},{5,4},{6,7},{7,6},{8,9},{9,8},{10,11... | collective-permute-start | bytes 393224 | tf_op jit(solution)/shard_map/ppermute | solution.py:43
  39.7 1.9 %collective-permute-start.5 = (bf16[64,1024]{1,0:T(8,128)(2,1)S(1)}, bf16[64,1024]{1,0:T(8,128)(2,1)S(1)}, u32[]{:S(2)}, u32[]{:S(2)}) collective-permute-start(bf16[64,1024]{1,0:T(8,128)(2,1)S(1)} %get-tuple-element.54), channel_id=1, source_target_pairs={{0,3},{1,2},{2,1},{3,0},{4,7},{5,6},{6,5},{7,4},{8,11},{9,10},{10,... | collective-permute-start | bytes 393224 | tf_op jit(solution)/shard_map/ppermute | solution.py:43
  45.8 1.9 %fusion.108 = f32[1024,640]{1,0:T(8,128)S(1)} fusion(bf16[1024,1024]{0,1:T(8,128)(2,1)S(1)} %get-tuple-element.134, bf16[640,1024]{1,0:T(8,128)(2,1)S(1)} %get-tuple-element.137, f32[1024,640]{0,1:T(8,128)S(1)} %fusion.116), kind=kOutput, calls=%fused_computation.240 | convolution fusion | flops 1344798720 | bytes 8650752 | tf_op jit(solution)/shard_map/dot_general | solution.py:28
  49.0 3.1 %fusion.4 = bf16[1024,1024]{0,1:T(8,128)(2,1)S(1)} fusion(f32[1024,1024]{1,0:T(8,128)S(1)} %get-tuple-element.135, bf16[1024,640]{1,0:T(8,128)(2,1)S(1)} %copy-done, bf16[640,1024]{1,0:T(8,128)(2,1)S(1)} %get-tuple-element.137, f32[1024,640]{0,1:T(8,128)S(1)} %fusion.116), kind=kOutput, calls=%fused_computation.12 | convolution fusion | flops 1354235904 | bytes 11534336 | tf_op jit(solution)/shard_map/dot_general | solution.py:20
  61.8 1.7 %collective-permute-start.9 = (bf16[64,128]{1,0:T(8,128)(2,1)S(1)}, bf16[64,128]{1,0:T(8,128)(2,1)S(1)}, u32[]{:S(2)}, u32[]{:S(2)}) collective-permute-start(bf16[64,128]{1,0:T(8,128)(2,1)S(1)} %get-tuple-element.122), channel_id=1, source_target_pairs={{0,4},{4,8},{8,12},{12,0},{1,5},{5,9},{9,13},{13,1},{2,6},{6,10},{... | collective-permute-start | bytes 49160 | tf_op jit(solution)/shard_map/ppermute | solution.py:38
  63.5 2.7 %fusion = f32[64,4096]{1,0:T(8,128)S(1)} fusion(bf16[64,1024]{1,0:T(8,128)(2,1)S(1)} %bitcast.224, bf16[4352,1024]{1,0:T(8,128)(2,1)S(1)} %bitcast.202), kind=kOutput, calls=%fused_computation.7 | convolution fusion | flops 536870912 | bytes 9568256 | tf_op jit(solution)/shard_map/dot_general | solution.py:28
  69.1 2.2 %collective-permute-start.13 = (bf16[64,1024]{1,0:T(8,128)(2,1)S(1)}, bf16[64,1024]{1,0:T(8,128)(2,1)S(1)}, u32[]{:S(2)}, u32[]{:S(2)}) collective-permute-start(bf16[64,1024]{1,0:T(8,128)(2,1)S(1)} %get-tuple-element.117), channel_id=1, source_target_pairs={{0,2},{1,3},{2,0},{3,1},{4,6},{5,7},{6,4},{7,5},{8,10},{9,11},{10,... | collective-permute-start | bytes 393224 | tf_op jit(solution)/shard_map/ppermute | solution.py:43
  71.8 4.4 %collective-permute-done.12 = bf16[64,1536]{1,0:T(8,128)(2,1)S(1)} collective-permute-done((bf16[64,1536]{1,0:T(8,128)(2,1)S(1)}, bf16[64,1536]{1,0:T(8,128)(2,1)S(1)}, u32[]{:S(2)}, u32[]{:S(2)}) %collective-permute-start.12) | collective-permute-done | bytes 196640 | tf_op jit(solution)/shard_map/ppermute | solution.py:43
  77.0 3.6 %collective-permute-done.14 = bf16[64,1024]{1,0:T(8,128)(2,1)S(1)} collective-permute-done((bf16[64,1024]{1,0:T(8,128)(2,1)S(1)}, bf16[64,1024]{1,0:T(8,128)(2,1)S(1)}, u32[]{:S(2)}, u32[]{:S(2)}) %collective-permute-start.14) | collective-permute-done | bytes 131104 | tf_op jit(solution)/shard_map/ppermute | solution.py:43
  81.4 2.4 %collective-permute-start.19 = (f32[64,512]{1,0:T(8,128)S(1)}, f32[64,512]{1,0:T(8,128)S(1)}, u32[]{:S(2)}, u32[]{:S(2)}) collective-permute-start(f32[64,512]{1,0:T(8,128)S(1)} %fusion.30), channel_id=1, source_target_pairs={{0,4},{4,0},{8,12},{12,8},{1,5},{5,1},{9,13},{13,9},{2,6},{6,2},{1... | collective-permute-start | bytes 393224 | tf_op jit(solution)/shard_map/ppermute | solution.py:43
  89.5 3.5 %collective-permute-start.22 = (bf16[64,1152]{1,0:T(8,128)(2,1)S(1)}, bf16[64,1152]{1,0:T(8,128)(2,1)S(1)}, u32[]{:S(2)}, u32[]{:S(2)}) collective-permute-start(bf16[64,1152]{1,0:T(8,128)(2,1)S(1)} %pad_maximum_fusion.8), channel_id=1, source_target_pairs={{0,2},{1,3},{2,0},{3,1},{4,6},{5,7},{6,4},{7,5},{8,10},{9,11},{10,... | collective-permute-start | bytes 442376 | tf_op jit(solution)/shard_map/ppermute | solution.py:43
  94.3 3.2 %collective-permute-done.21 = bf16[64,640]{1,0:T(8,128)(2,1)S(1)} collective-permute-done((bf16[64,640]{1,0:T(8,128)(2,1)S(1)}, bf16[64,640]{1,0:T(8,128)(2,1)S(1)}, u32[]{:S(2)}, u32[]{:S(2)}) %collective-permute-start.21) | collective-permute-done | bytes 81952 | tf_op jit(solution)/shard_map/ppermute | solution.py:43
  97.5 3.5 %collective-permute-done.23 = bf16[64,640]{1,0:T(8,128)(2,1)S(1)} collective-permute-done((bf16[64,640]{1,0:T(8,128)(2,1)S(1)}, bf16[64,640]{1,0:T(8,128)(2,1)S(1)}, u32[]{:S(2)}, u32[]{:S(2)}) %collective-permute-start.23) | collective-permute-done | bytes 81952 | tf_op jit(solution)/shard_map/ppermute | solution.py:43
  101.3 2.7 %collective-permute-start.24 = (bf16[136,640]{1,0:T(8,128)(2,1)S(1)}, bf16[136,640]{1,0:T(8,128)(2,1)S(1)}, u32[]{:S(2)}, u32[]{:S(2)}) collective-permute-start(bf16[136,640]{1,0:T(8,128)(2,1)S(1)} %pad_maximum_fusion.5), channel_id=1, source_target_pairs={{0,1},{1,0},{2,3},{3,2},{4,5},{5,4},{6,7},{7,6},{8,9},{9,8},{10,11... | collective-permute-start | bytes 522248 | tf_op jit(solution)/shard_map/ppermute | solution.py:43
  104.4 1.9 %collective-permute-start.26 = (bf16[64,640]{1,0:T(8,128)(2,1)S(1)}, bf16[64,640]{1,0:T(8,128)(2,1)S(1)}, u32[]{:S(2)}, u32[]{:S(2)}) collective-permute-start(bf16[64,640]{1,0:T(8,128)(2,1)S(1)} %get-tuple-element.110), channel_id=1, source_target_pairs={{0,3},{1,2},{2,1},{3,0},{4,7},{5,6},{6,5},{7,4},{8,11},{9,10},{10,... | collective-permute-start | bytes 245768 | tf_op jit(solution)/shard_map/ppermute | solution.py:43
  109.3 2.9 %collective-permute-done.26 = bf16[64,640]{1,0:T(8,128)(2,1)S(1)} collective-permute-done((bf16[64,640]{1,0:T(8,128)(2,1)S(1)}, bf16[64,640]{1,0:T(8,128)(2,1)S(1)}, u32[]{:S(2)}, u32[]{:S(2)}) %collective-permute-start.26) | collective-permute-done | bytes 81952 | tf_op jit(solution)/shard_map/ppermute | solution.py:43
  112.2 3.4 %collective-permute-start.30 = (f32[64,512]{1,0:T(8,128)S(1)}, f32[64,512]{1,0:T(8,128)S(1)}, u32[]{:S(2)}, u32[]{:S(2)}) collective-permute-start(f32[64,512]{1,0:T(8,128)S(1)} %convert_add_fusion.3), channel_id=1, source_target_pairs={{0,4},{4,0},{8,12},{12,8},{1,5},{5,1},{9,13},{13,9},{2,6},{6,2},{1... | collective-permute-start | bytes 393224 | tf_op jit(solution)/shard_map/ppermute | solution.py:43
  117.4 1.9 %collective-permute-start.28 = (f32[64,512]{1,0:T(8,128)S(1)}, f32[64,512]{1,0:T(8,128)S(1)}, u32[]{:S(2)}, u32[]{:S(2)}) collective-permute-start(f32[64,512]{1,0:T(8,128)S(1)} %convert_add_fusion.4), channel_id=1, source_target_pairs={{0,4},{4,0},{8,12},{12,8},{1,5},{5,1},{9,13},{13,9},{2,6},{6,2},{1... | collective-permute-start | bytes 393224 | tf_op jit(solution)/shard_map/ppermute | solution.py:43
  (158 shorter events, 40.1 us)
Async XLA Ops:
  3.0 27.5 %collective-permute-start = (bf16[160,1024]{1,0:T(8,128)(2,1)}, bf16[160,1024]{1,0:T(8,128)(2,1)S(1)}, u32[]{:S(2)}, u32[]{:S(2)}) collective-permute-start(bf16[160,1024]{1,0:T(8,128)(2,1)} %get-tuple-element.105), channel_id=1, source_target_pairs={{0,1},{1,2},{2,3},{3,0},{4,5},{5,6},{6,7},{7,4},{8,9},{9,10},{10,1... | collective-permute-start | bytes 983048 | tf_op jit(solution)/shard_map/ppermute | solution.py:38
  5.1 25.3 %collective-permute-start.1 = (bf16[160,1024]{1,0:T(8,128)(2,1)S(1)}, bf16[160,1024]{1,0:T(8,128)(2,1)S(1)}, u32[]{:S(2)}, u32[]{:S(2)}) collective-permute-start(bf16[160,1024]{1,0:T(8,128)(2,1)S(1)} %get-tuple-element.104), channel_id=1, source_target_pairs={{0,2},{1,3},{2,0},{3,1},{4,6},{5,7},{6,4},{7,5},{8,10},{9,11},{10,... | collective-permute-start | bytes 983048 | tf_op jit(solution)/shard_map/ppermute | solution.py:38
  7.4 23.0 %collective-permute-start.2 = (bf16[160,1024]{1,0:T(8,128)(2,1)S(1)}, bf16[160,1024]{1,0:T(8,128)(2,1)S(1)}, u32[]{:S(2)}, u32[]{:S(2)}) collective-permute-start(bf16[160,1024]{1,0:T(8,128)(2,1)S(1)} %get-tuple-element.103), channel_id=1, source_target_pairs={{0,3},{1,0},{2,1},{3,2},{4,7},{5,4},{6,5},{7,6},{8,11},{9,8},{10,9... | collective-permute-start | bytes 983048 | tf_op jit(solution)/shard_map/ppermute | solution.py:38
  33.0 20.8 %collective-permute-start.3 = (bf16[64,1024]{1,0:T(8,128)(2,1)S(1)}, bf16[64,1024]{1,0:T(8,128)(2,1)S(1)}, u32[]{:S(2)}, u32[]{:S(2)}) collective-permute-start(bf16[64,1024]{1,0:T(8,128)(2,1)S(1)} %get-tuple-element.54), channel_id=1, source_target_pairs={{0,1},{1,0},{2,3},{3,2},{4,5},{5,4},{6,7},{7,6},{8,9},{9,8},{10,11... | collective-permute-start | bytes 393224 | tf_op jit(solution)/shard_map/ppermute | solution.py:43
  39.4 14.4 %collective-permute-start.4 = (bf16[64,1024]{1,0:T(8,128)(2,1)S(1)}, bf16[64,1024]{1,0:T(8,128)(2,1)S(1)}, u32[]{:S(2)}, u32[]{:S(2)}) collective-permute-start(bf16[64,1024]{1,0:T(8,128)(2,1)S(1)} %get-tuple-element.54), channel_id=1, source_target_pairs={{0,2},{1,3},{2,0},{3,1},{4,6},{5,7},{6,4},{7,5},{8,10},{9,11},{10,... | collective-permute-start | bytes 393224 | tf_op jit(solution)/shard_map/ppermute | solution.py:43
  39.7 14.1 %collective-permute-start.5 = (bf16[64,1024]{1,0:T(8,128)(2,1)S(1)}, bf16[64,1024]{1,0:T(8,128)(2,1)S(1)}, u32[]{:S(2)}, u32[]{:S(2)}) collective-permute-start(bf16[64,1024]{1,0:T(8,128)(2,1)S(1)} %get-tuple-element.54), channel_id=1, source_target_pairs={{0,3},{1,2},{2,1},{3,0},{4,7},{5,6},{6,5},{7,4},{8,11},{9,10},{10,... | collective-permute-start | bytes 393224 | tf_op jit(solution)/shard_map/ppermute | solution.py:43
  47.8 6.0 %collective-permute-start.6 = (bf16[2,4,64,640]{3,2,1,0:T(8,128)(2,1)S(1)}, bf16[2,4,64,640]{3,2,1,0:T(8,128)(2,1)S(1)}, u32[]{:S(2)}, u32[]{:S(2)}) collective-permute-start(bf16[2,4,64,640]{3,2,1,0:T(8,128)(2,1)S(1)} %fusion.38), channel_id=1, source_target_pairs={{0,4},{4,0},{8,12},{12,8},{1,5},{5,1},{9,13},{13,9},{2,6},{6,2},{1... | collective-permute-start | bytes 1966088 | tf_op jit(solution)/shard_map/ppermute | solution.py:43
  54.0 13.1 %collective-permute-start.11 = (f32[64,512]{1,0:T(8,128)S(1)}, f32[64,512]{1,0:T(8,128)S(1)}, u32[]{:S(2)}, u32[]{:S(2)}) collective-permute-start(f32[64,512]{1,0:T(8,128)S(1)} %fusion.33), channel_id=1, source_target_pairs={{0,4},{4,0},{8,12},{12,8},{1,5},{5,1},{9,13},{13,9},{2,6},{6,2},{1... | collective-permute-start | bytes 393224 | tf_op jit(solution)/shard_map/ppermute | solution.py:43
  61.7 4.5 %collective-permute-start.10 = (bf16[64,128]{1,0:T(8,128)(2,1)S(1)}, bf16[64,128]{1,0:T(8,128)(2,1)S(1)}, u32[]{:S(2)}, u32[]{:S(2)}) collective-permute-start(bf16[64,128]{1,0:T(8,128)(2,1)S(1)} %get-tuple-element.123), channel_id=1, source_target_pairs={{0,12},{4,0},{8,4},{12,8},{1,13},{5,1},{9,5},{13,9},{2,14},{6,2},{... | collective-permute-start | bytes 49160 | tf_op jit(solution)/shard_map/ppermute | solution.py:38
  67.3 8.9 %collective-permute-start.12 = (bf16[64,1536]{1,0:T(8,128)(2,1)S(1)}, bf16[64,1536]{1,0:T(8,128)(2,1)S(1)}, u32[]{:S(2)}, u32[]{:S(2)}) collective-permute-start(bf16[64,1536]{1,0:T(8,128)(2,1)S(1)} %pad_maximum_fusion.4), channel_id=1, source_target_pairs={{0,1},{1,0},{2,3},{3,2},{4,5},{5,4},{6,7},{7,6},{8,9},{9,8},{10,11... | collective-permute-start | bytes 589832 | tf_op jit(solution)/shard_map/ppermute | solution.py:43
  68.8 12.2 %collective-permute-start.17 = (bf16[256,640]{1,0:T(8,128)(2,1)S(1)}, bf16[256,640]{1,0:T(8,128)(2,1)S(1)}, u32[]{:S(2)}, u32[]{:S(2)}) collective-permute-start(bf16[256,640]{1,0:T(8,128)(2,1)S(1)} %bitcast.210), channel_id=1, source_target_pairs={{0,8},{4,12},{8,0},{12,4},{1,9},{5,13},{9,1},{13,5},{2,10},{6,14},... | collective-permute-start | bytes 983048 | tf_op jit(solution)/shard_map/ppermute | solution.py:38
  69.1 7.9 %collective-permute-start.13 = (bf16[64,1024]{1,0:T(8,128)(2,1)S(1)}, bf16[64,1024]{1,0:T(8,128)(2,1)S(1)}, u32[]{:S(2)}, u32[]{:S(2)}) collective-permute-start(bf16[64,1024]{1,0:T(8,128)(2,1)S(1)} %get-tuple-element.117), channel_id=1, source_target_pairs={{0,2},{1,3},{2,0},{3,1},{4,6},{5,7},{6,4},{7,5},{8,10},{9,11},{10,... | collective-permute-start | bytes 393224 | tf_op jit(solution)/shard_map/ppermute | solution.py:43
  71.2 9.3 %collective-permute-start.14 = (bf16[64,1024]{1,0:T(8,128)(2,1)S(1)}, bf16[64,1024]{1,0:T(8,128)(2,1)S(1)}, u32[]{:S(2)}, u32[]{:S(2)}) collective-permute-start(bf16[64,1024]{1,0:T(8,128)(2,1)S(1)} %get-tuple-element.116), channel_id=1, source_target_pairs={{0,3},{1,2},{2,1},{3,0},{4,7},{5,6},{6,5},{7,4},{8,11},{9,10},{10,... | collective-permute-start | bytes 393224 | tf_op jit(solution)/shard_map/ppermute | solution.py:43
  76.2 4.7 %collective-permute-start.16 = (f32[8,128]{1,0:T(8,128)S(1)}, f32[8,128]{1,0:T(8,128)S(1)}, u32[]{:S(2)}, u32[]{:S(2)}) collective-permute-start(f32[8,128]{1,0:T(8,128)S(1)} %bitcast.223), channel_id=1, source_target_pairs={{0,4},{4,0},{8,12},{12,8},{1,5},{5,1},{9,13},{13,9},{2,6},{6,2},{1... | collective-permute-start | bytes 12296 | tf_op jit(solution)/shard_map/ppermute | solution.py:43
  81.4 5.4 %collective-permute-start.19 = (f32[64,512]{1,0:T(8,128)S(1)}, f32[64,512]{1,0:T(8,128)S(1)}, u32[]{:S(2)}, u32[]{:S(2)}) collective-permute-start(f32[64,512]{1,0:T(8,128)S(1)} %fusion.30), channel_id=1, source_target_pairs={{0,4},{4,0},{8,12},{12,8},{1,5},{5,1},{9,13},{13,9},{2,6},{6,2},{1... | collective-permute-start | bytes 393224 | tf_op jit(solution)/shard_map/ppermute | solution.py:43
  89.1 12.0 %collective-permute-start.20 = (bf16[328,640]{1,0:T(8,128)(2,1)S(1)}, bf16[328,640]{1,0:T(8,128)(2,1)S(1)}, u32[]{:S(2)}, u32[]{:S(2)}) collective-permute-start(bf16[328,640]{1,0:T(8,128)(2,1)S(1)} %pad_maximum_fusion.1), channel_id=1, source_target_pairs={{0,8},{4,12},{8,0},{12,4},{1,9},{5,13},{9,1},{13,5},{2,10},{6,14},... | collective-permute-start | bytes 1259528 | tf_op jit(solution)/shard_map/ppermute | solution.py:38
  89.5 11.6 %collective-permute-start.22 = (bf16[64,1152]{1,0:T(8,128)(2,1)S(1)}, bf16[64,1152]{1,0:T(8,128)(2,1)S(1)}, u32[]{:S(2)}, u32[]{:S(2)}) collective-permute-start(bf16[64,1152]{1,0:T(8,128)(2,1)S(1)} %pad_maximum_fusion.8), channel_id=1, source_target_pairs={{0,2},{1,3},{2,0},{3,1},{4,6},{5,7},{6,4},{7,5},{8,10},{9,11},{10,... | collective-permute-start | bytes 442376 | tf_op jit(solution)/shard_map/ppermute | solution.py:43
  92.9 4.6 %collective-permute-start.21 = (bf16[64,640]{1,0:T(8,128)(2,1)S(1)}, bf16[64,640]{1,0:T(8,128)(2,1)S(1)}, u32[]{:S(2)}, u32[]{:S(2)}) collective-permute-start(bf16[64,640]{1,0:T(8,128)(2,1)S(1)} %get-tuple-element.114), channel_id=1, source_target_pairs={{0,1},{1,0},{2,3},{3,2},{4,5},{5,4},{6,7},{7,6},{8,9},{9,8},{10,11... | collective-permute-start | bytes 245768 | tf_op jit(solution)/shard_map/ppermute | solution.py:43
  92.9 8.1 %collective-permute-start.23 = (bf16[64,640]{1,0:T(8,128)(2,1)S(1)}, bf16[64,640]{1,0:T(8,128)(2,1)S(1)}, u32[]{:S(2)}, u32[]{:S(2)}) collective-permute-start(bf16[64,640]{1,0:T(8,128)(2,1)S(1)} %get-tuple-element.112), channel_id=1, source_target_pairs={{0,3},{1,2},{2,1},{3,0},{4,7},{5,6},{6,5},{7,4},{8,11},{9,10},{10,... | collective-permute-start | bytes 245768 | tf_op jit(solution)/shard_map/ppermute | solution.py:43
  101.3 6.3 %collective-permute-start.24 = (bf16[136,640]{1,0:T(8,128)(2,1)S(1)}, bf16[136,640]{1,0:T(8,128)(2,1)S(1)}, u32[]{:S(2)}, u32[]{:S(2)}) collective-permute-start(bf16[136,640]{1,0:T(8,128)(2,1)S(1)} %pad_maximum_fusion.5), channel_id=1, source_target_pairs={{0,1},{1,0},{2,3},{3,2},{4,5},{5,4},{6,7},{7,6},{8,9},{9,8},{10,11... | collective-permute-start | bytes 522248 | tf_op jit(solution)/shard_map/ppermute | solution.py:43
  104.2 5.2 %collective-permute-start.25 = (bf16[64,640]{1,0:T(8,128)(2,1)S(1)}, bf16[64,640]{1,0:T(8,128)(2,1)S(1)}, u32[]{:S(2)}, u32[]{:S(2)}) collective-permute-start(bf16[64,640]{1,0:T(8,128)(2,1)S(1)} %get-tuple-element.111), channel_id=1, source_target_pairs={{0,2},{1,3},{2,0},{3,1},{4,6},{5,7},{6,4},{7,5},{8,10},{9,11},{10,... | collective-permute-start | bytes 245768 | tf_op jit(solution)/shard_map/ppermute | solution.py:43
  104.4 7.8 %collective-permute-start.26 = (bf16[64,640]{1,0:T(8,128)(2,1)S(1)}, bf16[64,640]{1,0:T(8,128)(2,1)S(1)}, u32[]{:S(2)}, u32[]{:S(2)}) collective-permute-start(bf16[64,640]{1,0:T(8,128)(2,1)S(1)} %get-tuple-element.110), channel_id=1, source_target_pairs={{0,3},{1,2},{2,1},{3,0},{4,7},{5,6},{6,5},{7,4},{8,11},{9,10},{10,... | collective-permute-start | bytes 245768 | tf_op jit(solution)/shard_map/ppermute | solution.py:43
  107.7 9.7 %collective-permute-start.27 = (bf16[72,640]{1,0:T(8,128)(2,1)S(1)}, bf16[72,640]{1,0:T(8,128)(2,1)S(1)}, u32[]{:S(2)}, u32[]{:S(2)}) collective-permute-start(bf16[72,640]{1,0:T(8,128)(2,1)S(1)} %fusion.56), channel_id=1, source_target_pairs={{0,2},{1,3},{2,0},{3,1},{4,6},{5,7},{6,4},{7,5},{8,10},{9,11},{10,... | collective-permute-start | bytes 276488 | tf_op jit(solution)/shard_map/ppermute | solution.py:43
  112.2 9.0 %collective-permute-start.30 = (f32[64,512]{1,0:T(8,128)S(1)}, f32[64,512]{1,0:T(8,128)S(1)}, u32[]{:S(2)}, u32[]{:S(2)}) collective-permute-start(f32[64,512]{1,0:T(8,128)S(1)} %convert_add_fusion.3), channel_id=1, source_target_pairs={{0,4},{4,0},{8,12},{12,8},{1,5},{5,1},{9,13},{13,9},{2,6},{6,2},{1... | collective-permute-start | bytes 393224 | tf_op jit(solution)/shard_map/ppermute | solution.py:43
  (19 other events, 151.9 us)

commit v4 on v3

--- a/solution.py
+++ b/solution.py
@@ -267,23 +267,26 @@
     near_dec = pick(term, me_y, 0)
     far = [pick(term, (me_y + d) % n_y, 0).reshape(rows, feat) for d in range(1, n_y)]
     far = to_rows_y([piece.astype(BF) for piece in far])
-    context_b, cell_loss = lax.optimization_barrier(
-        (context_b, distortion / feat + rate / LATENT, got[0])
-    )[:2]
+    context_b, cell_loss, pre_enc = lax.optimization_barrier(
+        (context_b, distortion / feat + rate / LATENT, pre_enc, got[0])
+    )[:3]
+    slope = silu_slope(pre_enc)
     hyper = mm_cells(context_b, d_params)
     hyper = hyper + swap(hyper, "horiz", 1)
     cell_loss = cell_loss.reshape(-1, EDGE)
     cell_loss = cell_loss + swap(cell_loss, "horiz", 1)
     d_total = (d_latent + direct + d_neighbour).astype(BF)
-    d_total, hyper, cell_loss, *far = lax.optimization_barrier((d_total, hyper, cell_loss, *far))
+    d_total, slope, hyper, cell_loss, *far = lax.optimization_barrier(
+        (d_total, slope, hyper, cell_loss, *far)
+    )
 
     half_enc = halves(hidden_enc, lambda block: mm_cells(d_total, block))
     half_enc = half_enc[0] + swap(half_enc[1], "horiz", 1)
 
     def enc_rows(side):
         weight = pick(enc_out.reshape(n_y, 2, rows, LATENT), side, 1).reshape(n_y * rows, LATENT)
-        preact = pick(pre_enc.reshape(n_y, 2, rows, cells), side, 1).reshape(n_y * rows, cells)
-        d_pre = lax.optimization_barrier((mm(weight, d_total) * silu_slope(preact)).astype(BF))
+        factor = pick(slope.reshape(n_y, 2, rows, cells), side, 1).reshape(n_y * rows, cells)
+        d_pre = lax.optimization_barrier((mm(weight, d_total) * factor).astype(BF))
         return mm_cells(d_pre, columns)
 
     other = swap(enc_rows(1 - core).astype(BF), "horiz", 1)

time: 124 us -> 123 us (level)
  other arithmetic: 24.5 us -> 25.8 us
    dot_general x10, matrix products: 11.9 us -> 10.5 us  [mm(): return jnp.dot(left, right, preferred_element_type=F32)]
    mul x0 -> x1, other arithmetic: none -> 1.38 us  [silu_slope(): return squash * (1.0 + preact * (1.0 - squash))]
  transfers between devices with their start and end apart: 31 -> 31, of which waited for: 9 -> 9; matrix products, arithmetic and copies ran while one was open for 38% -> 39% of each run, Pallas kernels for 0% -> 0%
where the time goes in v4:
time: 123 us
  starting transfers between devices  42.1 us (34%)
  other arithmetic  25.8 us (21%)
  matrix products  23.3 us (19%)
  waiting for transfers between devices  20.7 us (17%)
  local copies, waits for them, and re-layouts  4.88 us (4%)
  between operations  3.35 us (3%)
  Pallas kernels  2.48 us (2%)
    ppermute x22, starting transfers between devices, swap(): return lax.ppermute(block, axis, [(i, i ^ bit) for i in range(count)])  33 us
    ppermute x22, waiting for transfers between devices, swap(): return lax.ppermute(block, axis, [(i, i ^ bit) for i in range(count)])  19.1 us
    convert_element_type x1, other arithmetic, local(): counts = counts.astype(BF)  15.1 us
    dot_general x10, matrix products, mm(): return jnp.dot(left, right, preferred_element_type=F32)  10.5 us
    dot_general x11, matrix products, mm_cells(): lax.dot_general(left, right, (((1,), (1,)), ((), ())), preferred_element_...  9.63 us
    ppermute x9, starting transfers between devices, shift(): lax.ppermute(block, axis, [(i, (i + step) % count) for i in range(count)])  9.13 us
    dot_general x3, matrix products, mm_rows(): lax.dot_general(left, right, (((0,), (0,)), ((), ())), preferred_element_...  3.17 us
    pallas_call x1, Pallas kernels, encode(): pl.pallas_call(functools.partial(encode_kernel, hidden // 4), out_shape=[...  2.48 us
  transfers between devices with their start and end apart: 31, of which 9 were waited for; matrix products, arithmetic and copies ran while one was open for 39% of the time, Pallas kernels for 0%

profile of v4, /device:TPU:1, one launch (start us, length us, event | category | flops | bytes accessed | tf_op | source)
XLA Modules:
  0.0 122.7 jit_solution(2785326222373864756)
XLA Ops:
  0.7 2.2 %constant_dynamic-slice_fusion.2 = (bf16[160,1024]{1,0:T(8,128)(2,1)S(1)}, bf16[160,1024]{1,0:T(8,128)(2,1)S(1)}, bf16[160,1024]{1,0:T(8,128)(2,1)}, bf16[160,1024]{1,0:T(8,128)(2,1)S(1)}) fusion(bf16[160,4096]{1,0:T(8,128)(2,1)} %bitcast.177, s32[]{:T(128)S(6)} %select_n.213, s32[]{:T(128)S(6)} %select_n.211, s32[]{:T(128)S(6)} %select_n.209, s32[]{:T(128)S(6)} %select_n.207), kind=kLoop, calls=%fused_computation.167 | loop fusion | bytes 2621456 | tf_op jit(solution)/shard_map/dynamic_slice | solution.py:183
  3.0 2.1 %collective-permute-start = (bf16[160,1024]{1,0:T(8,128)(2,1)}, bf16[160,1024]{1,0:T(8,128)(2,1)S(1)}, u32[]{:S(2)}, u32[]{:S(2)}) collective-permute-start(bf16[160,1024]{1,0:T(8,128)(2,1)} %get-tuple-element.109), channel_id=1, source_target_pairs={{0,1},{1,2},{2,3},{3,0},{4,5},{5,6},{6,7},{7,4},{8,9},{9,10},{10,1... | collective-permute-start | bytes 983048 | tf_op jit(solution)/shard_map/ppermute | solution.py:38
  5.1 2.3 %collective-permute-start.1 = (bf16[160,1024]{1,0:T(8,128)(2,1)S(1)}, bf16[160,1024]{1,0:T(8,128)(2,1)S(1)}, u32[]{:S(2)}, u32[]{:S(2)}) collective-permute-start(bf16[160,1024]{1,0:T(8,128)(2,1)S(1)} %get-tuple-element.108), channel_id=1, source_target_pairs={{0,2},{1,3},{2,0},{3,1},{4,6},{5,7},{6,4},{7,5},{8,10},{9,11},{10,... | collective-permute-start | bytes 983048 | tf_op jit(solution)/shard_map/ppermute | solution.py:38
  11.4 15.1 %add_convert_fusion = bf16[4352,1024]{1,0:T(8,128)(2,1)} fusion(s32[1024]{0:T(1024)S(1)} %bitcast.188, s32[1024]{0:T(1024)S(1)} %bitcast.189, s32[1024]{0:T(1024)S(1)} %bitcast.190, s32[1024]{0:T(1024)S(1)} %bitcast.191, s32[1024]{0:T(1024)S(1)} %bitcast.192, s32[1024]{0:T(1024)S(1)} %bitcast.187), kind=kLoop, calls=%fused_computation | loop fusion | flops 80216064 | bytes 8937472 | tf_op jit(solution)/shard_map/convert_element_type | solution.py:200
  27.8 2.7 %fusion.16.refs_4_ = bf16[1024,640]{1,0:T(8,128)(2,1)S(1)} fusion(bf16[1024,640]{1,0:T(8,128)(2,1)} %param.9, s32[640]{0:T(1024)S(1)} %fusion.79), kind=kOutput, calls=%fused_computation.36 | convolution fusion | flops 839925760 | bytes 2624000 | tf_op jit(solution)/shard_map/dot_general | solution.py:20
  30.5 2.5 %shard_map.135 = (bf16[640,1024]{1,0:T(8,128)(2,1)S(1)}, f32[1024,1024]{1,0:T(8,128)S(1)}, bf16[1024,1024]{1,0:T(8,128)(2,1)S(1)}, bf16[64,1024]{1,0:T(8,128)(2,1)S(1)}) custom-call(bf16[160,1024]{1,0:T(8,128)(2,1)S(1)} %get-tuple-element.51.refs_0_, bf16[160,1024]{1,0:T(8,128)(2,1)S(1)} %collective-permute-done.refs_1_, ...), custom_call_target="tpu_custom_call" | custom-call | flops 1476395008 | bytes 10223616 | tf_op jit(solution)/shard_map/pallas_call | solution.py:151
  32.9 6.5 %collective-permute-start.3 = (bf16[64,1024]{1,0:T(8,128)(2,1)S(1)}, bf16[64,1024]{1,0:T(8,128)(2,1)S(1)}, u32[]{:S(2)}, u32[]{:S(2)}) collective-permute-start(bf16[64,1024]{1,0:T(8,128)(2,1)S(1)} %get-tuple-element.56), channel_id=1, source_target_pairs={{0,1},{1,0},{2,3},{3,2},{4,5},{5,4},{6,7},{7,6},{8,9},{9,8},{10,11... | collective-permute-start | bytes 393224 | tf_op jit(solution)/shard_map/ppermute | solution.py:43
  39.7 1.9 %collective-permute-start.5 = (bf16[64,1024]{1,0:T(8,128)(2,1)S(1)}, bf16[64,1024]{1,0:T(8,128)(2,1)S(1)}, u32[]{:S(2)}, u32[]{:S(2)}) collective-permute-start(bf16[64,1024]{1,0:T(8,128)(2,1)S(1)} %get-tuple-element.56), channel_id=1, source_target_pairs={{0,3},{1,2},{2,1},{3,0},{4,7},{5,6},{6,5},{7,4},{8,11},{9,10},{10,... | collective-permute-start | bytes 393224 | tf_op jit(solution)/shard_map/ppermute | solution.py:43
  45.8 1.9 %fusion.96 = f32[1024,640]{1,0:T(8,128)S(1)} fusion(bf16[1024,1024]{1,0:T(8,128)(2,1)S(1)} %get-tuple-element.138, bf16[640,1024]{1,0:T(8,128)(2,1)S(1)} %get-tuple-element.141, f32[1024,640]{0,1:T(8,128)S(1)} %fusion.104), kind=kOutput, calls=%fused_computation.227 | convolution fusion | flops 1344798720 | bytes 8650752 | tf_op jit(solution)/shard_map/dot_general | solution.py:28
  48.9 2.9 %fusion.4 = bf16[1024,1024]{1,0:T(8,128)(2,1)S(1)} fusion(f32[1024,1024]{0,1:T(8,128)S(1)} %get-tuple-element.139, bf16[1024,640]{1,0:T(8,128)(2,1)S(1)} %copy-done, bf16[640,1024]{1,0:T(8,128)(2,1)S(1)} %get-tuple-element.141, f32[1024,640]{0,1:T(8,128)S(1)} %fusion.104), kind=kOutput, calls=%fused_computation.12 | convolution fusion | flops 1354235904 | bytes 11534336 | tf_op jit(solution)/shard_map/dot_general | solution.py:20
  60.7 1.7 %collective-permute-start.9 = (bf16[64,128]{1,0:T(8,128)(2,1)S(1)}, bf16[64,128]{1,0:T(8,128)(2,1)S(1)}, u32[]{:S(2)}, u32[]{:S(2)}) collective-permute-start(bf16[64,128]{1,0:T(8,128)(2,1)S(1)} %get-tuple-element.126), channel_id=1, source_target_pairs={{0,4},{4,8},{8,12},{12,0},{1,5},{5,9},{9,13},{13,1},{2,6},{6,10},{... | collective-permute-start | bytes 49160 | tf_op jit(solution)/shard_map/ppermute | solution.py:38
  62.5 2.7 %fusion = f32[64,4096]{1,0:T(8,128)S(1)} fusion(bf16[64,1024]{1,0:T(8,128)(2,1)S(1)} %bitcast.194, bf16[4352,1024]{1,0:T(8,128)(2,1)S(1)} %bitcast.172), kind=kOutput, calls=%fused_computation.7 | convolution fusion | flops 536870912 | bytes 9568256 | tf_op jit(solution)/shard_map/dot_general | solution.py:28
  68.0 2.2 %collective-permute-start.13 = (bf16[64,1024]{1,0:T(8,128)(2,1)S(1)}, bf16[64,1024]{1,0:T(8,128)(2,1)S(1)}, u32[]{:S(2)}, u32[]{:S(2)}) collective-permute-start(bf16[64,1024]{1,0:T(8,128)(2,1)S(1)} %get-tuple-element.121), channel_id=1, source_target_pairs={{0,2},{1,3},{2,0},{3,1},{4,6},{5,7},{6,4},{7,5},{8,10},{9,11},{10,... | collective-permute-start | bytes 393224 | tf_op jit(solution)/shard_map/ppermute | solution.py:43
  70.7 4.4 %collective-permute-done.12 = bf16[64,1536]{1,0:T(8,128)(2,1)S(1)} collective-permute-done((bf16[64,1536]{1,0:T(8,128)(2,1)S(1)}, bf16[64,1536]{1,0:T(8,128)(2,1)S(1)}, u32[]{:S(2)}, u32[]{:S(2)}) %collective-permute-start.12) | collective-permute-done | bytes 196640 | tf_op jit(solution)/shard_map/ppermute | solution.py:43
  77.3 2.2 %collective-permute-done.14 = bf16[64,1024]{1,0:T(8,128)(2,1)S(1)} collective-permute-done((bf16[64,1024]{1,0:T(8,128)(2,1)S(1)}, bf16[64,1024]{1,0:T(8,128)(2,1)S(1)}, u32[]{:S(2)}, u32[]{:S(2)}) %collective-permute-start.14) | collective-permute-done | bytes 131104 | tf_op jit(solution)/shard_map/ppermute | solution.py:43
  80.3 2.4 %collective-permute-start.19 = (f32[64,512]{1,0:T(8,128)S(1)}, f32[64,512]{1,0:T(8,128)S(1)}, u32[]{:S(2)}, u32[]{:S(2)}) collective-permute-start(f32[64,512]{1,0:T(8,128)S(1)} %fusion.18), channel_id=1, source_target_pairs={{0,4},{4,0},{8,12},{12,8},{1,5},{5,1},{9,13},{13,9},{2,6},{6,2},{1... | collective-permute-start | bytes 393224 | tf_op jit(solution)/shard_map/ppermute | solution.py:43
  88.4 3.5 %collective-permute-start.22 = (bf16[64,1152]{1,0:T(8,128)(2,1)S(1)}, bf16[64,1152]{1,0:T(8,128)(2,1)S(1)}, u32[]{:S(2)}, u32[]{:S(2)}) collective-permute-start(bf16[64,1152]{1,0:T(8,128)(2,1)S(1)} %pad_maximum_fusion.8), channel_id=1, source_target_pairs={{0,2},{1,3},{2,0},{3,1},{4,6},{5,7},{6,4},{7,5},{8,10},{9,11},{10,... | collective-permute-start | bytes 442376 | tf_op jit(solution)/shard_map/ppermute | solution.py:43
  93.2 3.2 %collective-permute-done.21 = bf16[64,640]{1,0:T(8,128)(2,1)S(1)} collective-permute-done((bf16[64,640]{1,0:T(8,128)(2,1)S(1)}, bf16[64,640]{1,0:T(8,128)(2,1)S(1)}, u32[]{:S(2)}, u32[]{:S(2)}) %collective-permute-start.21) | collective-permute-done | bytes 81952 | tf_op jit(solution)/shard_map/ppermute | solution.py:43
  96.5 3.8 %collective-permute-done.23 = bf16[64,640]{1,0:T(8,128)(2,1)S(1)} collective-permute-done((bf16[64,640]{1,0:T(8,128)(2,1)S(1)}, bf16[64,640]{1,0:T(8,128)(2,1)S(1)}, u32[]{:S(2)}, u32[]{:S(2)}) %collective-permute-start.23) | collective-permute-done | bytes 81952 | tf_op jit(solution)/shard_map/ppermute | solution.py:43
  100.5 2.5 %collective-permute-start.24 = (bf16[136,640]{1,0:T(8,128)(2,1)S(1)}, bf16[136,640]{1,0:T(8,128)(2,1)S(1)}, u32[]{:S(2)}, u32[]{:S(2)}) collective-permute-start(bf16[136,640]{1,0:T(8,128)(2,1)S(1)} %pad_maximum_fusion.5), channel_id=1, source_target_pairs={{0,1},{1,0},{2,3},{3,2},{4,5},{5,4},{6,7},{7,6},{8,9},{9,8},{10,11... | collective-permute-start | bytes 522248 | tf_op jit(solution)/shard_map/ppermute | solution.py:43
  103.3 1.9 %collective-permute-start.26 = (bf16[64,640]{1,0:T(8,128)(2,1)S(1)}, bf16[64,640]{1,0:T(8,128)(2,1)S(1)}, u32[]{:S(2)}, u32[]{:S(2)}) collective-permute-start(bf16[64,640]{1,0:T(8,128)(2,1)S(1)} %get-tuple-element.114), channel_id=1, source_target_pairs={{0,3},{1,2},{2,1},{3,0},{4,7},{5,6},{6,5},{7,4},{8,11},{9,10},{10,... | collective-permute-start | bytes 245768 | tf_op jit(solution)/shard_map/ppermute | solution.py:43
  108.3 2.9 %collective-permute-done.26 = bf16[64,640]{1,0:T(8,128)(2,1)S(1)} collective-permute-done((bf16[64,640]{1,0:T(8,128)(2,1)S(1)}, bf16[64,640]{1,0:T(8,128)(2,1)S(1)}, u32[]{:S(2)}, u32[]{:S(2)}) %collective-permute-start.26) | collective-permute-done | bytes 81952 | tf_op jit(solution)/shard_map/ppermute | solution.py:43
  111.1 3.4 %collective-permute-start.30 = (f32[64,512]{1,0:T(8,128)S(1)}, f32[64,512]{1,0:T(8,128)S(1)}, u32[]{:S(2)}, u32[]{:S(2)}) collective-permute-start(f32[64,512]{1,0:T(8,128)S(1)} %convert_add_fusion.3), channel_id=1, source_target_pairs={{0,4},{4,0},{8,12},{12,8},{1,5},{5,1},{9,13},{13,9},{2,6},{6,2},{1... | collective-permute-start | bytes 393224 | tf_op jit(solution)/shard_map/ppermute | solution.py:43
  116.3 1.9 %collective-permute-start.28 = (f32[64,512]{1,0:T(8,128)S(1)}, f32[64,512]{1,0:T(8,128)S(1)}, u32[]{:S(2)}, u32[]{:S(2)}) collective-permute-start(f32[64,512]{1,0:T(8,128)S(1)} %convert_add_fusion.4), channel_id=1, source_target_pairs={{0,4},{4,0},{8,12},{12,8},{1,5},{5,1},{9,13},{13,9},{2,6},{6,2},{1... | collective-permute-start | bytes 393224 | tf_op jit(solution)/shard_map/ppermute | solution.py:43
  (159 shorter events, 40.7 us)
Async XLA Ops:
  3.0 27.5 %collective-permute-start = (bf16[160,1024]{1,0:T(8,128)(2,1)}, bf16[160,1024]{1,0:T(8,128)(2,1)S(1)}, u32[]{:S(2)}, u32[]{:S(2)}) collective-permute-start(bf16[160,1024]{1,0:T(8,128)(2,1)} %get-tuple-element.109), channel_id=1, source_target_pairs={{0,1},{1,2},{2,3},{3,0},{4,5},{5,6},{6,7},{7,4},{8,9},{9,10},{10,1... | collective-permute-start | bytes 983048 | tf_op jit(solution)/shard_map/ppermute | solution.py:38
  5.1 25.3 %collective-permute-start.1 = (bf16[160,1024]{1,0:T(8,128)(2,1)S(1)}, bf16[160,1024]{1,0:T(8,128)(2,1)S(1)}, u32[]{:S(2)}, u32[]{:S(2)}) collective-permute-start(bf16[160,1024]{1,0:T(8,128)(2,1)S(1)} %get-tuple-element.108), channel_id=1, source_target_pairs={{0,2},{1,3},{2,0},{3,1},{4,6},{5,7},{6,4},{7,5},{8,10},{9,11},{10,... | collective-permute-start | bytes 983048 | tf_op jit(solution)/shard_map/ppermute | solution.py:38
  7.4 23.0 %collective-permute-start.2 = (bf16[160,1024]{1,0:T(8,128)(2,1)S(1)}, bf16[160,1024]{1,0:T(8,128)(2,1)S(1)}, u32[]{:S(2)}, u32[]{:S(2)}) collective-permute-start(bf16[160,1024]{1,0:T(8,128)(2,1)S(1)} %get-tuple-element.107), channel_id=1, source_target_pairs={{0,3},{1,0},{2,1},{3,2},{4,7},{5,4},{6,5},{7,6},{8,11},{9,8},{10,9... | collective-permute-start | bytes 983048 | tf_op jit(solution)/shard_map/ppermute | solution.py:38
  32.9 20.2 %collective-permute-start.3 = (bf16[64,1024]{1,0:T(8,128)(2,1)S(1)}, bf16[64,1024]{1,0:T(8,128)(2,1)S(1)}, u32[]{:S(2)}, u32[]{:S(2)}) collective-permute-start(bf16[64,1024]{1,0:T(8,128)(2,1)S(1)} %get-tuple-element.56), channel_id=1, source_target_pairs={{0,1},{1,0},{2,3},{3,2},{4,5},{5,4},{6,7},{7,6},{8,9},{9,8},{10,11... | collective-permute-start | bytes 393224 | tf_op jit(solution)/shard_map/ppermute | solution.py:43
  39.4 13.7 %collective-permute-start.4 = (bf16[64,1024]{1,0:T(8,128)(2,1)S(1)}, bf16[64,1024]{1,0:T(8,128)(2,1)S(1)}, u32[]{:S(2)}, u32[]{:S(2)}) collective-permute-start(bf16[64,1024]{1,0:T(8,128)(2,1)S(1)} %get-tuple-element.56), channel_id=1, source_target_pairs={{0,2},{1,3},{2,0},{3,1},{4,6},{5,7},{6,4},{7,5},{8,10},{9,11},{10,... | collective-permute-start | bytes 393224 | tf_op jit(solution)/shard_map/ppermute | solution.py:43
  39.7 13.5 %collective-permute-start.5 = (bf16[64,1024]{1,0:T(8,128)(2,1)S(1)}, bf16[64,1024]{1,0:T(8,128)(2,1)S(1)}, u32[]{:S(2)}, u32[]{:S(2)}) collective-permute-start(bf16[64,1024]{1,0:T(8,128)(2,1)S(1)} %get-tuple-element.56), channel_id=1, source_target_pairs={{0,3},{1,2},{2,1},{3,0},{4,7},{5,6},{6,5},{7,4},{8,11},{9,10},{10,... | collective-permute-start | bytes 393224 | tf_op jit(solution)/shard_map/ppermute | solution.py:43
  47.7 5.5 %collective-permute-start.6 = (bf16[2,4,64,640]{3,2,1,0:T(8,128)(2,1)S(1)}, bf16[2,4,64,640]{3,2,1,0:T(8,128)(2,1)S(1)}, u32[]{:S(2)}, u32[]{:S(2)}) collective-permute-start(bf16[2,4,64,640]{3,2,1,0:T(8,128)(2,1)S(1)} %fusion.26), channel_id=1, source_target_pairs={{0,4},{4,0},{8,12},{12,8},{1,5},{5,1},{9,13},{13,9},{2,6},{6,2},{1... | collective-permute-start | bytes 1966088 | tf_op jit(solution)/shard_map/ppermute | solution.py:43
  53.3 12.7 %collective-permute-start.11 = (f32[64,512]{1,0:T(8,128)S(1)}, f32[64,512]{1,0:T(8,128)S(1)}, u32[]{:S(2)}, u32[]{:S(2)}) collective-permute-start(f32[64,512]{1,0:T(8,128)S(1)} %fusion.21), channel_id=1, source_target_pairs={{0,4},{4,0},{8,12},{12,8},{1,5},{5,1},{9,13},{13,9},{2,6},{6,2},{1... | collective-permute-start | bytes 393224 | tf_op jit(solution)/shard_map/ppermute | solution.py:43
  60.7 4.5 %collective-permute-start.10 = (bf16[64,128]{1,0:T(8,128)(2,1)S(1)}, bf16[64,128]{1,0:T(8,128)(2,1)S(1)}, u32[]{:S(2)}, u32[]{:S(2)}) collective-permute-start(bf16[64,128]{1,0:T(8,128)(2,1)S(1)} %get-tuple-element.127), channel_id=1, source_target_pairs={{0,12},{4,0},{8,4},{12,8},{1,13},{5,1},{9,5},{13,9},{2,14},{6,2},{... | collective-permute-start | bytes 49160 | tf_op jit(solution)/shard_map/ppermute | solution.py:38
  66.2 8.9 %collective-permute-start.12 = (bf16[64,1536]{1,0:T(8,128)(2,1)S(1)}, bf16[64,1536]{1,0:T(8,128)(2,1)S(1)}, u32[]{:S(2)}, u32[]{:S(2)}) collective-permute-start(bf16[64,1536]{1,0:T(8,128)(2,1)S(1)} %pad_maximum_fusion.4), channel_id=1, source_target_pairs={{0,1},{1,0},{2,3},{3,2},{4,5},{5,4},{6,7},{7,6},{8,9},{9,8},{10,11... | collective-permute-start | bytes 589832 | tf_op jit(solution)/shard_map/ppermute | solution.py:43
  67.7 12.2 %collective-permute-start.17 = (bf16[256,640]{1,0:T(8,128)(2,1)S(1)}, bf16[256,640]{1,0:T(8,128)(2,1)S(1)}, u32[]{:S(2)}, u32[]{:S(2)}) collective-permute-start(bf16[256,640]{1,0:T(8,128)(2,1)S(1)} %bitcast.180), channel_id=1, source_target_pairs={{0,8},{4,12},{8,0},{12,4},{1,9},{5,13},{9,1},{13,5},{2,10},{6,14},... | collective-permute-start | bytes 983048 | tf_op jit(solution)/shard_map/ppermute | solution.py:38
  68.0 9.3 %collective-permute-start.13 = (bf16[64,1024]{1,0:T(8,128)(2,1)S(1)}, bf16[64,1024]{1,0:T(8,128)(2,1)S(1)}, u32[]{:S(2)}, u32[]{:S(2)}) collective-permute-start(bf16[64,1024]{1,0:T(8,128)(2,1)S(1)} %get-tuple-element.121), channel_id=1, source_target_pairs={{0,2},{1,3},{2,0},{3,1},{4,6},{5,7},{6,4},{7,5},{8,10},{9,11},{10,... | collective-permute-start | bytes 393224 | tf_op jit(solution)/shard_map/ppermute | solution.py:43
  70.2 9.3 %collective-permute-start.14 = (bf16[64,1024]{1,0:T(8,128)(2,1)S(1)}, bf16[64,1024]{1,0:T(8,128)(2,1)S(1)}, u32[]{:S(2)}, u32[]{:S(2)}) collective-permute-start(bf16[64,1024]{1,0:T(8,128)(2,1)S(1)} %get-tuple-element.120), channel_id=1, source_target_pairs={{0,3},{1,2},{2,1},{3,0},{4,7},{5,6},{6,5},{7,4},{8,11},{9,10},{10,... | collective-permute-start | bytes 393224 | tf_op jit(solution)/shard_map/ppermute | solution.py:43
  75.1 4.7 %collective-permute-start.16 = (f32[8,128]{1,0:T(8,128)S(1)}, f32[8,128]{1,0:T(8,128)S(1)}, u32[]{:S(2)}, u32[]{:S(2)}) collective-permute-start(f32[8,128]{1,0:T(8,128)S(1)} %bitcast.193), channel_id=1, source_target_pairs={{0,4},{4,0},{8,12},{12,8},{1,5},{5,1},{9,13},{13,9},{2,6},{6,2},{1... | collective-permute-start | bytes 12296 | tf_op jit(solution)/shard_map/ppermute | solution.py:43
  80.3 5.0 %collective-permute-start.19 = (f32[64,512]{1,0:T(8,128)S(1)}, f32[64,512]{1,0:T(8,128)S(1)}, u32[]{:S(2)}, u32[]{:S(2)}) collective-permute-start(f32[64,512]{1,0:T(8,128)S(1)} %fusion.18), channel_id=1, source_target_pairs={{0,4},{4,0},{8,12},{12,8},{1,5},{5,1},{9,13},{13,9},{2,6},{6,2},{1... | collective-permute-start | bytes 393224 | tf_op jit(solution)/shard_map/ppermute | solution.py:43
  88.0 12.3 %collective-permute-start.20 = (bf16[328,640]{1,0:T(8,128)(2,1)S(1)}, bf16[328,640]{1,0:T(8,128)(2,1)S(1)}, u32[]{:S(2)}, u32[]{:S(2)}) collective-permute-start(bf16[328,640]{1,0:T(8,128)(2,1)S(1)} %pad_maximum_fusion.1), channel_id=1, source_target_pairs={{0,8},{4,12},{8,0},{12,4},{1,9},{5,13},{9,1},{13,5},{2,10},{6,14},... | collective-permute-start | bytes 1259528 | tf_op jit(solution)/shard_map/ppermute | solution.py:38
  88.4 11.9 %collective-permute-start.22 = (bf16[64,1152]{1,0:T(8,128)(2,1)S(1)}, bf16[64,1152]{1,0:T(8,128)(2,1)S(1)}, u32[]{:S(2)}, u32[]{:S(2)}) collective-permute-start(bf16[64,1152]{1,0:T(8,128)(2,1)S(1)} %pad_maximum_fusion.8), channel_id=1, source_target_pairs={{0,2},{1,3},{2,0},{3,1},{4,6},{5,7},{6,4},{7,5},{8,10},{9,11},{10,... | collective-permute-start | bytes 442376 | tf_op jit(solution)/shard_map/ppermute | solution.py:43
  91.9 4.6 %collective-permute-start.21 = (bf16[64,640]{1,0:T(8,128)(2,1)S(1)}, bf16[64,640]{1,0:T(8,128)(2,1)S(1)}, u32[]{:S(2)}, u32[]{:S(2)}) collective-permute-start(bf16[64,640]{1,0:T(8,128)(2,1)S(1)} %get-tuple-element.118), channel_id=1, source_target_pairs={{0,1},{1,0},{2,3},{3,2},{4,5},{5,4},{6,7},{7,6},{8,9},{9,8},{10,11... | collective-permute-start | bytes 245768 | tf_op jit(solution)/shard_map/ppermute | solution.py:43
  91.9 8.4 %collective-permute-start.23 = (bf16[64,640]{1,0:T(8,128)(2,1)S(1)}, bf16[64,640]{1,0:T(8,128)(2,1)S(1)}, u32[]{:S(2)}, u32[]{:S(2)}) collective-permute-start(bf16[64,640]{1,0:T(8,128)(2,1)S(1)} %get-tuple-element.116), channel_id=1, source_target_pairs={{0,3},{1,2},{2,1},{3,0},{4,7},{5,6},{6,5},{7,4},{8,11},{9,10},{10,... | collective-permute-start | bytes 245768 | tf_op jit(solution)/shard_map/ppermute | solution.py:43
  100.5 6.0 %collective-permute-start.24 = (bf16[136,640]{1,0:T(8,128)(2,1)S(1)}, bf16[136,640]{1,0:T(8,128)(2,1)S(1)}, u32[]{:S(2)}, u32[]{:S(2)}) collective-permute-start(bf16[136,640]{1,0:T(8,128)(2,1)S(1)} %pad_maximum_fusion.5), channel_id=1, source_target_pairs={{0,1},{1,0},{2,3},{3,2},{4,5},{5,4},{6,7},{7,6},{8,9},{9,8},{10,11... | collective-permute-start | bytes 522248 | tf_op jit(solution)/shard_map/ppermute | solution.py:43
  103.1 5.2 %collective-permute-start.25 = (bf16[64,640]{1,0:T(8,128)(2,1)S(1)}, bf16[64,640]{1,0:T(8,128)(2,1)S(1)}, u32[]{:S(2)}, u32[]{:S(2)}) collective-permute-start(bf16[64,640]{1,0:T(8,128)(2,1)S(1)} %get-tuple-element.115), channel_id=1, source_target_pairs={{0,2},{1,3},{2,0},{3,1},{4,6},{5,7},{6,4},{7,5},{8,10},{9,11},{10,... | collective-permute-start | bytes 245768 | tf_op jit(solution)/shard_map/ppermute | solution.py:43
  103.3 7.8 %collective-permute-start.26 = (bf16[64,640]{1,0:T(8,128)(2,1)S(1)}, bf16[64,640]{1,0:T(8,128)(2,1)S(1)}, u32[]{:S(2)}, u32[]{:S(2)}) collective-permute-start(bf16[64,640]{1,0:T(8,128)(2,1)S(1)} %get-tuple-element.114), channel_id=1, source_target_pairs={{0,3},{1,2},{2,1},{3,0},{4,7},{5,6},{6,5},{7,4},{8,11},{9,10},{10,... | collective-permute-start | bytes 245768 | tf_op jit(solution)/shard_map/ppermute | solution.py:43
  106.6 9.6 %collective-permute-start.27 = (bf16[72,640]{1,0:T(8,128)(2,1)S(1)}, bf16[72,640]{1,0:T(8,128)(2,1)S(1)}, u32[]{:S(2)}, u32[]{:S(2)}) collective-permute-start(bf16[72,640]{1,0:T(8,128)(2,1)S(1)} %fusion.44), channel_id=1, source_target_pairs={{0,2},{1,3},{2,0},{3,1},{4,6},{5,7},{6,4},{7,5},{8,10},{9,11},{10,... | collective-permute-start | bytes 276488 | tf_op jit(solution)/shard_map/ppermute | solution.py:43
  111.1 9.0 %collective-permute-start.30 = (f32[64,512]{1,0:T(8,128)S(1)}, f32[64,512]{1,0:T(8,128)S(1)}, u32[]{:S(2)}, u32[]{:S(2)}) collective-permute-start(f32[64,512]{1,0:T(8,128)S(1)} %convert_add_fusion.3), channel_id=1, source_target_pairs={{0,4},{4,0},{8,12},{12,8},{1,5},{5,1},{9,13},{13,9},{2,6},{6,2},{1... | collective-permute-start | bytes 393224 | tf_op jit(solution)/shard_map/ppermute | solution.py:43
  (19 other events, 159.8 us)

commit v5 on v4

--- a/solution.py
+++ b/solution.py
@@ -270,27 +270,28 @@
     context_b, cell_loss, pre_enc = lax.optimization_barrier(
         (context_b, distortion / feat + rate / LATENT, pre_enc, got[0])
     )[:3]
-    slope = silu_slope(pre_enc)
+    slope = silu_slope(pre_enc).reshape(n_y, 2, rows, cells)
+    weight = enc_out.reshape(n_y, 2, rows, LATENT)
+    weight = [pick(weight, side, 1).reshape(n_y * rows, LATENT) for side in (core, 1 - core)]
+    slope = [pick(slope, side, 1).reshape(n_y * rows, cells) for side in (core, 1 - core)]
     hyper = mm_cells(context_b, d_params)
     hyper = hyper + swap(hyper, "horiz", 1)
     cell_loss = cell_loss.reshape(-1, EDGE)
     cell_loss = cell_loss + swap(cell_loss, "horiz", 1)
     d_total = (d_latent + direct + d_neighbour).astype(BF)
-    d_total, slope, hyper, cell_loss, *far = lax.optimization_barrier(
-        (d_total, slope, hyper, cell_loss, *far)
+    d_total, slope, weight, hyper, cell_loss, *far = lax.optimization_barrier(
+        (d_total, slope, weight, hyper, cell_loss, *far)
     )
 
     half_enc = halves(hidden_enc, lambda block: mm_cells(d_total, block))
     half_enc = half_enc[0] + swap(half_enc[1], "horiz", 1)
 
     def enc_rows(side):
-        weight = pick(enc_out.reshape(n_y, 2, rows, LATENT), side, 1).reshape(n_y * rows, LATENT)
-        factor = pick(slope.reshape(n_y, 2, rows, cells), side, 1).reshape(n_y * rows, cells)
-        d_pre = lax.optimization_barrier((mm(weight, d_total) * factor).astype(BF))
-        return mm_cells(d_pre, columns)
-
-    other = swap(enc_rows(1 - core).astype(BF), "horiz", 1)
-    near = (enc_rows(core) + other.astype(F32)).reshape(n_y, rows, feat)
+        d_pre = (mm(weight[side], d_total) * slope[side]).astype(BF)
+        return mm_cells(lax.optimization_barrier(d_pre), columns)
+
+    other = swap(enc_rows(1).astype(BF), "horiz", 1)
+    near = (enc_rows(0) + other.astype(F32)).reshape(n_y, rows, feat)
     rider = pack(jnp.concatenate([half_enc, hyper], axis=1), cell_loss)
     sent = [pick(near, (me_y + d) % n_y, 0).astype(BF) for d in range(1, n_y)]
     sent = [jnp.concatenate([piece, rider], axis=0) for piece in sent]
@@ -342,7 +343,7 @@
         half_dec = half_dec.astype(F32) + swap(half_dec, "level", bit).astype(F32)
         bit *= 2
     half_dec = sum_pairs(half_dec, "horiz", 2, n_h, BF)
-    grad_dec_in = both_halves(after(half_dec, *got_enc))
+    grad_dec_in = both_halves(after(half_dec, got_enc[0]))
     loss = (jnp.sum(cell_loss) / (part * n_h)).reshape(1)
     grad_enc_out = both_halves(half_enc).T
     grad_enc_in = pick(near, me_l, 0)

time: 123 us -> 123 us (level)
  transfers between devices with their start and end apart: 31 -> 31, of which waited for: 9 -> 8; matrix products, arithmetic and copies ran while one was open for 39% -> 39% of each run, Pallas kernels for 0% -> 0%
where the time goes in v5:
time: 123 us
  starting transfers between devices  42.3 us (34%)
  other arithmetic  25.8 us (21%)
  matrix products  23.3 us (19%)
  waiting for transfers between devices  20.5 us (17%)
  local copies, waits for them, and re-layouts  4.76 us (4%)
  between operations  3.35 us (3%)
  Pallas kernels  2.48 us (2%)
    ppermute x22, starting transfers between devices, swap(): return lax.ppermute(block, axis, [(i, i ^ bit) for i in range(count)])  33.2 us
    ppermute x22, waiting for transfers between devices, swap(): return lax.ppermute(block, axis, [(i, i ^ bit) for i in range(count)])  18.9 us
    convert_element_type x1, other arithmetic, local(): counts = counts.astype(BF)  15.1 us
    dot_general x10, matrix products, mm(): return jnp.dot(left, right, preferred_element_type=F32)  10.6 us
    dot_general x11, matrix products, mm_cells(): lax.dot_general(left, right, (((1,), (1,)), ((), ())), preferred_element_...  9.63 us
    ppermute x9, starting transfers between devices, shift(): lax.ppermute(block, axis, [(i, (i + step) % count) for i in range(count)])  9.13 us
    dot_general x3, matrix products, mm_rows(): lax.dot_general(left, right, (((0,), (0,)), ((), ())), preferred_element_...  3.17 us
    pallas_call x1, Pallas kernels, encode(): pl.pallas_call(functools.partial(encode_kernel, hidden // 4), out_shape=[...  2.48 us
  transfers between devices with their start and end apart: 31, of which 8 were waited for; matrix products, arithmetic and copies ran while one was open for 39% of the time, Pallas kernels for 0%

profile of v5, /device:TPU:1, one launch (start us, length us, event | category | flops | bytes accessed | tf_op | source)
XLA Modules:
  0.0 122.6 jit_solution(1788500875639026488)
XLA Ops:
  0.7 2.2 %constant_dynamic-slice_fusion.2 = (bf16[160,1024]{1,0:T(8,128)(2,1)S(1)}, bf16[160,1024]{1,0:T(8,128)(2,1)S(1)}, bf16[160,1024]{1,0:T(8,128)(2,1)}, bf16[160,1024]{1,0:T(8,128)(2,1)S(1)}) fusion(bf16[160,4096]{1,0:T(8,128)(2,1)} %bitcast.173, s32[]{:T(128)S(6)} %select_n.211, s32[]{:T(128)S(6)} %select_n.209, s32[]{:T(128)S(6)} %select_n.207, s32[]{:T(128)S(6)} %select_n.205), kind=kLoop, calls=%fused_computation.165 | loop fusion | bytes 2621456 | tf_op jit(solution)/shard_map/dynamic_slice | solution.py:183
  3.0 2.1 %collective-permute-start = (bf16[160,1024]{1,0:T(8,128)(2,1)}, bf16[160,1024]{1,0:T(8,128)(2,1)S(1)}, u32[]{:S(2)}, u32[]{:S(2)}) collective-permute-start(bf16[160,1024]{1,0:T(8,128)(2,1)} %get-tuple-element.115), channel_id=1, source_target_pairs={{0,1},{1,2},{2,3},{3,0},{4,5},{5,6},{6,7},{7,4},{8,9},{9,10},{10,1... | collective-permute-start | bytes 983048 | tf_op jit(solution)/shard_map/ppermute | solution.py:38
  5.1 2.3 %collective-permute-start.1 = (bf16[160,1024]{1,0:T(8,128)(2,1)S(1)}, bf16[160,1024]{1,0:T(8,128)(2,1)S(1)}, u32[]{:S(2)}, u32[]{:S(2)}) collective-permute-start(bf16[160,1024]{1,0:T(8,128)(2,1)S(1)} %get-tuple-element.114), channel_id=1, source_target_pairs={{0,2},{1,3},{2,0},{3,1},{4,6},{5,7},{6,4},{7,5},{8,10},{9,11},{10,... | collective-permute-start | bytes 983048 | tf_op jit(solution)/shard_map/ppermute | solution.py:38
  11.4 15.1 %add_convert_fusion = bf16[4352,1024]{1,0:T(8,128)(2,1)} fusion(s32[1024]{0:T(1024)S(1)} %bitcast.184, s32[1024]{0:T(1024)S(1)} %bitcast.185, s32[1024]{0:T(1024)S(1)} %bitcast.186, s32[1024]{0:T(1024)S(1)} %bitcast.187, s32[1024]{0:T(1024)S(1)} %bitcast.188, s32[1024]{0:T(1024)S(1)} %bitcast.183), kind=kLoop, calls=%fused_computation | loop fusion | flops 80216064 | bytes 8937472 | tf_op jit(solution)/shard_map/convert_element_type | solution.py:200
  27.8 2.7 %fusion.14.refs_4_ = bf16[1024,640]{1,0:T(8,128)(2,1)S(1)} fusion(bf16[1024,640]{1,0:T(8,128)(2,1)} %param.9, s32[640]{0:T(1024)S(1)} %fusion.77), kind=kOutput, calls=%fused_computation.34 | convolution fusion | flops 839925760 | bytes 2624000 | tf_op jit(solution)/shard_map/dot_general | solution.py:20
  30.5 2.5 %shard_map.135 = (bf16[640,1024]{1,0:T(8,128)(2,1)S(1)}, f32[1024,1024]{1,0:T(8,128)S(1)}, bf16[1024,1024]{1,0:T(8,128)(2,1)S(1)}, bf16[64,1024]{1,0:T(8,128)(2,1)S(1)}) custom-call(bf16[160,1024]{1,0:T(8,128)(2,1)S(1)} %get-tuple-element.54.refs_0_, bf16[160,1024]{1,0:T(8,128)(2,1)S(1)} %collective-permute-done.refs_1_, ...), custom_call_target="tpu_custom_call" | custom-call | flops 1476395008 | bytes 10223616 | tf_op jit(solution)/shard_map/pallas_call | solution.py:151
  32.9 6.5 %collective-permute-start.3 = (bf16[64,1024]{1,0:T(8,128)(2,1)S(1)}, bf16[64,1024]{1,0:T(8,128)(2,1)S(1)}, u32[]{:S(2)}, u32[]{:S(2)}) collective-permute-start(bf16[64,1024]{1,0:T(8,128)(2,1)S(1)} %get-tuple-element.59), channel_id=1, source_target_pairs={{0,1},{1,0},{2,3},{3,2},{4,5},{5,4},{6,7},{7,6},{8,9},{9,8},{10,11... | collective-permute-start | bytes 393224 | tf_op jit(solution)/shard_map/ppermute | solution.py:43
  39.7 1.9 %collective-permute-start.5 = (bf16[64,1024]{1,0:T(8,128)(2,1)S(1)}, bf16[64,1024]{1,0:T(8,128)(2,1)S(1)}, u32[]{:S(2)}, u32[]{:S(2)}) collective-permute-start(bf16[64,1024]{1,0:T(8,128)(2,1)S(1)} %get-tuple-element.59), channel_id=1, source_target_pairs={{0,3},{1,2},{2,1},{3,0},{4,7},{5,6},{6,5},{7,4},{8,11},{9,10},{10,... | collective-permute-start | bytes 393224 | tf_op jit(solution)/shard_map/ppermute | solution.py:43
  45.8 1.9 %fusion.94 = f32[1024,640]{1,0:T(8,128)S(1)} fusion(bf16[1024,1024]{1,0:T(8,128)(2,1)S(1)} %get-tuple-element.144, bf16[640,1024]{1,0:T(8,128)(2,1)S(1)} %get-tuple-element.147, f32[1024,640]{0,1:T(8,128)S(1)} %fusion.102), kind=kOutput, calls=%fused_computation.225 | convolution fusion | flops 1344798720 | bytes 8650752 | tf_op jit(solution)/shard_map/dot_general | solution.py:28
  48.9 2.9 %fusion.4 = bf16[1024,1024]{1,0:T(8,128)(2,1)S(1)} fusion(f32[1024,1024]{0,1:T(8,128)S(1)} %get-tuple-element.145, bf16[1024,640]{1,0:T(8,128)(2,1)S(1)} %copy-done, bf16[640,1024]{1,0:T(8,128)(2,1)S(1)} %get-tuple-element.147, f32[1024,640]{0,1:T(8,128)S(1)} %fusion.102), kind=kOutput, calls=%fused_computation.12 | convolution fusion | flops 1354235904 | bytes 11534336 | tf_op jit(solution)/shard_map/dot_general | solution.py:20
  60.7 1.7 %collective-permute-start.9 = (bf16[64,128]{1,0:T(8,128)(2,1)S(1)}, bf16[64,128]{1,0:T(8,128)(2,1)S(1)}, u32[]{:S(2)}, u32[]{:S(2)}) collective-permute-start(bf16[64,128]{1,0:T(8,128)(2,1)S(1)} %get-tuple-element.132), channel_id=1, source_target_pairs={{0,4},{4,8},{8,12},{12,0},{1,5},{5,9},{9,13},{13,1},{2,6},{6,10},{... | collective-permute-start | bytes 49160 | tf_op jit(solution)/shard_map/ppermute | solution.py:38
  62.5 2.7 %fusion = f32[64,4096]{1,0:T(8,128)S(1)} fusion(bf16[64,1024]{1,0:T(8,128)(2,1)S(1)} %bitcast.190, bf16[4352,1024]{1,0:T(8,128)(2,1)S(1)} %bitcast.166), kind=kOutput, calls=%fused_computation.7 | convolution fusion | flops 536870912 | bytes 9568256 | tf_op jit(solution)/shard_map/dot_general | solution.py:28
  68.0 2.2 %collective-permute-start.13 = (bf16[64,1024]{1,0:T(8,128)(2,1)S(1)}, bf16[64,1024]{1,0:T(8,128)(2,1)S(1)}, u32[]{:S(2)}, u32[]{:S(2)}) collective-permute-start(bf16[64,1024]{1,0:T(8,128)(2,1)S(1)} %get-tuple-element.127), channel_id=1, source_target_pairs={{0,2},{1,3},{2,0},{3,1},{4,6},{5,7},{6,4},{7,5},{8,10},{9,11},{10,... | collective-permute-start | bytes 393224 | tf_op jit(solution)/shard_map/ppermute | solution.py:43
  70.7 4.4 %collective-permute-done.12 = bf16[64,1536]{1,0:T(8,128)(2,1)S(1)} collective-permute-done((bf16[64,1536]{1,0:T(8,128)(2,1)S(1)}, bf16[64,1536]{1,0:T(8,128)(2,1)S(1)}, u32[]{:S(2)}, u32[]{:S(2)}) %collective-permute-start.12) | collective-permute-done | bytes 196640 | tf_op jit(solution)/shard_map/ppermute | solution.py:43
  77.3 2.2 %collective-permute-done.14 = bf16[64,1024]{1,0:T(8,128)(2,1)S(1)} collective-permute-done((bf16[64,1024]{1,0:T(8,128)(2,1)S(1)}, bf16[64,1024]{1,0:T(8,128)(2,1)S(1)}, u32[]{:S(2)}, u32[]{:S(2)}) %collective-permute-start.14) | collective-permute-done | bytes 131104 | tf_op jit(solution)/shard_map/ppermute | solution.py:43
  80.6 2.4 %collective-permute-start.19 = (f32[64,512]{1,0:T(8,128)S(1)}, f32[64,512]{1,0:T(8,128)S(1)}, u32[]{:S(2)}, u32[]{:S(2)}) collective-permute-start(f32[64,512]{1,0:T(8,128)S(1)} %fusion.16), channel_id=1, source_target_pairs={{0,4},{4,0},{8,12},{12,8},{1,5},{5,1},{9,13},{13,9},{2,6},{6,2},{1... | collective-permute-start | bytes 393224 | tf_op jit(solution)/shard_map/ppermute | solution.py:43
  88.2 3.5 %collective-permute-start.22 = (bf16[64,1152]{1,0:T(8,128)(2,1)S(1)}, bf16[64,1152]{1,0:T(8,128)(2,1)S(1)}, u32[]{:S(2)}, u32[]{:S(2)}) collective-permute-start(bf16[64,1152]{1,0:T(8,128)(2,1)S(1)} %pad_maximum_fusion.8), channel_id=1, source_target_pairs={{0,2},{1,3},{2,0},{3,1},{4,6},{5,7},{6,4},{7,5},{8,10},{9,11},{10,... | collective-permute-start | bytes 442376 | tf_op jit(solution)/shard_map/ppermute | solution.py:43
  93.1 3.2 %collective-permute-done.21 = bf16[64,640]{1,0:T(8,128)(2,1)S(1)} collective-permute-done((bf16[64,640]{1,0:T(8,128)(2,1)S(1)}, bf16[64,640]{1,0:T(8,128)(2,1)S(1)}, u32[]{:S(2)}, u32[]{:S(2)}) %collective-permute-start.21) | collective-permute-done | bytes 81952 | tf_op jit(solution)/shard_map/ppermute | solution.py:43
  96.3 3.8 %collective-permute-done.23 = bf16[64,640]{1,0:T(8,128)(2,1)S(1)} collective-permute-done((bf16[64,640]{1,0:T(8,128)(2,1)S(1)}, bf16[64,640]{1,0:T(8,128)(2,1)S(1)}, u32[]{:S(2)}, u32[]{:S(2)}) %collective-permute-start.23) | collective-permute-done | bytes 81952 | tf_op jit(solution)/shard_map/ppermute | solution.py:43
  100.4 2.5 %collective-permute-start.24 = (bf16[136,640]{1,0:T(8,128)(2,1)S(1)}, bf16[136,640]{1,0:T(8,128)(2,1)S(1)}, u32[]{:S(2)}, u32[]{:S(2)}) collective-permute-start(bf16[136,640]{1,0:T(8,128)(2,1)S(1)} %pad_maximum_fusion.5), channel_id=1, source_target_pairs={{0,1},{1,0},{2,3},{3,2},{4,5},{5,4},{6,7},{7,6},{8,9},{9,8},{10,11... | collective-permute-start | bytes 522248 | tf_op jit(solution)/shard_map/ppermute | solution.py:43
  103.2 1.9 %collective-permute-start.26 = (bf16[64,640]{1,0:T(8,128)(2,1)S(1)}, bf16[64,640]{1,0:T(8,128)(2,1)S(1)}, u32[]{:S(2)}, u32[]{:S(2)}) collective-permute-start(bf16[64,640]{1,0:T(8,128)(2,1)S(1)} %get-tuple-element.120), channel_id=1, source_target_pairs={{0,3},{1,2},{2,1},{3,0},{4,7},{5,6},{6,5},{7,4},{8,11},{9,10},{10,... | collective-permute-start | bytes 245768 | tf_op jit(solution)/shard_map/ppermute | solution.py:43
  108.1 3.6 %collective-permute-start.30 = (f32[64,512]{1,0:T(8,128)S(1)}, f32[64,512]{1,0:T(8,128)S(1)}, u32[]{:S(2)}, u32[]{:S(2)}) collective-permute-start(f32[64,512]{1,0:T(8,128)S(1)} %convert_add_fusion.3), channel_id=1, source_target_pairs={{0,4},{4,0},{8,12},{12,8},{1,5},{5,1},{9,13},{13,9},{2,6},{6,2},{1... | collective-permute-start | bytes 393224 | tf_op jit(solution)/shard_map/ppermute | solution.py:43
  112.4 3.7 %collective-permute-done.27 = bf16[72,640]{1,0:T(8,128)(2,1)S(1)} collective-permute-done((bf16[72,640]{1,0:T(8,128)(2,1)S(1)}, bf16[72,640]{1,0:T(8,128)(2,1)S(1)}, u32[]{:S(2)}, u32[]{:S(2)}) %collective-permute-start.27) | collective-permute-done | bytes 92192 | tf_op jit(solution)/shard_map/ppermute | solution.py:43
  116.2 1.9 %collective-permute-start.28 = (f32[64,512]{1,0:T(8,128)S(1)}, f32[64,512]{1,0:T(8,128)S(1)}, u32[]{:S(2)}, u32[]{:S(2)}) collective-permute-start(f32[64,512]{1,0:T(8,128)S(1)} %convert_add_fusion.4), channel_id=1, source_target_pairs={{0,4},{4,0},{8,12},{12,8},{1,5},{5,1},{9,13},{13,9},{2,6},{6,2},{1... | collective-permute-start | bytes 393224 | tf_op jit(solution)/shard_map/ppermute | solution.py:43
  (159 shorter events, 39.5 us)
Async XLA Ops:
  3.0 27.5 %collective-permute-start = (bf16[160,1024]{1,0:T(8,128)(2,1)}, bf16[160,1024]{1,0:T(8,128)(2,1)S(1)}, u32[]{:S(2)}, u32[]{:S(2)}) collective-permute-start(bf16[160,1024]{1,0:T(8,128)(2,1)} %get-tuple-element.115), channel_id=1, source_target_pairs={{0,1},{1,2},{2,3},{3,0},{4,5},{5,6},{6,7},{7,4},{8,9},{9,10},{10,1... | collective-permute-start | bytes 983048 | tf_op jit(solution)/shard_map/ppermute | solution.py:38
  5.1 25.3 %collective-permute-start.1 = (bf16[160,1024]{1,0:T(8,128)(2,1)S(1)}, bf16[160,1024]{1,0:T(8,128)(2,1)S(1)}, u32[]{:S(2)}, u32[]{:S(2)}) collective-permute-start(bf16[160,1024]{1,0:T(8,128)(2,1)S(1)} %get-tuple-element.114), channel_id=1, source_target_pairs={{0,2},{1,3},{2,0},{3,1},{4,6},{5,7},{6,4},{7,5},{8,10},{9,11},{10,... | collective-permute-start | bytes 983048 | tf_op jit(solution)/shard_map/ppermute | solution.py:38
  7.4 23.0 %collective-permute-start.2 = (bf16[160,1024]{1,0:T(8,128)(2,1)S(1)}, bf16[160,1024]{1,0:T(8,128)(2,1)S(1)}, u32[]{:S(2)}, u32[]{:S(2)}) collective-permute-start(bf16[160,1024]{1,0:T(8,128)(2,1)S(1)} %get-tuple-element.113), channel_id=1, source_target_pairs={{0,3},{1,0},{2,1},{3,2},{4,7},{5,4},{6,5},{7,6},{8,11},{9,8},{10,9... | collective-permute-start | bytes 983048 | tf_op jit(solution)/shard_map/ppermute | solution.py:38
  32.9 20.2 %collective-permute-start.3 = (bf16[64,1024]{1,0:T(8,128)(2,1)S(1)}, bf16[64,1024]{1,0:T(8,128)(2,1)S(1)}, u32[]{:S(2)}, u32[]{:S(2)}) collective-permute-start(bf16[64,1024]{1,0:T(8,128)(2,1)S(1)} %get-tuple-element.59), channel_id=1, source_target_pairs={{0,1},{1,0},{2,3},{3,2},{4,5},{5,4},{6,7},{7,6},{8,9},{9,8},{10,11... | collective-permute-start | bytes 393224 | tf_op jit(solution)/shard_map/ppermute | solution.py:43
  39.4 13.7 %collective-permute-start.4 = (bf16[64,1024]{1,0:T(8,128)(2,1)S(1)}, bf16[64,1024]{1,0:T(8,128)(2,1)S(1)}, u32[]{:S(2)}, u32[]{:S(2)}) collective-permute-start(bf16[64,1024]{1,0:T(8,128)(2,1)S(1)} %get-tuple-element.59), channel_id=1, source_target_pairs={{0,2},{1,3},{2,0},{3,1},{4,6},{5,7},{6,4},{7,5},{8,10},{9,11},{10,... | collective-permute-start | bytes 393224 | tf_op jit(solution)/shard_map/ppermute | solution.py:43
  39.7 13.5 %collective-permute-start.5 = (bf16[64,1024]{1,0:T(8,128)(2,1)S(1)}, bf16[64,1024]{1,0:T(8,128)(2,1)S(1)}, u32[]{:S(2)}, u32[]{:S(2)}) collective-permute-start(bf16[64,1024]{1,0:T(8,128)(2,1)S(1)} %get-tuple-element.59), channel_id=1, source_target_pairs={{0,3},{1,2},{2,1},{3,0},{4,7},{5,6},{6,5},{7,4},{8,11},{9,10},{10,... | collective-permute-start | bytes 393224 | tf_op jit(solution)/shard_map/ppermute | solution.py:43
  47.7 5.5 %collective-permute-start.6 = (bf16[2,4,64,640]{3,2,1,0:T(8,128)(2,1)S(1)}, bf16[2,4,64,640]{3,2,1,0:T(8,128)(2,1)S(1)}, u32[]{:S(2)}, u32[]{:S(2)}) collective-permute-start(bf16[2,4,64,640]{3,2,1,0:T(8,128)(2,1)S(1)} %fusion.24), channel_id=1, source_target_pairs={{0,4},{4,0},{8,12},{12,8},{1,5},{5,1},{9,13},{13,9},{2,6},{6,2},{1... | collective-permute-start | bytes 1966088 | tf_op jit(solution)/shard_map/ppermute | solution.py:43
  53.3 12.7 %collective-permute-start.11 = (f32[64,512]{1,0:T(8,128)S(1)}, f32[64,512]{1,0:T(8,128)S(1)}, u32[]{:S(2)}, u32[]{:S(2)}) collective-permute-start(f32[64,512]{1,0:T(8,128)S(1)} %fusion.19), channel_id=1, source_target_pairs={{0,4},{4,0},{8,12},{12,8},{1,5},{5,1},{9,13},{13,9},{2,6},{6,2},{1... | collective-permute-start | bytes 393224 | tf_op jit(solution)/shard_map/ppermute | solution.py:43
  66.2 8.9 %collective-permute-start.12 = (bf16[64,1536]{1,0:T(8,128)(2,1)S(1)}, bf16[64,1536]{1,0:T(8,128)(2,1)S(1)}, u32[]{:S(2)}, u32[]{:S(2)}) collective-permute-start(bf16[64,1536]{1,0:T(8,128)(2,1)S(1)} %pad_maximum_fusion.4), channel_id=1, source_target_pairs={{0,1},{1,0},{2,3},{3,2},{4,5},{5,4},{6,7},{7,6},{8,9},{9,8},{10,11... | collective-permute-start | bytes 589832 | tf_op jit(solution)/shard_map/ppermute | solution.py:43
  67.7 12.5 %collective-permute-start.17 = (bf16[256,640]{1,0:T(8,128)(2,1)S(1)}, bf16[256,640]{1,0:T(8,128)(2,1)S(1)}, u32[]{:S(2)}, u32[]{:S(2)}) collective-permute-start(bf16[256,640]{1,0:T(8,128)(2,1)S(1)} %bitcast.176), channel_id=1, source_target_pairs={{0,8},{4,12},{8,0},{12,4},{1,9},{5,13},{9,1},{13,5},{2,10},{6,14},... | collective-permute-start | bytes 983048 | tf_op jit(solution)/shard_map/ppermute | solution.py:38
  68.0 9.3 %collective-permute-start.13 = (bf16[64,1024]{1,0:T(8,128)(2,1)S(1)}, bf16[64,1024]{1,0:T(8,128)(2,1)S(1)}, u32[]{:S(2)}, u32[]{:S(2)}) collective-permute-start(bf16[64,1024]{1,0:T(8,128)(2,1)S(1)} %get-tuple-element.127), channel_id=1, source_target_pairs={{0,2},{1,3},{2,0},{3,1},{4,6},{5,7},{6,4},{7,5},{8,10},{9,11},{10,... | collective-permute-start | bytes 393224 | tf_op jit(solution)/shard_map/ppermute | solution.py:43
  70.2 9.3 %collective-permute-start.14 = (bf16[64,1024]{1,0:T(8,128)(2,1)S(1)}, bf16[64,1024]{1,0:T(8,128)(2,1)S(1)}, u32[]{:S(2)}, u32[]{:S(2)}) collective-permute-start(bf16[64,1024]{1,0:T(8,128)(2,1)S(1)} %get-tuple-element.126), channel_id=1, source_target_pairs={{0,3},{1,2},{2,1},{3,0},{4,7},{5,6},{6,5},{7,4},{8,11},{9,10},{10,... | collective-permute-start | bytes 393224 | tf_op jit(solution)/shard_map/ppermute | solution.py:43
  75.1 5.0 %collective-permute-start.16 = (f32[8,128]{1,0:T(8,128)S(1)}, f32[8,128]{1,0:T(8,128)S(1)}, u32[]{:S(2)}, u32[]{:S(2)}) collective-permute-start(f32[8,128]{1,0:T(8,128)S(1)} %bitcast.189), channel_id=1, source_target_pairs={{0,4},{4,0},{8,12},{12,8},{1,5},{5,1},{9,13},{13,9},{2,6},{6,2},{1... | collective-permute-start | bytes 12296 | tf_op jit(solution)/shard_map/ppermute | solution.py:43
  75.6 4.5 %collective-permute-start.15 = (f32[64,128]{1,0:T(8,128)S(1)}, f32[64,128]{1,0:T(8,128)S(1)}, u32[]{:S(2)}, u32[]{:S(2)}) collective-permute-start(f32[64,128]{1,0:T(8,128)S(1)} %fusion.34), channel_id=1, source_target_pairs={{0,4},{4,0},{8,12},{12,8},{1,5},{5,1},{9,13},{13,9},{2,6},{6,2},{1... | collective-permute-start | bytes 98312 | tf_op jit(solution)/shard_map/ppermute | solution.py:43
  80.6 4.5 %collective-permute-start.19 = (f32[64,512]{1,0:T(8,128)S(1)}, f32[64,512]{1,0:T(8,128)S(1)}, u32[]{:S(2)}, u32[]{:S(2)}) collective-permute-start(f32[64,512]{1,0:T(8,128)S(1)} %fusion.16), channel_id=1, source_target_pairs={{0,4},{4,0},{8,12},{12,8},{1,5},{5,1},{9,13},{13,9},{2,6},{6,2},{1... | collective-permute-start | bytes 393224 | tf_op jit(solution)/shard_map/ppermute | solution.py:43
  87.8 12.3 %collective-permute-start.20 = (bf16[328,640]{1,0:T(8,128)(2,1)S(1)}, bf16[328,640]{1,0:T(8,128)(2,1)S(1)}, u32[]{:S(2)}, u32[]{:S(2)}) collective-permute-start(bf16[328,640]{1,0:T(8,128)(2,1)S(1)} %pad_maximum_fusion.1), channel_id=1, source_target_pairs={{0,8},{4,12},{8,0},{12,4},{1,9},{5,13},{9,1},{13,5},{2,10},{6,14},... | collective-permute-start | bytes 1259528 | tf_op jit(solution)/shard_map/ppermute | solution.py:38
  88.2 11.9 %collective-permute-start.22 = (bf16[64,1152]{1,0:T(8,128)(2,1)S(1)}, bf16[64,1152]{1,0:T(8,128)(2,1)S(1)}, u32[]{:S(2)}, u32[]{:S(2)}) collective-permute-start(bf16[64,1152]{1,0:T(8,128)(2,1)S(1)} %pad_maximum_fusion.8), channel_id=1, source_target_pairs={{0,2},{1,3},{2,0},{3,1},{4,6},{5,7},{6,4},{7,5},{8,10},{9,11},{10,... | collective-permute-start | bytes 442376 | tf_op jit(solution)/shard_map/ppermute | solution.py:43
  91.7 4.6 %collective-permute-start.21 = (bf16[64,640]{1,0:T(8,128)(2,1)S(1)}, bf16[64,640]{1,0:T(8,128)(2,1)S(1)}, u32[]{:S(2)}, u32[]{:S(2)}) collective-permute-start(bf16[64,640]{1,0:T(8,128)(2,1)S(1)} %get-tuple-element.124), channel_id=1, source_target_pairs={{0,1},{1,0},{2,3},{3,2},{4,5},{5,4},{6,7},{7,6},{8,9},{9,8},{10,11... | collective-permute-start | bytes 245768 | tf_op jit(solution)/shard_map/ppermute | solution.py:43
  91.7 8.4 %collective-permute-start.23 = (bf16[64,640]{1,0:T(8,128)(2,1)S(1)}, bf16[64,640]{1,0:T(8,128)(2,1)S(1)}, u32[]{:S(2)}, u32[]{:S(2)}) collective-permute-start(bf16[64,640]{1,0:T(8,128)(2,1)S(1)} %get-tuple-element.122), channel_id=1, source_target_pairs={{0,3},{1,2},{2,1},{3,0},{4,7},{5,6},{6,5},{7,4},{8,11},{9,10},{10,... | collective-permute-start | bytes 245768 | tf_op jit(solution)/shard_map/ppermute | solution.py:43
  100.4 6.0 %collective-permute-start.24 = (bf16[136,640]{1,0:T(8,128)(2,1)S(1)}, bf16[136,640]{1,0:T(8,128)(2,1)S(1)}, u32[]{:S(2)}, u32[]{:S(2)}) collective-permute-start(bf16[136,640]{1,0:T(8,128)(2,1)S(1)} %pad_maximum_fusion.5), channel_id=1, source_target_pairs={{0,1},{1,0},{2,3},{3,2},{4,5},{5,4},{6,7},{7,6},{8,9},{9,8},{10,11... | collective-permute-start | bytes 522248 | tf_op jit(solution)/shard_map/ppermute | solution.py:43
  102.9 8.8 %collective-permute-start.25 = (bf16[64,640]{1,0:T(8,128)(2,1)S(1)}, bf16[64,640]{1,0:T(8,128)(2,1)S(1)}, u32[]{:S(2)}, u32[]{:S(2)}) collective-permute-start(bf16[64,640]{1,0:T(8,128)(2,1)S(1)} %get-tuple-element.121), channel_id=1, source_target_pairs={{0,2},{1,3},{2,0},{3,1},{4,6},{5,7},{6,4},{7,5},{8,10},{9,11},{10,... | collective-permute-start | bytes 245768 | tf_op jit(solution)/shard_map/ppermute | solution.py:43
  103.2 8.5 %collective-permute-start.26 = (bf16[64,640]{1,0:T(8,128)(2,1)S(1)}, bf16[64,640]{1,0:T(8,128)(2,1)S(1)}, u32[]{:S(2)}, u32[]{:S(2)}) collective-permute-start(bf16[64,640]{1,0:T(8,128)(2,1)S(1)} %get-tuple-element.120), channel_id=1, source_target_pairs={{0,3},{1,2},{2,1},{3,0},{4,7},{5,6},{6,5},{7,4},{8,11},{9,10},{10,... | collective-permute-start | bytes 245768 | tf_op jit(solution)/shard_map/ppermute | solution.py:43
  106.5 9.6 %collective-permute-start.27 = (bf16[72,640]{1,0:T(8,128)(2,1)S(1)}, bf16[72,640]{1,0:T(8,128)(2,1)S(1)}, u32[]{:S(2)}, u32[]{:S(2)}) collective-permute-start(bf16[72,640]{1,0:T(8,128)(2,1)S(1)} %fusion.42), channel_id=1, source_target_pairs={{0,2},{1,3},{2,0},{3,1},{4,6},{5,7},{6,4},{7,5},{8,10},{9,11},{10,... | collective-permute-start | bytes 276488 | tf_op jit(solution)/shard_map/ppermute | solution.py:43
  108.1 11.8 %collective-permute-start.30 = (f32[64,512]{1,0:T(8,128)S(1)}, f32[64,512]{1,0:T(8,128)S(1)}, u32[]{:S(2)}, u32[]{:S(2)}) collective-permute-start(f32[64,512]{1,0:T(8,128)S(1)} %convert_add_fusion.3), channel_id=1, source_target_pairs={{0,4},{4,0},{8,12},{12,8},{1,5},{5,1},{9,13},{13,9},{2,6},{6,2},{1... | collective-permute-start | bytes 393224 | tf_op jit(solution)/shard_map/ppermute | solution.py:43
  (19 other events, 160.1 us)
